TPU v7x, 32 devices: a whole 2x2x4 slice. The times are simulated.
32 devices in a mesh: rep: 2 (over y), fsdp: 8 (over z, x), seq: 2 (over core).
Axes of the slice: x: 2, y: 2, z: 4, core: 2. Of those that a mesh axis runs over, the one named last changes fastest.
Arguments:
- queries: bfloat16 [16, 256, 1536], P(('rep', 'fsdp'), 'seq'), parts along dimension 0, may hold values from -6 to 6
- image_keys: bfloat16 [16, 256, 1536], P(('rep', 'fsdp'), 'seq'), parts along dimension 0, may hold values from -6 to 6
- image_values: bfloat16 [16, 256, 1536], P(('rep', 'fsdp'), 'seq'), parts along dimension 0, may hold values from -6 to 6
- text_keys: bfloat16 [16, 128, 1536], P(('rep', 'fsdp')), parts along dimension 0, may hold values from -6 to 6
- text_values: bfloat16 [16, 128, 1536], P(('rep', 'fsdp')), parts along dimension 0, may hold values from -6 to 6
- control_hint: bfloat16 [16, 256, 128], P(('rep', 'fsdp'), 'seq'), parts along dimension 0, may hold values from -6 to 6
- proj_out: bfloat16 [1536, 3072], P('fsdp', 'seq'), may hold values from -0.15625 to 0.15625
- adapter_down: bfloat16 [1536, 128], P('fsdp'), may hold values from -0.15625 to 0.15625
- adapter_up: bfloat16 [128, 3072], P(None, 'fsdp'), may hold values from -0.5 to 0.5
- cotangent: bfloat16 [16, 256, 3072], P(('rep', 'fsdp'), 'seq'), parts along dimension 0, may hold values from -6 to 6
Outputs:
- update: bfloat16 [16, 256, 3072], P(('rep', 'fsdp'), 'seq'), parts along dimension 0
- query_grad: bfloat16 [16, 256, 1536], P(('rep', 'fsdp'), 'seq'), parts along dimension 0
- key_grad: bfloat16 [16, 256, 1536], P(('rep', 'fsdp'), 'seq'), parts along dimension 0
- value_grad: bfloat16 [16, 256, 1536], P(('rep', 'fsdp'), 'seq'), parts along dimension 0
- down_grad: float32 [3072, 128], P(('rep', 'fsdp', 'seq')), parts along dimension 0
- up_grad: float32 [256, 3072], P('rep', ('fsdp', 'seq')), parts along dimension 0
There are 2 independent parts, one for each index of `rep`. A program takes and returns all parts, laid end to end along the dimension named above; an argument that names none is the same for every part. Nothing has to cross between parts.
All inputs are finite; a program needn't handle non-finite values.
Results may differ from a plain program's by a relative error of at most 0.011.
Values may be sent and summed in bfloat16 or wider, within the bound.
No kernel may reach another device: no remote copies, remote signals or barrier semaphores. Data moves between devices by JAX's collectives and lax.ppermute only.
A program may use at most 128 MiB of HBM per device.

v0:
```python
import jax
import jax.numpy as jnp
from jax import lax
from jax.sharding import PartitionSpec as P

HD = 128


def partner(value, axis, bit):
    mask = 2**bit
    pairs = [(source, source ^ mask) for source in range(lax.axis_size(axis))]
    return lax.ppermute(value, axis, pairs)


def split_heads(matrix):
    return matrix.reshape(matrix.shape[0], matrix.shape[1] // HD, HD)


def head_scores(query_rows, key_rows):
    return jnp.einsum(
        "qhd,khd->hqk",
        split_heads(query_rows),
        split_heads(key_rows),
        preferred_element_type=jnp.float32,
    ) * HD ** (-0.5)


def local(
    queries,
    image_keys,
    image_values,
    text_keys,
    text_values,
    control_hint,
    proj_out,
    adapter_down,
    adapter_up,
    cotangent,
):
    factor = HD ** (-0.5)
    query_rows = queries[0]
    local_rows = query_rows.shape[0]
    inner = query_rows.shape[1]
    seq_index = lax.axis_index("seq")
    near_start = seq_index * local_rows
    far_start = (1 - seq_index) * local_rows
    cot_rows = cotangent[0]
    half_out = lax.all_gather(proj_out, "fsdp", axis=0, tiled=True)
    down_full, up_full = (
        lax.all_gather(adapter_down, "fsdp", axis=0, tiled=True),
        lax.all_gather(adapter_up, "fsdp", axis=1, tiled=True),
    )
    pair_keys, pair_values = (
        lax.all_gather(image_keys[0], "seq", axis=0, tiled=True),
        lax.all_gather(image_values[0], "seq", axis=0, tiled=True),
    )
    all_keys = jnp.concatenate([pair_keys, text_keys[0]], 0)
    all_values = jnp.concatenate([pair_values, text_values[0]], 0)
    image_rows = pair_keys.shape[0]
    scores = head_scores(query_rows, all_keys)
    row_max = jnp.max(scores, -1, keepdims=True)
    log_total = row_max + jnp.log(jnp.sum(jnp.exp(scores - row_max), -1, keepdims=True))
    attn_prob = jnp.exp(scores - log_total)
    prob_half = attn_prob.astype(jnp.bfloat16)
    value_heads = split_heads(all_values)
    attn = (
        jnp.einsum("hqk,khd->qhd", prob_half, value_heads, preferred_element_type=jnp.float32)
        .reshape(local_rows, inner)
        .astype(jnp.bfloat16)
    )
    pre_act = jnp.dot(attn, down_full, preferred_element_type=jnp.float32) + control_hint[0].astype(
        jnp.float32
    )
    logistic = jax.nn.sigmoid(pre_act)
    adapter_act = (pre_act * logistic).astype(jnp.bfloat16)
    act_back = jnp.einsum("td,rd->tr", cot_rows, up_full, preferred_element_type=jnp.float32)
    act_grad = (act_back * logistic * (1.0 + pre_act * (1.0 - logistic))).astype(jnp.bfloat16)
    full_out = lax.all_gather(half_out, "seq", axis=1, tiled=True)
    update = (
        jnp.dot(attn, full_out, preferred_element_type=jnp.float32)
        + jnp.dot(adapter_act, up_full, preferred_element_type=jnp.float32)
    ).astype(jnp.bfloat16)
    back_sum = jnp.einsum("td,hd->th", cot_rows, full_out, preferred_element_type=jnp.float32)
    attn_grad = (
        back_sum + jnp.einsum("tr,hr->th", act_grad, down_full, preferred_element_type=jnp.float32)
    ).astype(jnp.bfloat16)
    grad_scale = float(lax.axis_size("fsdp") * lax.axis_size("seq") * local_rows) ** (-0.5)
    down_term = (
        jnp.einsum("th,tr->hr", attn, act_grad, preferred_element_type=jnp.float32) * grad_scale
    )
    up_term = (
        jnp.einsum("tr,td->rd", adapter_act, cot_rows, preferred_element_type=jnp.float32)
        * grad_scale
    )
    down_grad, up_grad = (
        lax.psum_scatter(down_term, ("fsdp", "seq"), scatter_dimension=0, tiled=True),
        lax.psum_scatter(up_term, ("fsdp", "seq"), scatter_dimension=1, tiled=True),
    )
    grad_heads = split_heads(attn_grad)
    delta = jnp.einsum(
        "qhd,qhd->hq", grad_heads, split_heads(attn), preferred_element_type=jnp.float32
    )[:, :, None]
    prob_grad = jnp.einsum(
        "qhd,khd->hqk", grad_heads, value_heads, preferred_element_type=jnp.float32
    )
    score_grad = (attn_prob * (prob_grad - delta)).astype(jnp.bfloat16)
    query_grad = (
        (
            jnp.einsum(
                "hqk,khd->qhd",
                score_grad,
                split_heads(all_keys),
                preferred_element_type=jnp.float32,
            )
            * factor
        )
        .reshape(local_rows, inner)
        .astype(jnp.bfloat16)
    )
    key_terms = jnp.einsum(
        "hqk,qhd->khd",
        score_grad[:, :, :image_rows],
        split_heads(query_rows),
        preferred_element_type=jnp.float32,
    ).reshape(image_rows, inner)
    value_terms = jnp.einsum(
        "hqk,qhd->khd", prob_half[:, :, :image_rows], grad_heads, preferred_element_type=jnp.float32
    ).reshape(image_rows, inner)
    key_far, value_far = (
        partner(
            lax.dynamic_slice_in_dim(key_terms, far_start, local_rows, 0).astype(jnp.bfloat16),
            "seq",
            0,
        ).astype(jnp.float32),
        partner(
            lax.dynamic_slice_in_dim(value_terms, far_start, local_rows, 0).astype(jnp.bfloat16),
            "seq",
            0,
        ).astype(jnp.float32),
    )
    key_sum = lax.dynamic_slice_in_dim(key_terms, near_start, local_rows, 0) + key_far
    value_sum = lax.dynamic_slice_in_dim(value_terms, near_start, local_rows, 0) + value_far
    key_grad = (key_sum * factor).astype(jnp.bfloat16)
    value_grad = value_sum.astype(jnp.bfloat16)
    return (update[None], query_grad[None], key_grad[None], value_grad[None], down_grad, up_grad)


def solution(mesh):
    return jax.shard_map(
        local,
        mesh=mesh,
        in_specs=(
            P(("rep", "fsdp"), "seq", None),
            P(("rep", "fsdp"), "seq", None),
            P(("rep", "fsdp"), "seq", None),
            P(("rep", "fsdp"), None, None),
            P(("rep", "fsdp"), None, None),
            P(("rep", "fsdp"), "seq", None),
            P("fsdp", "seq"),
            P("fsdp", None),
            P(None, "fsdp"),
            P(("rep", "fsdp"), "seq", None),
        ),
        out_specs=(
            P(("rep", "fsdp"), "seq", None),
            P(("rep", "fsdp"), "seq", None),
            P(("rep", "fsdp"), "seq", None),
            P(("rep", "fsdp"), "seq", None),
            P(("rep", "fsdp", "seq"), None),
            P("rep", ("fsdp", "seq")),
        ),
        check_vma=False,
    )
```

profile of v0, /device:TPU:0, one launch (start us, length us, event | category | flops | bytes accessed | tf_op | source)
XLA Modules:
  0.0 300.1 jit_solution(4145482247313183524)
XLA Ops:
  8.8 84.8 %all-gather.5.cloned.1.call-done = bf16[1536,1536]{1,0:T(8,128)(2,1)} async-done(((bf16[192,1536]{1,0:T(8,128)(2,1)}), bf16[1536,1536]{1,0:T(8,128)(2,1)}) %all-gather.5.cloned.1.call-update) | async-done | bytes 4718608 | tf_op jit(solution)/shard_map/all_gather | solution.py:48
  93.7 0.9 copy-done.17
  95.1 2.5 all-gather.1
  97.6 1.2 copy.38
  99.0 0.9 copy.39
  99.9 0.9 copy.35
  100.9 2.4 all-gather
  103.2 1.2 copy.34
  104.4 31.0 %all_gather.22 = bf16[1536,128]{1,0:T(8,128)(2,1)S(1)} all-gather(bf16[192,128]{1,0:T(8,128)(2,1)S(1)} %copy-done.26), channel_id=1, replica_groups=mesh['rep'=2,'fsdp'=8,'seq'=2] {'fsdp'}, dimensions={0}, use_global_device_ids=true | all-gather | bytes 442368 | tf_op jit(solution)/shard_map/all_gather | solution.py:50
  135.4 1.9 bitcast_reduce_fusion
  140.0 32.7 %all_gather.23 = bf16[128,3072]{1,0:T(8,128)(2,1)S(1)} all-gather(bf16[128,384]{1,0:T(8,128)(2,1)S(1)} %copy-done.25), channel_id=1, replica_groups=mesh['rep'=2,'fsdp'=8,'seq'=2] {'fsdp'}, dimensions={1}, use_global_device_ids=true | all-gather | bytes 884736 | tf_op jit(solution)/shard_map/all_gather | solution.py:51
  172.6 0.9 copy-done.1
  174.5 1.1 convolution_multiply_fusion.1
  175.9 2.5 convolution_multiply_fusion
  178.5 7.1 %fusion.17 = f32[128,1536]{1,0:T(8,128)S(1)} fusion(bf16[1536,3072]{1,0:T(8,128)(2,1)} %all-gather.7.cloned.1.call-done, bf16[1,128,3072]{2,1,0:T(8,128)(2,1)S(1)} %copy-done), kind=kOutput, calls=%fused_computation.32 | convolution fusion | flops 1207959552 | bytes 11010048 | tf_op jit(solution)/shard_map/td,hd->th/dot_general | solution.py:83
  185.6 1.0 fusion.2
  186.6 1.9 copy.43
  188.5 1.1 fusion.14
  189.6 2.3 multiply_convert_fusion
  192.0 1.3 fusion.7
  195.1 0.9 constant_dynamic-slice_fusion.1
  196.8 0.9 copy.55
  197.7 1.4 copy.76
  199.1 1.9 copy.77
  201.1 0.9 constant_dynamic-slice_fusion.3
  202.0 2.3 copy.74
  205.1 1.2 copy.75
  206.8 5.2 %fusion.26 = f32[128,3072]{1,0:T(8,128)S(1)} fusion(bf16[128,1536]{0,1:T(8,128)(2,1)S(1)} %bitcast.74, bf16[1536,3072]{1,0:T(8,128)(2,1)} %all-gather.7.cloned.1.call-done), kind=kOutput, calls=%fused_computation.50 | convolution fusion | flops 1207959552 | bytes 11403264 | tf_op jit(solution)/shard_map/dot_general | solution.py:80
  212.0 1.2 fusion.1
  213.3 0.9 fusion.20
  215.0 14.7 %reduce-scatter.3.cloned.1.call-done = f32[96,128]{1,0:T(8,128)} async-done(((f32[1536,128]{1,0:T(8,128)}), f32[96,128]{1,0:T(8,128)}) %reduce-scatter.3.cloned.1.call-update) | async-done | bytes 49168 | tf_op jit(solution)/shard_map/reduce_scatter | solution.py:96
  229.7 63.0 %reduce-scatter.5.cloned.1.call-done = f32[128,192]{0,1:T(8,128)} async-done(((f32[128,3072]{0,1:T(8,128)}), f32[128,192]{0,1:T(8,128)}) %reduce-scatter.5.cloned.1.call-update) | async-done | bytes 98320 | tf_op jit(solution)/shard_map/reduce_scatter | solution.py:97
  (81 shorter events, 10.2 us)
Async XLA Ops:
  8.0 165.5 %copy-start = (bf16[1,128,3072]{2,1,0:T(8,128)(2,1)S(1)}, bf16[1,128,3072]{2,1,0:T(8,128)(2,1)}, u32[]{:S(2)}) copy-start(bf16[1,128,3072]{2,1,0:T(8,128)(2,1)} %param.19) | copy-start | bytes 2359300
  8.0 85.6 %all-gather.5.cloned.1.call-start = ((), (), s32[]{:S(2)}) async-start(), calls=%async_computation.2 | async-start | bytes 5308416 | tf_op jit(solution)/shard_map/all_gather | solution.py:48
  8.7 169.7 %all-gather.7.cloned.1.call-start = ((), (), s32[]{:S(2)}) async-start(), calls=%async_computation.3 | async-start | bytes 14155776 | tf_op jit(solution)/shard_map/all_gather | solution.py:78
  93.6 1.0 copy-start.17
  93.6 1.2 copy-start.18
  93.7 136.0 %reduce-scatter.3.cloned.1.call-start = ((), (), s32[]{:S(2)}) async-start(), calls=%async_computation.4 | async-start | bytes 835584 | tf_op jit(solution)/shard_map/reduce_scatter | solution.py:96
  94.9 40.5 %copy-start.6 = (bf16[1,128,1536]{1,2,0:T(8,128)(2,1)}, bf16[1,128,1536]{1,2,0:T(8,128)(2,1)S(1)}, u32[]{:S(2)}) copy-start(bf16[1,128,1536]{1,2,0:T(8,128)(2,1)S(1)} %copy.40) | copy-start | bytes 1179652
  95.1 3.7 %copy-start.19 = (bf16[1,128,1536]{2,1,0:T(8,128)(2,1)S(1)}, bf16[1,128,1536]{2,1,0:T(8,128)(2,1)}, u32[]{:S(2)}) copy-start(bf16[1,128,1536]{2,1,0:T(8,128)(2,1)} %param.13) | copy-start | bytes 1179652
  97.6 2.3 copy-start.20
  98.8 2.1 copy-start.22
  99.9 4.5 %copy-start.26 = (bf16[192,128]{1,0:T(8,128)(2,1)S(1)}, bf16[192,128]{1,0:T(8,128)(2,1)}, u32[]{:S(2)}) copy-start(bf16[192,128]{1,0:T(8,128)(2,1)} %param.17) | copy-start | bytes 147460
  135.4 4.0 %copy-start.4 = (bf16[1536,128]{1,0:T(8,128)(2,1)}, bf16[1536,128]{1,0:T(8,128)(2,1)S(1)}, u32[]{:S(2)}) copy-start(bf16[1536,128]{1,0:T(8,128)(2,1)S(1)} %all_gather.22) | copy-start | bytes 1179652
  137.7 1.1 copy-start.10
  137.7 1.2 copy-start.13
  138.1 1.3 copy-start.8
  138.9 1.1 copy-start.25
  140.0 34.0 %copy-start.15 = (f32[128,128]{1,0:T(8,128)}, f32[128,128]{1,0:T(8,128)S(1)}, u32[]{:S(2)}) copy-start(f32[128,128]{1,0:T(8,128)S(1)} %convolution_add_fusion.2) | copy-start | bytes 196612
  172.6 0.9 copy-start.1
  175.7 117.0 %reduce-scatter.5.cloned.1.call-start = ((), (), s32[]{:S(2)}) async-start(), calls=%async_computation.5 | async-start | bytes 1671168 | tf_op jit(solution)/shard_map/reduce_scatter | solution.py:97
  178.4 7.1 %copy-start.5 = (bf16[1536,128]{1,0:T(8,128)(2,1)S(1)}, bf16[1536,128]{1,0:T(8,128)(2,1)}, u32[]{:S(2)}) copy-start(bf16[1536,128]{1,0:T(8,128)(2,1)} %copy-done.4) | copy-start | bytes 1179652
  178.5 7.1 %copy-start.24 = (bf16[128,128]{1,0:T(8,128)(2,1)S(1)}, bf16[128,128]{1,0:T(8,128)(2,1)}, u32[]{:S(2)}) copy-start(bf16[128,128]{1,0:T(8,128)(2,1)} %copy-done.23) | copy-start | bytes 98308
  189.6 2.3 copy-start.12
  189.6 2.3 copy-start.14
  192.0 1.3 copy-start.7
  193.3 1.0 copy-start.3
  193.3 1.4 copy-start.9
  195.0 1.8 copy-start.21
  206.3 5.8 %copy-start.2 = (bf16[128,3072]{1,0:T(8,128)(2,1)S(1)}, bf16[128,3072]{1,0:T(8,128)(2,1)}, u32[]{:S(2)}) copy-start(bf16[128,3072]{1,0:T(8,128)(2,1)} %copy-done.1) | copy-start | bytes 2359300
  206.3 5.8 %copy-start.16 = (f32[128,128]{1,0:T(8,128)S(1)}, f32[128,128]{1,0:T(8,128)}, u32[]{:S(2)}) copy-start(f32[128,128]{1,0:T(8,128)} %copy-done.15) | copy-start | bytes 196612
  206.3 7.0 %collective-permute-start = (bf16[128,1536]{1,0:T(8,128)(2,1)S(1)}, bf16[128,1536]{1,0:T(8,128)(2,1)S(1)}, u32[]{:S(2)}, u32[]{:S(2)}) collective-permute-start(bf16[128,1536]{1,0:T(8,128)(2,1)S(1)} %copy.75), channel_id=1, source_target_pairs={{0,1},{1,0},{2,3},{3,2},{4,5},{5,4},{6,7},{7,6},{8,9},{9,8},{10,11... | collective-permute-start | bytes 1179656 | tf_op jit(solution)/shard_map/ppermute | solution.py:12
  206.4 7.8 %collective-permute-start.1 = (bf16[128,1536]{1,0:T(8,128)(2,1)}, bf16[128,1536]{1,0:T(8,128)(2,1)S(1)}, u32[]{:S(2)}, u32[]{:S(2)}) collective-permute-start(bf16[128,1536]{1,0:T(8,128)(2,1)} %copy.77), channel_id=1, source_target_pairs={{0,1},{1,0},{2,3},{3,2},{4,5},{5,4},{6,7},{7,6},{8,9},{9,8},{10,11... | collective-permute-start | bytes 1179656 | tf_op jit(solution)/shard_map/ppermute | solution.py:12
  212.0 1.3 copy-start.11
  (2 other events, 1.4 us)
Sparse Core Ops, SparseCore 0:
  11.0 82.5 all-gather.4
  95.2 19.9 all-gather.6
Sparse Core Ops, SparseCore 1:
  175.8 53.8 reduce-scatter.2
  234.2 58.4 reduce-scatter.4
where the time goes:
time: 301 us; the launch traced here: 300 us
  waiting for transfers between devices  163 us (54%)
  blocking collectives  68.5 us (23%)
  matrix products  25.4 us (8%)
  local copies, waits for them, and re-layouts  22.5 us (7%)
  between operations  15.9 us (5%)
  other arithmetic  3.65 us (1%)
    all_gather x1, waiting for transfers between devices, local(): half_out = lax.all_gather(proj_out, 'fsdp', axis=0, tiled=True)  84.8 us
    reduce_scatter x1, waiting for transfers between devices, local(): lax.psum_scatter(up_term, ('fsdp', 'seq'), scatter_dimension=1, tiled=True)  63 us
    all_gather x1, blocking collectives, local(): lax.all_gather(adapter_up, 'fsdp', axis=1, tiled=True)  32.7 us
    all_gather x1, blocking collectives, local(): lax.all_gather(adapter_down, 'fsdp', axis=0, tiled=True)  31 us
    reduce_scatter x1, waiting for transfers between devices, local(): lax.psum_scatter(down_term, ('fsdp', 'seq'), scatter_dimension=0, tiled=T...  14.7 us
    unnamed x65, local copies, waits for them, and re-layouts  13.8 us
    dot_general x1, matrix products, local(): jnp.einsum('td,hd->th', cot_rows, full_out, preferred_element_type=jnp.fl...  7.06 us
  transfers between devices with their start and end apart: 6, of which 3 were waited for; matrix products, arithmetic and copies ran while one was open for 16% of the time, Pallas kernels for 0%

commit v1 on v0

v1 whole, which is shorter than its diff:
```python
import functools

import jax
import jax.numpy as jnp
from jax import lax
from jax.experimental import pallas as pl
from jax.experimental.pallas import tpu as pltpu
from jax.sharding import PartitionSpec as P

HD = 128
BATCHES = 4
ORDER = (0, 2, 4, 6, 1, 3, 5, 7)
FACTOR = HD ** (-0.5)
F32 = jnp.float32
BF16 = jnp.bfloat16
ROWS = (((0,), (0,)), ((), ()))
COLS = (((1,), (1,)), ((), ()))


def swap(value, axis, mask):
    pairs = [(source, source ^ mask) for source in range(lax.axis_size(axis))]
    return lax.ppermute(value, axis, pairs)


def ring_after(z):
    low, high = z % 2, z // 2
    return 2 * low + (1 - high)


def ring_before(z):
    low, high = z % 2, z // 2
    return 2 * (1 - low) + high


def ring_step(value):
    pairs = []
    for f in range(8):
        z, x = f // 2, f % 2
        pairs.append((f, ring_after(z) * 2 + x))
        pairs.append((8 + f, 8 + ring_before(z) * 2 + x))
    return lax.ppermute(value, ("rep", "fsdp"), pairs)


def dot(a, b, dims=None):
    if dims is None:
        return jnp.dot(a, b, preferred_element_type=F32)
    return lax.dot_general(a, b, dims, preferred_element_type=F32)


def batch_places(grouped):
    if not grouped:
        return list(range(BATCHES)), 0
    f = lax.axis_index("fsdp")
    rep = lax.axis_index("rep")
    z, x = f // 2, f % 2
    after, before = ring_after(z), ring_before(z)
    first = jnp.where(rep == 0, before, after)
    second = jnp.where(rep == 0, after, before)
    return [z, first, second, 3 - z], x


def softmax_parts(q, k):
    scores = dot(q, k, COLS) * FACTOR
    top = jnp.max(scores, -1, keepdims=True)
    weight = jnp.exp(scores - top)
    return weight * (1.0 / jnp.sum(weight, -1, keepdims=True))


def start_all(copies):
    for copy in copies:
        copy.start()


def forward_kernel(q, ko, kf, kt, vo, vf, vt, attn, keys, values, sems):
    rows, inner = q.shape
    copies = [
        pltpu.make_async_copy(source, target.at[pl.ds(i * rows, rows)], sems.at[j, i])
        for j, (sources, target) in enumerate((((ko, kf, kt), keys), ((vo, vf, vt), values)))
        for i, source in enumerate(sources)
    ]
    start_all(copies)
    for copy in copies:
        copy.wait()
    for h in range(inner // HD):
        c = slice(h * HD, (h + 1) * HD)
        prob = softmax_parts(q[:, c], keys[:, c]).astype(BF16)
        attn[:, c] = dot(prob, values[:, c]).astype(BF16)


def adapter_kernel(packed, scale, *refs):
    if packed:
        (mine, theirs, attn, cot, hint, down, up, act, act_grad, near, far, terms, sems) = refs
        f = lax.axis_index("fsdp")
        core = lax.axis_index("seq")
        copies = []
        for side, source in enumerate((mine, theirs)):
            half = core if side == 0 else 1 - core
            for place, mask in enumerate(ORDER):
                block = f ^ mask
                copies.append(
                    pltpu.make_async_copy(
                        source.at[place, pl.ds(0, 96)],
                        down.at[pl.ds(pl.multiple_of(block * 192 + half * 96, 32), 96)],
                        sems.at[len(copies)],
                    )
                )
                for j in range(3):
                    copies.append(
                        pltpu.make_async_copy(
                            source.at[place, pl.ds(96 + 64 * j, 64)],
                            up.at[
                                pl.ds(pl.multiple_of(half * 64, 64), 64),
                                pl.ds(pl.multiple_of(block * 384 + 128 * j, 128), 128),
                            ],
                            sems.at[len(copies)],
                        )
                    )
    else:
        (down_in, up_in, attn, cot, hint, down, up, act, act_grad, down_term, up_term, sems) = refs
        copies = [
            pltpu.make_async_copy(down_in, down, sems.at[0]),
            pltpu.make_async_copy(up_in, up, sems.at[1]),
        ]
    start_all(copies)
    for copy in copies:
        copy.wait()
    pre_act = dot(attn[...], down[...]) + hint[...].astype(F32)
    logistic = 1.0 / (1.0 + jnp.exp(-pre_act))
    act[...] = (pre_act * logistic).astype(BF16)
    act_back = dot(cot[...], up[...], COLS)
    act_grad[...] = (act_back * logistic * (1.0 + pre_act * (1.0 - logistic))).astype(BF16)
    inner, wide = attn.shape[1], cot.shape[1]
    if not packed:
        down_term[...] = dot(attn[...], act_grad[...], ROWS) * scale
        up_term[...] = dot(cot[...], act[...], ROWS) * scale
        return
    terms[pl.ds(0, inner)] = dot(attn[...], act_grad[...], ROWS) * scale
    terms[pl.ds(inner, wide)] = dot(cot[...], act[...], ROWS) * scale
    for place, mask in enumerate(ORDER):
        block = f ^ mask
        for target, half in ((near, core), (far, 1 - core)):
            piece = block * 2 + half
            target[place, 0:96] = terms[pl.ds(pl.multiple_of(piece * 96, 32), 96)]
            target[place, 96:288] = terms[pl.ds(pl.multiple_of(inner + piece * 192, 64), 192)]


def project_kernel(grouped, numbers, last, *refs):
    count = len(numbers)
    pieces = refs[: 2 * count]
    attn_own, attn_far, cot, cot_far = refs[2 * count : 2 * count + 4]
    rest = refs[2 * count + 4 :]
    total_in = None
    if numbers[0] > 0:
        total_in, rest = rest[0], rest[1:]
    if last:
        near, far, own, away, weights, sems = rest
    else:
        near, far, total, weights, sems = rest
    places, x = batch_places(grouped)
    core = lax.axis_index("seq")
    rows = attn_own.shape[0]
    depth = pieces[0].shape[0]
    half = pieces[0].shape[1]
    copies = []
    for i in range(count):
        for j in range(2):
            where = x if j == 0 else 1 - x
            start = where * depth if isinstance(x, int) else pl.multiple_of(where * depth, 32)
            copies.append(
                pltpu.make_async_copy(
                    pieces[2 * i + j], weights.at[i, pl.ds(start, depth)], sems.at[2 * i + j]
                )
            )
    start_all(copies)
    columns = pl.ds(pl.multiple_of(core * half, 128), half)
    cot_rows = jnp.concatenate([cot[:, columns], cot_far[...]], 0)
    total_now = total_in[...] if total_in is not None else None
    for i, number in enumerate(numbers):
        copies[2 * i].wait()
        copies[2 * i + 1].wait()
        back = dot(cot_rows, weights[i], COLS)
        near[:, i * 2 * depth : (i + 1) * 2 * depth] = back[:rows]
        far[:, i * 2 * depth : (i + 1) * 2 * depth] = back[rows:]
        place = pl.ds(pl.multiple_of(places[number] * 2 * depth, 128), 2 * depth)
        attn_rows = jnp.concatenate([attn_own[:, place], attn_far[:, place]], 0)
        term = dot(attn_rows, weights[i])
        total_now = term if total_now is None else total_now + term
    if last:
        own[...] = total_now[:rows]
        away[...] = total_now[rows:].astype(BF16)
    else:
        total[...] = total_now


def backward_kernel(grouped, numbers, *refs):
    (q, ko, kf, kt, vo, vf, vt, attn, near, far, act_grad, down) = refs[:12]
    dq, own, away, qs, keys, values, attns, downs, sems = refs[12:]
    count = len(numbers)
    rows = q.shape[0]
    width = qs.shape[2]
    places, _ = batch_places(grouped)
    copies = []
    for i, number in enumerate(numbers):
        place = pl.ds(pl.multiple_of(places[number] * width, 128), width)
        moves = [(q.at[:, place], qs.at[i]), (attn.at[:, place], attns.at[i])]
        moves.append((down.at[place], downs.at[i]))
        for j, (k, v) in enumerate(((ko, vo), (kf, vf), (kt, vt))):
            moves.append((k.at[:, place], keys.at[i, pl.ds(j * rows, rows)]))
            moves.append((v.at[:, place], values.at[i, pl.ds(j * rows, rows)]))
        group = [
            pltpu.make_async_copy(source, target, sems.at[i, j])
            for j, (source, target) in enumerate(moves)
        ]
        start_all(group)
        copies.append(group)
    for i in range(count):
        for copy in copies[i]:
            copy.wait()
        span = slice(i * width, (i + 1) * width)
        grad = (near[:, span] + far[:, span] + dot(act_grad[...], downs[i], COLS)).astype(BF16)
        for h in range(width // HD):
            c = slice(h * HD, (h + 1) * HD)
            o = slice(i * width + h * HD, i * width + (h + 1) * HD)
            prob = softmax_parts(qs[i, :, c], keys[i, :, c])
            prob_half = prob.astype(BF16)
            head = grad[:, c]
            delta = jnp.sum(head.astype(F32) * attns[i, :, c].astype(F32), -1, keepdims=True)
            prob_grad = dot(head, values[i, :, c], COLS)
            score_grad = (prob * (prob_grad - delta)).astype(BF16)
            dq[:, o] = (dot(score_grad, keys[i, :, c]) * FACTOR).astype(BF16)
            key_term = dot(score_grad[:, : 2 * rows], qs[i, :, c], ROWS)
            value_term = dot(prob_half[:, : 2 * rows], head, ROWS)
            own[0, :, o] = key_term[:rows]
            own[1, :, o] = value_term[:rows]
            away[0, :, o] = key_term[rows:].astype(BF16)
            away[1, :, o] = value_term[rows:].astype(BF16)


def finish_kernel(grouped, groups, *refs):
    count = len(groups)
    dq_parts, owns, aways = refs[:count], refs[count : 2 * count], refs[2 * count : 3 * count]
    own, away, act, up, update, dq, dk, dv = refs[3 * count :]
    places, _ = batch_places(grouped)
    core = lax.axis_index("seq")
    half = own.shape[1]
    for c, term in ((core, own[...]), (1 - core, away[...].astype(F32))):
        columns = pl.ds(pl.multiple_of(c * half, 128), half)
        update[:, columns] = (term + dot(act[...], up[:, columns])).astype(BF16)
    width = dq.shape[1] // BATCHES
    for g, numbers in enumerate(groups):
        for i, number in enumerate(numbers):
            place = pl.ds(pl.multiple_of(places[number] * width, 128), width)
            o = slice(i * width, (i + 1) * width)
            dq[:, place] = dq_parts[g][:, o]
            for j, target in enumerate((dk, dv)):
                value = owns[g][j, :, o] + aways[g][j, :, o].astype(F32)
                target[:, place] = (value * FACTOR if j == 0 else value).astype(BF16)


VMEM = pl.BlockSpec(memory_space=pltpu.VMEM)
ANY = pl.BlockSpec(memory_space=pl.ANY)


def shape(dims, dtype=BF16):
    return jax.ShapeDtypeStruct(dims, dtype)


def call(kernel, args, outs, in_specs, scratch, flops, megabytes):
    moved = sum(a.size * a.dtype.itemsize for a in (*args, *outs))
    return pl.pallas_call(
        kernel,
        out_shape=outs,
        in_specs=in_specs,
        out_specs=[VMEM] * len(outs),
        scratch_shapes=scratch,
        compiler_params=pltpu.CompilerParams(vmem_limit_bytes=megabytes * 2**20),
        cost_estimate=pl.CostEstimate(flops=flops, bytes_accessed=moved, transcendentals=0),
    )(*args)


def local(
    queries,
    image_keys,
    image_values,
    text_keys,
    text_values,
    control_hint,
    proj_out,
    adapter_down,
    adapter_up,
    cotangent,
):
    shards = lax.axis_size("fsdp")
    grouped = shards == 8 and lax.axis_size("rep") == 2 and lax.axis_size("seq") == 2
    q, ko, vo = queries[0], image_keys[0], image_values[0]
    kt, vt, hint, cot = text_keys[0], text_values[0], control_hint[0], cotangent[0]
    rows, inner = q.shape
    wide = cot.shape[1]
    half = proj_out.shape[1]
    rank = hint.shape[1]
    depth = inner // (2 * BATCHES)
    width = 2 * depth
    core = lax.axis_index("seq")
    scale = float(shards * lax.axis_size("seq") * rows) ** (-0.5)

    if grouped:
        z1 = ring_step(proj_out)
        x1 = swap(proj_out, "fsdp", 1)
        down_half = lax.dynamic_slice_in_dim(adapter_down, core * 96, 96, 0)
        up_half = lax.dynamic_slice_in_dim(adapter_up, core * 64, 64, 0)
        block = jnp.concatenate([down_half] + [up_half[:, 128 * j : 128 * j + 128] for j in range(3)], 0)[None]
        block = jnp.concatenate([block, swap(block, "fsdp", 2)], 0)
        both = swap(block, "fsdp", 4)
        block = jnp.concatenate([block, both], 0)
        mine = jnp.concatenate([block, swap(block, "fsdp", 1)], 0)
        theirs = swap(mine, "seq", 1)
        kf, vf = swap(ko, "seq", 1), swap(vo, "seq", 1)
        z2 = ring_step(z1)
        x2 = swap(z1, "fsdp", 1)
        y1 = swap(z1, "rep", 1)
        x3 = swap(z2, "fsdp", 1)
        y2 = swap(x2, "rep", 1)
        pieces = [proj_out, x1, z1, x2, y1, y2, z2, x3]
        adapters = (mine, theirs)
    else:
        half_out = lax.all_gather(proj_out, "fsdp", axis=0, tiled=True)
        pieces = [half_out[i * depth : (i + 1) * depth] for i in range(2 * BATCHES)]
        adapters = (
            lax.all_gather(adapter_down, "fsdp", axis=0, tiled=True),
            lax.all_gather(adapter_up, "fsdp", axis=1, tiled=True),
        )
        kf, vf = swap(ko, "seq", 1), swap(vo, "seq", 1)
    cot_far = swap(lax.dynamic_slice_in_dim(cot, (1 - core) * half, half, 1), "seq", 1)

    attention_flops = 2 * rows * 3 * rows * inner
    (attn,) = call(
        forward_kernel,
        (q, ko, kf, kt, vo, vf, vt),
        [shape((rows, inner))],
        [VMEM] + [ANY] * 6,
        [
            pltpu.VMEM((3 * rows, inner), BF16),
            pltpu.VMEM((3 * rows, inner), BF16),
            pltpu.SemaphoreType.DMA((2, 3)),
        ],
        40 * attention_flops,
        16,
    )
    attn_far = swap(attn, "seq", 1)
    outs = [
        shape((inner, rank)),
        shape((rank, wide)),
        shape((rows, rank)),
        shape((rows, rank)),
    ]
    if grouped:
        outs += [shape((8, 288, rank), F32)] * 2
        scratch = [pltpu.VMEM((inner + wide, rank), F32), pltpu.SemaphoreType.DMA((64,))]
    else:
        outs += [shape((inner, rank), F32), shape((wide, rank), F32)]
        scratch = [pltpu.SemaphoreType.DMA((2,))]
    down, up, act, act_grad, first_term, second_term = call(
        functools.partial(adapter_kernel, grouped, scale),
        (*adapters, attn, cot, hint),
        outs,
        [ANY, ANY, VMEM, VMEM, VMEM],
        scratch,
        40 * rows * (inner + wide) * rank,
        24,
    )
    if grouped:
        term = first_term + swap(second_term, "seq", 1)
        for mask in (1, 4, 2):
            keep = term.shape[0] // 2
            term = term[:keep] + swap(term[keep:].astype(BF16), "fsdp", mask).astype(F32)
        down_grad, up_grad = term[0, :96], term[0, 96:].T
    else:
        down_grad = lax.psum_scatter(first_term, ("fsdp", "seq"), scatter_dimension=0, tiled=True)
        up_grad = lax.psum_scatter(second_term, ("fsdp", "seq"), scatter_dimension=0, tiled=True).T

    groups = ((0, 1), (2, 3))
    total = None
    dqs, owns, aways = [], [], []
    for numbers in groups:
        count = len(numbers)
        last = numbers[-1] == BATCHES - 1
        args = [pieces[2 * n + j] for n in numbers for j in range(2)] + [attn, attn_far, cot, cot_far]
        if total is not None:
            args.append(total)
        outs = [shape((rows, count * width), F32)] * 2
        if last:
            outs += [shape((rows, half), F32), shape((rows, half))]
        else:
            outs += [shape((2 * rows, half), F32)]
        results = call(
            functools.partial(project_kernel, grouped, numbers, last),
            tuple(args),
            outs,
            [ANY] * (2 * count) + [VMEM] * (len(args) - 2 * count),
            [pltpu.VMEM((count, width, half), BF16), pltpu.SemaphoreType.DMA((2 * count,))],
            8 * 2 * rows * count * width * half * 2,
            24,
        )
        near, far = results[:2]
        if last:
            own_update, away_update = results[2], swap(results[3], "seq", 1)
        else:
            total = results[2]
        dq, own, away = call(
            functools.partial(backward_kernel, grouped, numbers),
            (q, ko, kf, kt, vo, vf, vt, attn, near, swap(far, "seq", 1), act_grad, down),
            [
                shape((rows, count * width)),
                shape((2, rows, count * width), F32),
                shape((2, rows, count * width)),
            ],
            [ANY] * 8 + [VMEM] * 3 + [ANY],
            [
                pltpu.VMEM((count, rows, width), BF16),
                pltpu.VMEM((count, 3 * rows, width), BF16),
                pltpu.VMEM((count, 3 * rows, width), BF16),
                pltpu.VMEM((count, rows, width), BF16),
                pltpu.VMEM((count, width, rank), BF16),
                pltpu.SemaphoreType.DMA((count, 9)),
            ],
            60 * attention_flops,
            16,
        )
        dqs.append(dq)
        owns.append(own)
        aways.append(swap(away, "seq", 1))
    update, query_grad, key_grad, value_grad = call(
        functools.partial(finish_kernel, grouped, groups),
        (*dqs, *owns, *aways, own_update, away_update, act, up),
        [shape((rows, wide))] + [shape((rows, inner))] * 3,
        [VMEM] * (3 * len(groups) + 4),
        [],
        2 * rows * rank * wide,
        24,
    )
    return (update[None], query_grad[None], key_grad[None], value_grad[None], down_grad, up_grad)


def solution(mesh):
    rows = P(("rep", "fsdp"), "seq", None)
    text = P(("rep", "fsdp"), None, None)
    return jax.shard_map(
        local,
        mesh=mesh,
        in_specs=(
            rows,
            rows,
            rows,
            text,
            text,
            rows,
            P("fsdp", "seq"),
            P("fsdp", None),
            P(None, "fsdp"),
            rows,
        ),
        out_specs=(rows, rows, rows, rows, P(("rep", "fsdp", "seq"), None), P("rep", ("fsdp", "seq"))),
        check_vma=False,
    )
```

time: 301 us -> 102 us (0.34)
  waiting for transfers between devices: 163 us -> 47.7 us
  blocking collectives: 68.5 us -> 0 us
  matrix products: 25.4 us -> 0 us
  Pallas kernels: 0 us -> 24.3 us
  starting transfers between devices: 0.91 us -> 22.6 us
  local copies, waits for them, and re-layouts: 22.5 us -> 4.01 us
  between operations: 15.9 us -> 0.91 us
    all_gather x2 -> x0, waiting for transfers between devices: 84.9 us -> none  [the longest x1 84.8 us: local(): half_out = lax.all_gather(proj_out, 'fsdp', axis=0, tiled=True)]
    reduce_scatter x2 -> x0, waiting for transfers between devices: 77.6 us -> none  [the longest x1 63 us: local(): lax.psum_scatter(up_term, ('fsdp', 'seq'), scatter_dimension=1, tiled=True)]
    all_gather x4 -> x0, blocking collectives: 68.5 us -> none  [the longest x1 32.7 us: local(): lax.all_gather(adapter_up, 'fsdp', axis=1, tiled=True)]
    ppermute x2 -> x24, waiting for transfers between devices: 0.01 us -> 47.7 us  [the longest x22 43 us: swap(): return lax.ppermute(value, axis, pairs)]
    dot_general x14 -> x0, matrix products: 25.4 us -> none  [the longest x1 7.06 us: local(): jnp.einsum('td,hd->th', cot_rows, full_out, preferred_element_type=jnp.fl...]
    pallas_call x0 -> x7, Pallas kernels: none -> 24.3 us  [call(): pl.pallas_call(kernel, out_shape=outs, in_specs=in_specs, out_specs=[VMEM...]
    ppermute x2 -> x24, starting transfers between devices: 0.57 us -> 22.6 us  [the longest x22 21 us: swap(): return lax.ppermute(value, axis, pairs)]
    unnamed x65 -> x22, local copies, waits for them, and re-layouts: 13.8 us -> 1.8 us
  transfers between devices with their start and end apart: 6 -> 24, of which waited for: 3 -> 12; matrix products, arithmetic and copies ran while one was open for 16% -> 1% of each run, Pallas kernels for 0% -> 24%
where the time goes in v1:
time: 102 us
  waiting for transfers between devices  47.7 us (47%)
  Pallas kernels  24.3 us (24%)
  starting transfers between devices  22.6 us (22%)
  local copies, waits for them, and re-layouts  4.01 us (4%)
  other arithmetic  2.06 us (2%)
    ppermute x22, waiting for transfers between devices, swap(): return lax.ppermute(value, axis, pairs)  43 us
    pallas_call x7, Pallas kernels, call(): pl.pallas_call(kernel, out_shape=outs, in_specs=in_specs, out_specs=[VMEM...  24.3 us
    ppermute x22, starting transfers between devices, swap(): return lax.ppermute(value, axis, pairs)  21 us
    ppermute x2, waiting for transfers between devices, ring_step(): return lax.ppermute(value, ('rep', 'fsdp'), pairs)  4.65 us
  transfers between devices with their start and end apart: 24, of which 12 were waited for; matrix products, arithmetic and copies ran while one was open for 1% of the time, Pallas kernels for 24%

profile of v1, /device:TPU:0, one launch (start us, length us, event | category | flops | bytes accessed | tf_op | source)
XLA Modules:
  0.0 101.6 jit_solution(15399512606052163339)
XLA Ops:
  0.7 0.8 copy-done
  1.4 0.8 constant_dynamic-slice_fusion
  2.3 3.1 %collective-permute-start.8 = (bf16[1,288,128]{2,1,0:T(8,128)(2,1)S(1)}, bf16[1,288,128]{2,1,0:T(8,128)(2,1)S(1)}, u32[]{:S(2)}, u32[]{:S(2)}) collective-permute-start(bf16[1,288,128]{2,1,0:T(8,128)(2,1)S(1)} %maximum_bitcast_fusion), channel_id=1, source_target_pairs={{0,4},{2,6},{4,0},{6,2},{8,12},{10,14},{12,8},{14,10},{1,5},{3,7},... | collective-permute-start | bytes 221192 | tf_op jit(solution)/shard_map/ppermute | solution.py:22
  5.4 2.3 %collective-permute-done.8 = bf16[1,288,128]{2,1,0:T(8,128)(2,1)S(1)} collective-permute-done((bf16[1,288,128]{2,1,0:T(8,128)(2,1)S(1)}, bf16[1,288,128]{2,1,0:T(8,128)(2,1)S(1)}, u32[]{:S(2)}, u32[]{:S(2)}) %collective-permute-start.8) | collective-permute-done | bytes 73760 | tf_op jit(solution)/shard_map/ppermute | solution.py:22
  7.7 3.1 %collective-permute-start.9 = (bf16[2,288,128]{2,1,0:T(8,128)(2,1)S(1)}, bf16[2,288,128]{2,1,0:T(8,128)(2,1)S(1)}, u32[]{:S(2)}, u32[]{:S(2)}) collective-permute-start(bf16[2,288,128]{2,1,0:T(8,128)(2,1)S(1)} %pad_maximum_fusion.2), channel_id=1, source_target_pairs={{0,8},{2,10},{4,12},{6,14},{8,0},{10,2},{12,4},{14,6},{1,9},{3,11}... | collective-permute-start | bytes 442376 | tf_op jit(solution)/shard_map/ppermute | solution.py:22
  10.8 5.9 %collective-permute-done.9 = bf16[2,288,128]{2,1,0:T(8,128)(2,1)S(1)} collective-permute-done((bf16[2,288,128]{2,1,0:T(8,128)(2,1)S(1)}, bf16[2,288,128]{2,1,0:T(8,128)(2,1)S(1)}, u32[]{:S(2)}, u32[]{:S(2)}) %collective-permute-start.9) | collective-permute-done | bytes 147488 | tf_op jit(solution)/shard_map/ppermute | solution.py:22
  16.7 0.8 pad_maximum_fusion.1
  17.5 1.5 %collective-permute-start.10 = (bf16[4,288,128]{2,1,0:T(8,128)(2,1)}, bf16[4,288,128]{2,1,0:T(8,128)(2,1)}, u32[]{:S(2)}, u32[]{:S(2)}) collective-permute-start(bf16[4,288,128]{2,1,0:T(8,128)(2,1)} %pad_maximum_fusion.1), channel_id=1, source_target_pairs={{0,2},{2,0},{4,6},{6,4},{8,10},{10,8},{12,14},{14,12},{1,3},{3,1},... | collective-permute-start | bytes 884744 | tf_op jit(solution)/shard_map/ppermute | solution.py:22
  20.7 7.0 %collective-permute-done.10 = bf16[4,288,128]{2,1,0:T(8,128)(2,1)} collective-permute-done((bf16[4,288,128]{2,1,0:T(8,128)(2,1)}, bf16[4,288,128]{2,1,0:T(8,128)(2,1)}, u32[]{:S(2)}, u32[]{:S(2)}) %collective-permute-start.10) | collective-permute-done | bytes 294944 | tf_op jit(solution)/shard_map/ppermute | solution.py:22
  27.7 1.1 %pad_maximum_fusion.refs_0_ = bf16[8,288,128]{2,1,0:T(8,128)(2,1)S(1)} fusion(bf16[4,288,128]{2,1,0:T(8,128)(2,1)} %collective-permute-done.10, bf16[2,288,128]{2,1,0:T(8,128)(2,1)} %copy-done.10, bf16[1,288,128]{2,1,0:T(8,128)(2,1)S(1)} %collective-permute-done.8, bf16[1,288,128]{2,1,0:T(8,128)(2,1)S(1)} %maximum_bitcast_fusion), kind=kLoop, calls=%fused_computation.2 | loop fusion | flops 884736 | bytes 1179648 | tf_op jit(solution)/shard_map/concatenate | solution.py:315
  29.5 4.3 %collective-permute-done.3.refs_2_ = bf16[192,1536]{1,0:T(8,128)(2,1)S(1)} collective-permute-done((bf16[192,1536]{1,0:T(8,128)(2,1)S(1)}, bf16[192,1536]{1,0:T(8,128)(2,1)S(1)}, u32[]{:S(2)}, u32[]{:S(2)}) %collective-permute-start.3) | collective-permute-done | bytes 589856 | tf_op jit(solution)/shard_map/ppermute | solution.py:41
  33.8 1.0 collective-permute-start.14
  35.3 1.0 copy-done.7
  36.3 5.8 %shard_map.145.refs_4_.refs_2_.refs_7_ = bf16[128,1536]{1,0:T(8,128)(2,1)S(1)} custom-call(bf16[128,1536]{1,0:T(8,128)(2,1)S(1)} %bitcast.24, bf16[128,1536]{1,0:T(8,128)(2,1)S(1)} %bitcast.28, bf16[128,1536]{1,0:T(8,128)(2,1)} %collective-permute-done.kf.refs_2_, bf16[128,1536]{1,0:T(8,128)(2,1)S(1)} %bitcast.31, bf16[128,1536]{1,0:T(8,128)(2,1)S(1)} %bitcast.35, ...), custom_call_target="tpu_custom_call" | custom-call | flops 6039797760 | bytes 3145728 | tf_op jit(solution)/shard_map/pallas_call | solution.py:270
  42.2 3.0 %shard_map.147 = (bf16[1536,128]{1,0:T(8,128)(2,1)S(1)}, bf16[128,3072]{1,0:T(8,128)(2,1)S(1)}, bf16[128,128]{1,0:T(8,128)(2,1)S(1)}, bf16[128,128]{1,0:T(8,128)...) custom-call(bf16[8,288,128]{2,1,0:T(8,128)(2,1)S(1)} %pad_maximum_fusion.refs_0_, ...), custom_call_target="tpu_custom_call" | custom-call | flops 3019898880 | bytes 5996544 | tf_op jit(solution)/shard_map/pallas_call | solution.py:270
  45.8 1.5 %collective-permute-start.12 = (bf16[192,1536]{1,0:T(8,128)(2,1)S(1)}, bf16[192,1536]{1,0:T(8,128)(2,1)S(1)}, u32[]{:S(2)}, u32[]{:S(2)}) collective-permute-start(bf16[192,1536]{1,0:T(8,128)(2,1)S(1)} %collective-permute-done.3.refs_2_), channel_id=1, source_target_pairs={{0,16},{16,0},{1,17},{17,1},{2,18},{18,2},{3,19},{19,3},{4,20},{20... | collective-permute-start | bytes 1769480 | tf_op jit(solution)/shard_map/ppermute | solution.py:22
  47.7 1.2 %collective-permute-start.15 = (bf16[192,1536]{1,0:T(8,128)(2,1)S(1)}, bf16[192,1536]{1,0:T(8,128)(2,1)S(1)}, u32[]{:S(2)}, u32[]{:S(2)}) collective-permute-start(bf16[192,1536]{1,0:T(8,128)(2,1)S(1)} %collective-permute-done.14.refs_2_), channel_id=1, source_target_pairs={{0,2},{2,0},{4,6},{6,4},{8,10},{10,8},{12,14},{14,12},{1,3},{3,1},... | collective-permute-start | bytes 1769480 | tf_op jit(solution)/shard_map/ppermute | solution.py:22
  48.8 2.9 %collective-permute-done.4.refs_3_ = bf16[192,1536]{1,0:T(8,128)(2,1)S(1)} collective-permute-done((bf16[192,1536]{1,0:T(8,128)(2,1)S(1)}, bf16[192,1536]{1,0:T(8,128)(2,1)S(1)}, u32[]{:S(2)}, u32[]{:S(2)}) %collective-permute-start.4) | collective-permute-done | bytes 589856 | tf_op jit(solution)/shard_map/ppermute | solution.py:22
  51.7 2.8 %collective-permute-start.13 = (bf16[192,1536]{1,0:T(8,128)(2,1)S(1)}, bf16[192,1536]{1,0:T(8,128)(2,1)S(1)}, u32[]{:S(2)}, u32[]{:S(2)}) collective-permute-start(bf16[192,1536]{1,0:T(8,128)(2,1)S(1)} %collective-permute-done.4.refs_3_), channel_id=1, source_target_pairs={{0,16},{16,0},{1,17},{17,1},{2,18},{18,2},{3,19},{19,3},{4,20},{20... | collective-permute-start | bytes 1769480 | tf_op jit(solution)/shard_map/ppermute | solution.py:22
  54.5 2.6 %shard_map.146 = (f32[128,768]{1,0:T(8,128)S(1)}, f32[128,768]{1,0:T(8,128)S(1)}, f32[256,1536]{1,0:T(8,128)S(1)}) custom-call(bf16[192,1536]{1,0:T(8,128)(2,1)S(1)} %copy-done.2, bf16[192,1536]{1,0:T(8,128)(2,1)S(1)} %collective-permute-done.2.refs_1_, bf16[192,1536]{1,0:T(8,128)(2,1)S(1)} %collective-permute-done.3.refs_2_, ...), custom_call_target="tpu_custom_call" | custom-call | flops 4831838208 | bytes 6684672 | tf_op jit(solution)/shard_map/pallas_call | solution.py:270
  57.2 4.8 %collective-permute-done.12.refs_0_ = bf16[192,1536]{1,0:T(8,128)(2,1)S(1)} collective-permute-done((bf16[192,1536]{1,0:T(8,128)(2,1)S(1)}, bf16[192,1536]{1,0:T(8,128)(2,1)S(1)}, u32[]{:S(2)}, u32[]{:S(2)}) %collective-permute-start.12) | collective-permute-done | bytes 589856 | tf_op jit(solution)/shard_map/ppermute | solution.py:22
  62.0 1.4 %collective-permute-done.15.refs_3_ = bf16[192,1536]{1,0:T(8,128)(2,1)S(1)} collective-permute-done((bf16[192,1536]{1,0:T(8,128)(2,1)S(1)}, bf16[192,1536]{1,0:T(8,128)(2,1)S(1)}, u32[]{:S(2)}, u32[]{:S(2)}) %collective-permute-start.15) | collective-permute-done | bytes 589856 | tf_op jit(solution)/shard_map/ppermute | solution.py:22
  63.4 10.4 %collective-permute-done.13.refs_1_ = bf16[192,1536]{1,0:T(8,128)(2,1)S(1)} collective-permute-done((bf16[192,1536]{1,0:T(8,128)(2,1)S(1)}, bf16[192,1536]{1,0:T(8,128)(2,1)S(1)}, u32[]{:S(2)}, u32[]{:S(2)}) %collective-permute-start.13) | collective-permute-done | bytes 589856 | tf_op jit(solution)/shard_map/ppermute | solution.py:22
  73.8 2.7 %shard_map.149 = (f32[128,768]{1,0:T(8,128)S(1)}, f32[128,768]{1,0:T(8,128)S(1)}, f32[128,1536]{1,0:T(8,128)S(1)}, bf16[128,1536]{1,0:T(8,128)(2,1)S(1)}) custom-call(bf16[192,1536]{1,0:T(8,128)(2,1)S(1)} %collective-permute-done.12.refs_0_, bf16[192,1536]{1,0:T(8,128)(2,1)S(1)} %collective-permute-done.13.refs_1_, ...), custom_call_target="tpu_custom_call" | custom-call | flops 4831838208 | bytes 7864320 | tf_op jit(solution)/shard_map/pallas_call | solution.py:270
  76.7 1.6 %collective-permute-start.21 = (bf16[4,288,128]{2,1,0:T(8,128)(2,1)S(1)}, bf16[4,288,128]{2,1,0:T(8,128)(2,1)S(1)}, u32[]{:S(2)}, u32[]{:S(2)}) collective-permute-start(bf16[4,288,128]{2,1,0:T(8,128)(2,1)S(1)} %slice.63), channel_id=1, source_target_pairs={{0,2},{2,0},{4,6},{6,4},{8,10},{10,8},{12,14},{14,12},{1,3},{3,1},... | collective-permute-start | bytes 884744 | tf_op jit(solution)/shard_map/ppermute | solution.py:22
  78.3 4.2 %shard_map.148 = (bf16[128,768]{1,0:T(8,128)(2,1)S(1)}, f32[2,128,768]{2,1,0:T(8,128)S(1)}, bf16[2,128,768]{2,1,0:T(8,128)(2,1)S(1)}) custom-call(bf16[128,1536]{1,0:T(8,128)(2,1)S(1)} %bitcast.25, bf16[128,1536]{1,0:T(8,128)(2,1)S(1)} %bitcast.29, bf16[128,1536]{1,0:T(8,128)(2,1)} %collective-permute-done.kf.refs_2_, bf16[128,1536]{1,0:T(8,128)(2,1)S(1)} %bitcast.32, ...), custom_call_target="tpu_custom_call" | custom-call | flops 9059696640 | bytes 5734400 | tf_op jit(solution)/shard_map/pallas_call | solution.py:270
  83.1 3.1 %collective-permute-done.21 = bf16[4,288,128]{2,1,0:T(8,128)(2,1)S(1)} collective-permute-done((bf16[4,288,128]{2,1,0:T(8,128)(2,1)S(1)}, bf16[4,288,128]{2,1,0:T(8,128)(2,1)S(1)}, u32[]{:S(2)}, u32[]{:S(2)}) %collective-permute-start.21) | collective-permute-done | bytes 294944 | tf_op jit(solution)/shard_map/ppermute | solution.py:22
  86.3 2.3 %collective-permute-start.22 = (bf16[2,288,128]{2,1,0:T(8,128)(2,1)S(1)}, bf16[2,288,128]{2,1,0:T(8,128)(2,1)S(1)}, u32[]{:S(2)}, u32[]{:S(2)}) collective-permute-start(bf16[2,288,128]{2,1,0:T(8,128)(2,1)S(1)} %slice.64), channel_id=1, source_target_pairs={{0,8},{2,10},{4,12},{6,14},{8,0},{10,2},{12,4},{14,6},{1,9},{3,11}... | collective-permute-start | bytes 442376 | tf_op jit(solution)/shard_map/ppermute | solution.py:22
  88.6 4.2 %shard_map.150 = (bf16[128,768]{1,0:T(8,128)(2,1)S(1)}, f32[2,128,768]{2,1,0:T(8,128)S(1)}, bf16[2,128,768]{2,1,0:T(8,128)(2,1)S(1)}) custom-call(bf16[128,1536]{1,0:T(8,128)(2,1)S(1)} %bitcast.26, bf16[128,1536]{1,0:T(8,128)(2,1)S(1)} %bitcast.30, bf16[128,1536]{1,0:T(8,128)(2,1)} %collective-permute-done.kf.refs_2_, bf16[128,1536]{1,0:T(8,128)(2,1)S(1)} %bitcast.33, ...), custom_call_target="tpu_custom_call" | custom-call | flops 9059696640 | bytes 5734400 | tf_op jit(solution)/shard_map/pallas_call | solution.py:270
  93.0 2.9 %collective-permute-done.22 = bf16[2,288,128]{2,1,0:T(8,128)(2,1)S(1)} collective-permute-done((bf16[2,288,128]{2,1,0:T(8,128)(2,1)S(1)}, bf16[2,288,128]{2,1,0:T(8,128)(2,1)S(1)}, u32[]{:S(2)}, u32[]{:S(2)}) %collective-permute-start.22) | collective-permute-done | bytes 147488 | tf_op jit(solution)/shard_map/ppermute | solution.py:22
  96.3 1.6 %shard_map.151 = (bf16[128,3072]{1,0:T(8,128)(2,1)}, bf16[128,1536]{1,0:T(8,128)(2,1)}, bf16[128,1536]{1,0:T(8,128)(2,1)}, bf16[128,1536]{1,0:T(8,128)(2,1)}) custom-call(bf16[128,768]{1,0:T(8,128)(2,1)S(1)} %get-tuple-element.33.refs_0_, bf16[128,768]{1,0:T(8,128)(2,1)S(1)} %get-tuple-element.37.refs_1_, f32[2,128,768]{2,1,0:T(8,128)S(1)} %get-tuple-element.38.refs_2_, ...), custom_call_target="tpu_custom_call" | custom-call | flops 100663296 | bytes 6717440 | tf_op jit(solution)/shard_map/pallas_call | solution.py:270
  97.9 2.4 %collective-permute-done.23 = bf16[1,288,128]{2,1,0:T(8,128)(2,1)S(1)} collective-permute-done((bf16[1,288,128]{2,1,0:T(8,128)(2,1)S(1)}, bf16[1,288,128]{2,1,0:T(8,128)(2,1)S(1)}, u32[]{:S(2)}, u32[]{:S(2)}) %collective-permute-start.23) | collective-permute-done | bytes 73760 | tf_op jit(solution)/shard_map/ppermute | solution.py:22
  (61 shorter events, 6.6 us)
Async XLA Ops:
  0.6 18.4 %copy-start.2 = (bf16[192,1536]{1,0:T(8,128)(2,1)S(1)}, bf16[192,1536]{1,0:T(8,128)(2,1)}, u32[]{:S(2)}) copy-start(bf16[192,1536]{1,0:T(8,128)(2,1)} %refs_0_.1) | copy-start | bytes 1769476
  0.7 19.0 %copy-start.4 = (bf16[1,128,1536]{2,1,0:T(8,128)(2,1)S(1)}, bf16[1,128,1536]{2,1,0:T(8,128)(2,1)}, u32[]{:S(2)}) copy-start(bf16[1,128,1536]{2,1,0:T(8,128)(2,1)} %param.11) | copy-start | bytes 1179652
  1.4 27.4 %copy-start.1 = (bf16[1,128,3072]{2,1,0:T(8,128)(2,1)S(1)}, bf16[1,128,3072]{2,1,0:T(8,128)(2,1)}, u32[]{:S(2)}) copy-start(bf16[1,128,3072]{2,1,0:T(8,128)(2,1)} %param.19) | copy-start | bytes 2359300
  2.3 5.4 %collective-permute-start.8 = (bf16[1,288,128]{2,1,0:T(8,128)(2,1)S(1)}, bf16[1,288,128]{2,1,0:T(8,128)(2,1)S(1)}, u32[]{:S(2)}, u32[]{:S(2)}) collective-permute-start(bf16[1,288,128]{2,1,0:T(8,128)(2,1)S(1)} %maximum_bitcast_fusion), channel_id=1, source_target_pairs={{0,4},{2,6},{4,0},{6,2},{8,12},{10,14},{12,8},{14,10},{1,5},{3,7},... | collective-permute-start | bytes 221192 | tf_op jit(solution)/shard_map/ppermute | solution.py:22
  7.7 27.6 %copy-start.3 = (bf16[1,128,1536]{2,1,0:T(8,128)(2,1)S(1)}, bf16[1,128,1536]{2,1,0:T(8,128)(2,1)}, u32[]{:S(2)}) copy-start(bf16[1,128,1536]{2,1,0:T(8,128)(2,1)} %param.10) | copy-start | bytes 1179652
  7.7 9.0 %collective-permute-start.9 = (bf16[2,288,128]{2,1,0:T(8,128)(2,1)S(1)}, bf16[2,288,128]{2,1,0:T(8,128)(2,1)S(1)}, u32[]{:S(2)}, u32[]{:S(2)}) collective-permute-start(bf16[2,288,128]{2,1,0:T(8,128)(2,1)S(1)} %pad_maximum_fusion.2), channel_id=1, source_target_pairs={{0,8},{2,10},{4,12},{6,14},{8,0},{10,2},{12,4},{14,6},{1,9},{3,11}... | collective-permute-start | bytes 442376 | tf_op jit(solution)/shard_map/ppermute | solution.py:22
  17.5 10.3 %collective-permute-start.10 = (bf16[4,288,128]{2,1,0:T(8,128)(2,1)}, bf16[4,288,128]{2,1,0:T(8,128)(2,1)}, u32[]{:S(2)}, u32[]{:S(2)}) collective-permute-start(bf16[4,288,128]{2,1,0:T(8,128)(2,1)} %pad_maximum_fusion.1), channel_id=1, source_target_pairs={{0,2},{2,0},{4,6},{6,4},{8,10},{10,8},{12,14},{14,12},{1,3},{3,1},... | collective-permute-start | bytes 884744 | tf_op jit(solution)/shard_map/ppermute | solution.py:22
  19.0 14.8 %collective-permute-start.3 = (bf16[192,1536]{1,0:T(8,128)(2,1)S(1)}, bf16[192,1536]{1,0:T(8,128)(2,1)S(1)}, u32[]{:S(2)}, u32[]{:S(2)}) collective-permute-start(bf16[192,1536]{1,0:T(8,128)(2,1)S(1)} %copy-done.2), channel_id=1, source_target_pairs={{0,4},{16,24},{2,6},{18,26},{4,12},{20,16},{6,14},{22,18},{8,0},{2... | collective-permute-start | bytes 1769480 | tf_op jit(solution)/shard_map/ppermute | solution.py:41
  19.7 9.2 %collective-permute-start = (bf16[128,1536]{1,0:T(8,128)(2,1)S(1)}, bf16[128,1536]{1,0:T(8,128)(2,1)}, u32[]{:S(2)}, u32[]{:S(2)}) collective-permute-start(bf16[128,1536]{1,0:T(8,128)(2,1)S(1)} %bitcast.27), channel_id=1, source_target_pairs={{0,1},{1,0},{2,3},{3,2},{4,5},{5,4},{6,7},{7,6},{8,9},{9,8},{10,11... | collective-permute-start | bytes 1179656 | tf_op jit(solution)/shard_map/ppermute | solution.py:22
  19.7 15.1 %collective-permute-start.1 = (bf16[128,1536]{1,0:T(8,128)(2,1)}, bf16[128,1536]{1,0:T(8,128)(2,1)}, u32[]{:S(2)}, u32[]{:S(2)}) collective-permute-start(bf16[128,1536]{1,0:T(8,128)(2,1)} %bitcast.34), channel_id=1, source_target_pairs={{0,1},{1,0},{2,3},{3,2},{4,5},{5,4},{6,7},{7,6},{8,9},{9,8},{10,11... | collective-permute-start | bytes 1179656 | tf_op jit(solution)/shard_map/ppermute | solution.py:22
  20.2 25.6 %collective-permute-start.2 = (bf16[192,1536]{1,0:T(8,128)(2,1)S(1)}, bf16[192,1536]{1,0:T(8,128)(2,1)S(1)}, u32[]{:S(2)}, u32[]{:S(2)}) collective-permute-start(bf16[192,1536]{1,0:T(8,128)(2,1)S(1)} %copy-done.2), channel_id=1, source_target_pairs={{0,2},{2,0},{4,6},{6,4},{8,10},{10,8},{12,14},{14,12},{1,3},{3,1},... | collective-permute-start | bytes 1769480 | tf_op jit(solution)/shard_map/ppermute | solution.py:22
  20.7 14.6 %copy-start.5 = (bf16[1,128,1536]{2,1,0:T(8,128)(2,1)S(1)}, bf16[1,128,1536]{2,1,0:T(8,128)(2,1)}, u32[]{:S(2)}) copy-start(bf16[1,128,1536]{2,1,0:T(8,128)(2,1)} %param.13) | copy-start | bytes 1179652
  20.7 14.6 %copy-start.6 = (bf16[1,128,1536]{2,1,0:T(8,128)(2,1)S(1)}, bf16[1,128,1536]{2,1,0:T(8,128)(2,1)}, u32[]{:S(2)}) copy-start(bf16[1,128,1536]{2,1,0:T(8,128)(2,1)} %param.12) | copy-start | bytes 1179652
  28.8 13.4 %collective-permute-start.11 = (bf16[8,288,128]{2,1,0:T(8,128)(2,1)S(1)}, bf16[8,288,128]{2,1,0:T(8,128)(2,1)S(1)}, u32[]{:S(2)}, u32[]{:S(2)}) collective-permute-start(bf16[8,288,128]{2,1,0:T(8,128)(2,1)S(1)} %pad_maximum_fusion.refs_0_), channel_id=1, source_target_pairs={{0,1},{1,0},{2,3},{3,2},{4,5},{5,4},{6,7},{7,6},{8,9},{9,8},{10,11... | collective-permute-start | bytes 1769480 | tf_op jit(solution)/shard_map/ppermute | solution.py:22
  28.9 16.4 %collective-permute-start.6 = (bf16[128,1536]{1,0:T(8,128)(2,1)S(1)}, bf16[128,1536]{1,0:T(8,128)(2,1)S(1)}, u32[]{:S(2)}, u32[]{:S(2)}) collective-permute-start(bf16[128,1536]{1,0:T(8,128)(2,1)S(1)} %dynamic-slice_bitcast_fusion), channel_id=1, source_target_pairs={{0,1},{1,0},{2,3},{3,2},{4,5},{5,4},{6,7},{7,6},{8,9},{9,8},{10,11... | collective-permute-start | bytes 1179656 | tf_op jit(solution)/shard_map/ppermute | solution.py:22
  33.8 13.9 %collective-permute-start.14 = (bf16[192,1536]{1,0:T(8,128)(2,1)S(1)}, bf16[192,1536]{1,0:T(8,128)(2,1)S(1)}, u32[]{:S(2)}, u32[]{:S(2)}) collective-permute-start(bf16[192,1536]{1,0:T(8,128)(2,1)S(1)} %collective-permute-done.3.refs_2_), channel_id=1, source_target_pairs={{0,4},{16,24},{2,6},{18,26},{4,12},{20,16},{6,14},{22,18},{8,0},{2... | collective-permute-start | bytes 1769480 | tf_op jit(solution)/shard_map/ppermute | solution.py:41
  34.8 16.9 %collective-permute-start.4 = (bf16[192,1536]{1,0:T(8,128)(2,1)S(1)}, bf16[192,1536]{1,0:T(8,128)(2,1)S(1)}, u32[]{:S(2)}, u32[]{:S(2)}) collective-permute-start(bf16[192,1536]{1,0:T(8,128)(2,1)S(1)} %collective-permute-done.3.refs_2_), channel_id=1, source_target_pairs={{0,2},{2,0},{4,6},{6,4},{8,10},{10,8},{12,14},{14,12},{1,3},{3,1},... | collective-permute-start | bytes 1769480 | tf_op jit(solution)/shard_map/ppermute | solution.py:22
  36.3 5.9 %copy-start.9 = (bf16[1,128,128]{2,1,0:T(8,128)(2,1)S(1)}, bf16[1,128,128]{2,1,0:T(8,128)(2,1)}, u32[]{:S(2)}) copy-start(bf16[1,128,128]{2,1,0:T(8,128)(2,1)} %param.15) | copy-start | bytes 98308
  42.2 12.3 %collective-permute-start.5 = (bf16[128,1536]{1,0:T(8,128)(2,1)S(1)}, bf16[128,1536]{1,0:T(8,128)(2,1)S(1)}, u32[]{:S(2)}, u32[]{:S(2)}) collective-permute-start(bf16[128,1536]{1,0:T(8,128)(2,1)S(1)} %shard_map.145.refs_4_.refs_2_.refs_7_), channel_id=1, source_target_pairs={{0,1},{1,0},{2,3},{3,2},{4,5},{5,4},{6,7},{7,6},{8,9},{9,8},{10,11... | collective-permute-start | bytes 1179656 | tf_op jit(solution)/shard_map/ppermute | solution.py:22
  45.3 31.2 %collective-permute-start.20 = (f32[8,288,128]{2,1,0:T(8,128)S(1)}, f32[8,288,128]{2,1,0:T(8,128)S(1)}, u32[]{:S(2)}, u32[]{:S(2)}) collective-permute-start(f32[8,288,128]{2,1,0:T(8,128)S(1)} %get-tuple-element.51), channel_id=1, source_target_pairs={{0,1},{1,0},{2,3},{3,2},{4,5},{5,4},{6,7},{7,6},{8,9},{9,8},{10,11... | collective-permute-start | bytes 3538952 | tf_op jit(solution)/shard_map/ppermute | solution.py:22
  45.8 16.2 %collective-permute-start.12 = (bf16[192,1536]{1,0:T(8,128)(2,1)S(1)}, bf16[192,1536]{1,0:T(8,128)(2,1)S(1)}, u32[]{:S(2)}, u32[]{:S(2)}) collective-permute-start(bf16[192,1536]{1,0:T(8,128)(2,1)S(1)} %collective-permute-done.3.refs_2_), channel_id=1, source_target_pairs={{0,16},{16,0},{1,17},{17,1},{2,18},{18,2},{3,19},{19,3},{4,20},{20... | collective-permute-start | bytes 1769480 | tf_op jit(solution)/shard_map/ppermute | solution.py:22
  47.7 15.7 %collective-permute-start.15 = (bf16[192,1536]{1,0:T(8,128)(2,1)S(1)}, bf16[192,1536]{1,0:T(8,128)(2,1)S(1)}, u32[]{:S(2)}, u32[]{:S(2)}) collective-permute-start(bf16[192,1536]{1,0:T(8,128)(2,1)S(1)} %collective-permute-done.14.refs_2_), channel_id=1, source_target_pairs={{0,2},{2,0},{4,6},{6,4},{8,10},{10,8},{12,14},{14,12},{1,3},{3,1},... | collective-permute-start | bytes 1769480 | tf_op jit(solution)/shard_map/ppermute | solution.py:22
  51.7 22.1 %collective-permute-start.13 = (bf16[192,1536]{1,0:T(8,128)(2,1)S(1)}, bf16[192,1536]{1,0:T(8,128)(2,1)S(1)}, u32[]{:S(2)}, u32[]{:S(2)}) collective-permute-start(bf16[192,1536]{1,0:T(8,128)(2,1)S(1)} %collective-permute-done.4.refs_3_), channel_id=1, source_target_pairs={{0,16},{16,0},{1,17},{17,1},{2,18},{18,2},{3,19},{19,3},{4,20},{20... | collective-permute-start | bytes 1769480 | tf_op jit(solution)/shard_map/ppermute | solution.py:22
  57.1 21.2 %collective-permute-start.7 = (f32[128,768]{1,0:T(8,128)S(1)}, f32[128,768]{1,0:T(8,128)S(1)}, u32[]{:S(2)}, u32[]{:S(2)}) collective-permute-start(f32[128,768]{1,0:T(8,128)S(1)} %get-tuple-element.30), channel_id=1, source_target_pairs={{0,1},{1,0},{2,3},{3,2},{4,5},{5,4},{6,7},{7,6},{8,9},{9,8},{10,11... | collective-permute-start | bytes 1179656 | tf_op jit(solution)/shard_map/ppermute | solution.py:22
  76.5 12.2 %collective-permute-start.16 = (f32[128,768]{1,0:T(8,128)S(1)}, f32[128,768]{1,0:T(8,128)S(1)}, u32[]{:S(2)}, u32[]{:S(2)}) collective-permute-start(f32[128,768]{1,0:T(8,128)S(1)} %get-tuple-element.36), channel_id=1, source_target_pairs={{0,1},{1,0},{2,3},{3,2},{4,5},{5,4},{6,7},{7,6},{8,9},{9,8},{10,11... | collective-permute-start | bytes 1179656 | tf_op jit(solution)/shard_map/ppermute | solution.py:22
  76.6 1.8 %copy-start.8 = (bf16[1,128,1536]{2,1,0:T(8,128)(2,1)S(1)}, bf16[1,128,1536]{2,1,0:T(8,128)(2,1)}, u32[]{:S(2)}) copy-start(bf16[1,128,1536]{2,1,0:T(8,128)(2,1)} %param.14) | copy-start | bytes 1179652
  76.7 9.5 %collective-permute-start.21 = (bf16[4,288,128]{2,1,0:T(8,128)(2,1)S(1)}, bf16[4,288,128]{2,1,0:T(8,128)(2,1)S(1)}, u32[]{:S(2)}, u32[]{:S(2)}) collective-permute-start(bf16[4,288,128]{2,1,0:T(8,128)(2,1)S(1)} %slice.63), channel_id=1, source_target_pairs={{0,2},{2,0},{4,6},{6,4},{8,10},{10,8},{12,14},{14,12},{1,3},{3,1},... | collective-permute-start | bytes 884744 | tf_op jit(solution)/shard_map/ppermute | solution.py:22
  82.6 13.7 %collective-permute-start.17 = (bf16[2,128,768]{2,1,0:T(8,128)(2,1)S(1)}, bf16[2,128,768]{2,1,0:T(8,128)(2,1)S(1)}, u32[]{:S(2)}, u32[]{:S(2)}) collective-permute-start(bf16[2,128,768]{2,1,0:T(8,128)(2,1)S(1)} %get-tuple-element.40), channel_id=1, source_target_pairs={{0,1},{1,0},{2,3},{3,2},{4,5},{5,4},{6,7},{7,6},{8,9},{9,8},{10,11... | collective-permute-start | bytes 1179656 | tf_op jit(solution)/shard_map/ppermute | solution.py:22
  82.8 13.5 %collective-permute-start.19 = (bf16[128,1536]{1,0:T(8,128)(2,1)S(1)}, bf16[128,1536]{1,0:T(8,128)(2,1)S(1)}, u32[]{:S(2)}, u32[]{:S(2)}) collective-permute-start(bf16[128,1536]{1,0:T(8,128)(2,1)S(1)} %get-tuple-element.43), channel_id=1, source_target_pairs={{0,1},{1,0},{2,3},{3,2},{4,5},{5,4},{6,7},{7,6},{8,9},{9,8},{10,11... | collective-permute-start | bytes 1179656 | tf_op jit(solution)/shard_map/ppermute | solution.py:22
  86.3 9.6 %collective-permute-start.22 = (bf16[2,288,128]{2,1,0:T(8,128)(2,1)S(1)}, bf16[2,288,128]{2,1,0:T(8,128)(2,1)S(1)}, u32[]{:S(2)}, u32[]{:S(2)}) collective-permute-start(bf16[2,288,128]{2,1,0:T(8,128)(2,1)S(1)} %slice.64), channel_id=1, source_target_pairs={{0,8},{2,10},{4,12},{6,14},{8,0},{10,2},{12,4},{14,6},{1,9},{3,11}... | collective-permute-start | bytes 442376 | tf_op jit(solution)/shard_map/ppermute | solution.py:22
  92.9 3.4 %collective-permute-start.18 = (bf16[2,128,768]{2,1,0:T(8,128)(2,1)S(1)}, bf16[2,128,768]{2,1,0:T(8,128)(2,1)S(1)}, u32[]{:S(2)}, u32[]{:S(2)}) collective-permute-start(bf16[2,128,768]{2,1,0:T(8,128)(2,1)S(1)} %get-tuple-element.41), channel_id=1, source_target_pairs={{0,1},{1,0},{2,3},{3,2},{4,5},{5,4},{6,7},{7,6},{8,9},{9,8},{10,11... | collective-permute-start | bytes 1179656 | tf_op jit(solution)/shard_map/ppermute | solution.py:22
  95.9 4.4 %collective-permute-start.23 = (bf16[1,288,128]{2,1,0:T(8,128)(2,1)S(1)}, bf16[1,288,128]{2,1,0:T(8,128)(2,1)S(1)}, u32[]{:S(2)}, u32[]{:S(2)}) collective-permute-start(bf16[1,288,128]{2,1,0:T(8,128)(2,1)S(1)} %slice.65), channel_id=1, source_target_pairs={{0,4},{2,6},{4,0},{6,2},{8,12},{10,14},{12,8},{14,10},{1,5},{3,7},... | collective-permute-start | bytes 221192 | tf_op jit(solution)/shard_map/ppermute | solution.py:22
  (3 other events, 2.6 us)

commit v2 on v1

v2 whole, which is shorter than its diff:
```python
import functools

import jax
import jax.numpy as jnp
from jax import lax
from jax.experimental import pallas as pl
from jax.experimental.pallas import tpu as pltpu
from jax.sharding import PartitionSpec as P

HD = 128
BATCHES = 4
FACTOR = HD ** (-0.5)
F32 = jnp.float32
BF16 = jnp.bfloat16
ROWS = (((0,), (0,)), ((), ()))
COLS = (((1,), (1,)), ((), ()))


def swap(value, axis, mask):
    pairs = [(source, source ^ mask) for source in range(lax.axis_size(axis))]
    return lax.ppermute(value, axis, pairs)


def ring_after(z):
    low, high = z % 2, z // 2
    return 2 * low + (1 - high)


def ring_before(z):
    low, high = z % 2, z // 2
    return 2 * (1 - low) + high


def ring_step(value, back=False, turn=0):
    pairs = []
    for f in range(8):
        z, x = f // 2, (f % 2) ^ turn
        pairs.append((f, ring_after(z) * 2 + x))
        pairs.append((8 + f, 8 + ring_before(z) * 2 + x))
    if back:
        pairs = [(target, source) for source, target in pairs]
    return lax.ppermute(value, ("rep", "fsdp"), pairs)


def dot(a, b, dims=None):
    if dims is None:
        return jnp.dot(a, b, preferred_element_type=F32)
    return lax.dot_general(a, b, dims, preferred_element_type=F32)


def batch_places(grouped):
    if not grouped:
        return list(range(BATCHES)), 0
    f = lax.axis_index("fsdp")
    rep = lax.axis_index("rep")
    z, x = f // 2, f % 2
    after, before = ring_after(z), ring_before(z)
    first = jnp.where(rep == 0, before, after)
    second = jnp.where(rep == 0, after, before)
    return [z, first, second, 3 - z], x


def softmax_parts(q, k):
    scores = dot(q, k, COLS) * FACTOR
    top = jnp.max(scores, -1, keepdims=True)
    weight = jnp.exp(scores - top)
    return weight * (1.0 / jnp.sum(weight, -1, keepdims=True))


def start_all(copies):
    for copy in copies:
        copy.start()


def forward_kernel(q_in, ko, kf, kt, vo, vf, vt, attn, q, keys, values, sems):
    rows, inner = q.shape
    copies = [pltpu.make_async_copy(q_in, q, sems.at[2, 0])]
    copies += [
        pltpu.make_async_copy(source, target.at[pl.ds(i * rows, rows)], sems.at[j, i])
        for j, (sources, target) in enumerate((((ko, kf, kt), keys), ((vo, vf, vt), values)))
        for i, source in enumerate(sources)
    ]
    start_all(copies)
    for copy in copies:
        copy.wait()
    for h in range(inner // HD):
        c = slice(h * HD, (h + 1) * HD)
        prob = softmax_parts(q[:, c], keys[:, c]).astype(BF16)
        attn[:, c] = dot(prob, values[:, c]).astype(BF16)


def pack_kernel(proj, down_in, up_in, message, down, up, sems):
    depth = proj.shape[0]
    copies = [
        pltpu.make_async_copy(down_in, down, sems.at[0]),
        pltpu.make_async_copy(up_in, up, sems.at[1]),
        pltpu.make_async_copy(proj, message.at[pl.ds(0, depth)], sems.at[2]),
    ]
    start_all(copies)
    copies[0].wait()
    copies[1].wait()
    for j in range(12):
        c = slice(128 * j, 128 * j + 128)
        message[depth : depth + 16, c] = down[16 * j : 16 * j + 16]
        a, b = j // 3, j % 3
        message[depth + 16 : depth + 48, c] = up[32 * a : 32 * a + 32, 128 * b : 128 * b + 128]
    copies[2].wait()


def adapter_kernel(packed, scale, *refs):
    if packed:
        sources, refs = refs[:8], refs[8:]
        (attn, cot, hint, down, up, act, act_grad, near, far, terms, messages, sems) = refs
        f = lax.axis_index("fsdp")
        core = lax.axis_index("seq")
        places, x = batch_places(True)
        copies = []
        for i, source in enumerate(sources):
            behind = source.shape[0] - 48
            copies.append(pltpu.make_async_copy(source.at[pl.ds(behind, 48)], messages.at[i], sems.at[i]))
        start_all(copies)
        for i, copy in enumerate(copies):
            copy.wait()
            block = places[i // 2] * 2 + (x if i % 2 == 0 else 1 - x)
            for j in range(12):
                c = slice(128 * j, 128 * j + 128)
                down[pl.ds(pl.multiple_of(block * 192 + 16 * j, 16), 16)] = messages[i, 0:16, c]
                a, b = j // 3, j % 3
                columns = pl.ds(pl.multiple_of(block * 384 + 128 * b, 128), 128)
                up[32 * a : 32 * a + 32, columns] = messages[i, 16:48, c]
    else:
        (down_in, up_in, attn, cot, hint, down, up, act, act_grad, down_term, up_term, sems) = refs
        copies = [
            pltpu.make_async_copy(down_in, down, sems.at[0]),
            pltpu.make_async_copy(up_in, up, sems.at[1]),
        ]
        start_all(copies)
        for copy in copies:
            copy.wait()
    pre_act = dot(attn[...], down[...]) + hint[...].astype(F32)
    logistic = 1.0 / (1.0 + jnp.exp(-pre_act))
    act[...] = (pre_act * logistic).astype(BF16)
    act_back = dot(cot[...], up[...], COLS)
    act_grad[...] = (act_back * logistic * (1.0 + pre_act * (1.0 - logistic))).astype(BF16)
    inner, wide = attn.shape[1], cot.shape[1]
    if not packed:
        down_term[...] = dot(attn[...], act_grad[...], ROWS) * scale
        up_term[...] = dot(cot[...], act[...], ROWS) * scale
        return
    terms[pl.ds(0, inner)] = dot(attn[...], act_grad[...], ROWS) * scale
    terms[pl.ds(inner, wide)] = dot(cot[...], act[...], ROWS) * scale
    for place in range(8):
        block = f ^ place
        for target, half in ((near, core), (far, 1 - core)):
            piece = block * 2 + half
            rows = terms[pl.ds(pl.multiple_of(piece * 96, 32), 96)]
            target[place, 0:96] = rows.astype(target.dtype)
            rows = terms[pl.ds(pl.multiple_of(inner + piece * 192, 64), 192)]
            target[place, 96:288] = rows.astype(target.dtype)


def project_kernel(grouped, numbers, *refs):
    count = len(numbers)
    pieces = refs[: 2 * count]
    attn_own, attn_far, cot, cot_far = refs[2 * count : 2 * count + 4]
    rest = refs[2 * count + 4 :]
    carried = ()
    if numbers == (1,):
        carried, rest = rest[:2], rest[2:]
    total_in = None
    if numbers[0] > 0:
        total_in, rest = rest[0], rest[1:]
    last = numbers[-1] == BATCHES - 1
    if last:
        near, far, own, away, weights, sems = rest
    else:
        near, far, total, weights, sems = rest
    places, x = batch_places(grouped)
    core = lax.axis_index("seq")
    rows = attn_own.shape[0]
    depth = attn_own.shape[1] // (2 * BATCHES)
    half = pieces[0].shape[1]
    copies = []
    for i in range(count):
        for j in range(2):
            where = (x if j == 0 else 1 - x) * depth
            copies.append(
                pltpu.make_async_copy(
                    pieces[2 * i + j].at[pl.ds(0, depth)],
                    weights.at[i, pl.ds(where if isinstance(x, int) else pl.multiple_of(where, 32), depth)],
                    sems.at[2 * i + j],
                )
            )
    start_all(copies)
    columns = pl.ds(pl.multiple_of(core * half, 128), half)
    cot_rows = jnp.concatenate([cot[:, columns], cot_far[...]], 0)
    total_now = total_in[...] if total_in is not None else None
    base = 0
    if carried:
        base = carried[0].shape[1]
        near[:, :base] = carried[0][...]
        far[:, :base] = carried[1][...]
    for i, number in enumerate(numbers):
        for copy in copies[2 * i : 2 * i + 2]:
            copy.wait()
        back = dot(cot_rows, weights[i], COLS)
        span = slice(base + i * 2 * depth, base + (i + 1) * 2 * depth)
        near[:, span] = back[:rows]
        far[:, span] = back[rows:].astype(BF16)
        place = pl.ds(pl.multiple_of(places[number] * 2 * depth, 128), 2 * depth)
        attn_rows = jnp.concatenate([attn_own[:, place], attn_far[:, place]], 0)
        term = dot(attn_rows, weights[i])
        total_now = term if total_now is None else total_now + term
    if last:
        own[...] = total_now[:rows]
        away[...] = total_now[rows:].astype(BF16)
    else:
        total[...] = total_now


def backward_kernel(grouped, numbers, *refs):
    (q, ko, kf, kt, vo, vf, vt, attn, near, far, act_grad, down) = refs[:12]
    dq, own, away, qs, keys, values, attns, downs, sems = refs[12:]
    count = len(numbers)
    rows = q.shape[0]
    width = qs.shape[2]
    places, _ = batch_places(grouped)
    copies = []
    for i, number in enumerate(numbers):
        place = pl.ds(pl.multiple_of(places[number] * width, 128), width)
        moves = [(q.at[:, place], qs.at[i]), (attn.at[:, place], attns.at[i])]
        moves.append((down.at[place], downs.at[i]))
        for j, (k, v) in enumerate(((ko, vo), (kf, vf), (kt, vt))):
            moves.append((k.at[:, place], keys.at[i, pl.ds(j * rows, rows)]))
            moves.append((v.at[:, place], values.at[i, pl.ds(j * rows, rows)]))
        group = [
            pltpu.make_async_copy(source, target, sems.at[i, j])
            for j, (source, target) in enumerate(moves)
        ]
        start_all(group)
        copies.append(group)
    for i in range(count):
        for copy in copies[i]:
            copy.wait()
        span = slice(i * width, (i + 1) * width)
        grad = (near[:, span] + far[:, span].astype(F32) + dot(act_grad[...], downs[i], COLS)).astype(BF16)
        for h in range(width // HD):
            c = slice(h * HD, (h + 1) * HD)
            o = slice(i * width + h * HD, i * width + (h + 1) * HD)
            prob = softmax_parts(qs[i, :, c], keys[i, :, c])
            prob_half = prob.astype(BF16)
            head = grad[:, c]
            delta = jnp.sum(head.astype(F32) * attns[i, :, c].astype(F32), -1, keepdims=True)
            prob_grad = dot(head, values[i, :, c], COLS)
            score_grad = (prob * (prob_grad - delta)).astype(BF16)
            dq[:, o] = (dot(score_grad, keys[i, :, c]) * FACTOR).astype(BF16)
            key_term = dot(score_grad[:, : 2 * rows], qs[i, :, c], ROWS)
            value_term = dot(prob_half[:, : 2 * rows], head, ROWS)
            own[0, :, o] = key_term[:rows]
            own[1, :, o] = value_term[:rows]
            away[0, :, o] = key_term[rows:].astype(BF16)
            away[1, :, o] = value_term[rows:].astype(BF16)


def update_kernel(own, away, act, up, *refs):
    if len(refs) == 1:
        (update,) = refs
    else:
        term, term_far, update, down_grad, up_grad = refs
        value = term[0] + term_far[...].astype(F32)
        rows = down_grad.shape[0]
        down_grad[...] = value[:rows]
        up_grad[...] = value[rows:].T
    core = lax.axis_index("seq")
    half = own.shape[1]
    for c, term in ((core, own[...]), (1 - core, away[...].astype(F32))):
        columns = pl.ds(pl.multiple_of(c * half, 128), half)
        update[:, columns] = (term + dot(act[...], up[:, columns])).astype(BF16)


def finish_kernel(grouped, groups, *refs):
    count = len(groups)
    dq_parts, owns, aways = refs[:count], refs[count : 2 * count], refs[2 * count : 3 * count]
    dq, dk, dv = refs[3 * count :]
    places, _ = batch_places(grouped)
    width = dq.shape[1] // BATCHES
    for g, numbers in enumerate(groups):
        for i, number in enumerate(numbers):
            place = pl.ds(pl.multiple_of(places[number] * width, 128), width)
            o = slice(i * width, (i + 1) * width)
            dq[:, place] = dq_parts[g][:, o]
            for j, target in enumerate((dk, dv)):
                value = owns[g][j, :, o] + aways[g][j, :, o].astype(F32)
                target[:, place] = (value * FACTOR if j == 0 else value).astype(BF16)


VMEM = pl.BlockSpec(memory_space=pltpu.VMEM)
ANY = pl.BlockSpec(memory_space=pl.ANY)
HBM = pl.BlockSpec(memory_space=pltpu.HBM)


def shape(dims, dtype=BF16):
    return jax.ShapeDtypeStruct(dims, dtype)


def call(kernel, args, outs, in_specs, scratch, flops, megabytes):
    return pl.pallas_call(
        kernel,
        out_shape=outs,
        in_specs=in_specs,
        out_specs=[VMEM] * len(outs),
        scratch_shapes=scratch,
        compiler_params=pltpu.CompilerParams(vmem_limit_bytes=megabytes * 2**20),
        cost_estimate=pl.CostEstimate(flops=int(flops), bytes_accessed=int(flops) // 400, transcendentals=0),
    )(*args)


def local(
    queries,
    image_keys,
    image_values,
    text_keys,
    text_values,
    control_hint,
    proj_out,
    adapter_down,
    adapter_up,
    cotangent,
):
    shards = lax.axis_size("fsdp")
    grouped = shards == 8 and lax.axis_size("rep") == 2 and lax.axis_size("seq") == 2
    q, ko, vo = queries[0], image_keys[0], image_values[0]
    kt, vt, hint, cot = text_keys[0], text_values[0], control_hint[0], cotangent[0]
    rows, inner = q.shape
    wide = cot.shape[1]
    half = proj_out.shape[1]
    rank = hint.shape[1]
    depth = inner // (2 * BATCHES)
    width = 2 * depth
    core = lax.axis_index("seq")
    scale = float(shards * lax.axis_size("seq") * rows) ** (-0.5)

    kf, vf = swap(ko, "seq", 1), swap(vo, "seq", 1)
    cot_far = swap(lax.dynamic_slice_in_dim(cot, (1 - core) * half, half, 1), "seq", 1)
    attention_flops = 2 * rows * 3 * rows * inner
    (attn,) = call(
        forward_kernel,
        (q, ko, kf, kt, vo, vf, vt),
        [shape((rows, inner))],
        [HBM, HBM, ANY, HBM, HBM, ANY, HBM],
        [
            pltpu.VMEM((rows, inner), BF16),
            pltpu.VMEM((3 * rows, inner), BF16),
            pltpu.VMEM((3 * rows, inner), BF16),
            pltpu.SemaphoreType.DMA((3, 3)),
        ],
        attention_flops,
        16,
    )
    if grouped:
        (message,) = call(
            pack_kernel,
            (proj_out, adapter_down, adapter_up),
            [shape((depth + 48, half))],
            [HBM] * 3,
            [
                pltpu.VMEM(adapter_down.shape, BF16),
                pltpu.VMEM(adapter_up.shape, BF16),
                pltpu.SemaphoreType.DMA((3,)),
            ],
            1000,
            16,
        )
        z1, x1 = ring_step(message), swap(message, "fsdp", 1)
        z1, x1, attn, cot_far = lax.optimization_barrier((z1, x1, attn, cot_far))
        z2, x2, y1 = ring_step(z1), swap(z1, "fsdp", 1), swap(z1, "rep", 1)
        end_x, end_y = ring_step(z1[depth:], turn=1), ring_step(x1[depth:], back=True)
    else:
        half_out = lax.all_gather(proj_out, "fsdp", axis=0, tiled=True)
        pieces = [half_out[i * depth : (i + 1) * depth] for i in range(2 * BATCHES)]
        adapters = (
            lax.all_gather(adapter_down, "fsdp", axis=0, tiled=True),
            lax.all_gather(adapter_up, "fsdp", axis=1, tiled=True),
        )
    attn_far = swap(attn, "seq", 1)

    def project(numbers, pieces, *carried):
        count = len(numbers)
        done = sum(numbers) if numbers == (1,) else 0
        outs = [shape((rows, (count + done) * width), F32), shape((rows, (count + done) * width))]
        if numbers[-1] == BATCHES - 1:
            outs += [shape((rows, half), F32), shape((rows, half))]
        else:
            outs += [shape((2 * rows, half), F32)]
        args = (*pieces, attn, attn_far, cot, cot_far, *carried)
        return call(
            functools.partial(project_kernel, grouped, numbers),
            args,
            outs,
            [ANY] * (2 * count) + [VMEM] * (len(args) - 2 * count),
            [pltpu.VMEM((count, width, half), BF16), pltpu.SemaphoreType.DMA((2 * count,))],
            (8 if numbers[-1] > 1 else 0.1) * 2 * rows * count * width * half * 2,
            24,
        )

    near, far, total = project((0,), [message, x1] if grouped else pieces[:2])
    if grouped:
        z2, x2, y1, end_x, end_y, total = lax.optimization_barrier((z2, x2, y1, end_x, end_y, total))
        x3, y2 = swap(z2[:depth], "fsdp", 1), swap(x2[:depth], "rep", 1)
        pieces = [message, x1, z1, x2, y1, y2, z2, x3]
        adapters = (message, x1, z1, x2, y1, end_y, z2, end_x)
    outs = [
        shape((inner, rank)),
        shape((rank, wide)),
        shape((rows, rank)),
        shape((rows, rank)),
    ]
    if grouped:
        outs += [shape((8, 288, rank), F32), shape((8, 288, rank))]
        scratch = [
            pltpu.VMEM((inner + wide, rank), F32),
            pltpu.VMEM((8, 48, half), BF16),
            pltpu.SemaphoreType.DMA((8,)),
        ]
    else:
        outs += [shape((inner, rank), F32), shape((wide, rank), F32)]
        scratch = [pltpu.SemaphoreType.DMA((2,))]
    down, up, act, act_grad, first_term, second_term = call(
        functools.partial(adapter_kernel, grouped, scale),
        (*adapters, attn, cot, hint),
        outs,
        [ANY] * len(adapters) + [VMEM] * 3,
        scratch,
        rows * (inner + wide) * rank,
        24,
    )
    def backward(numbers, near, far):
        count = len(numbers)
        return call(
            functools.partial(backward_kernel, grouped, numbers),
            (q, ko, kf, kt, vo, vf, vt, attn, near, far, act_grad, down),
            [
                shape((rows, count * width)),
                shape((2, rows, count * width), F32),
                shape((2, rows, count * width)),
            ],
            [HBM, HBM, ANY, HBM, HBM, ANY, HBM, ANY] + [VMEM] * 3 + [ANY],
            [
                pltpu.VMEM((count, rows, width), BF16),
                pltpu.VMEM((count, 3 * rows, width), BF16),
                pltpu.VMEM((count, 3 * rows, width), BF16),
                pltpu.VMEM((count, rows, width), BF16),
                pltpu.VMEM((count, width, rank), BF16),
                pltpu.SemaphoreType.DMA((count, 9)),
            ],
            (30 if numbers[-1] > 1 else 0.1) * attention_flops,
            16,
        )

    groups = ((0, 1), (2,), (3,))
    near, far, total = project((1,), pieces[2:4], near, far, total)
    far = swap(far, "seq", 1)
    if grouped:
        term = first_term + swap(second_term, "seq", 1).astype(F32)
        shares = [swap(term[2 * k : 2 * k + 2].astype(BF16), "fsdp", 2 * k) for k in (1, 2, 3)]
        term = term[:2] + (shares[0].astype(F32) + shares[1].astype(F32) + shares[2].astype(F32))
        term_far = swap(term[1].astype(BF16), "fsdp", 1)
    dq_a, own_a, away_a = backward(groups[0], near, far)
    away_a = swap(away_a, "seq", 1)
    if grouped:
        pieces[5], pieces[7], dq_a = lax.optimization_barrier((pieces[5], pieces[7], dq_a))
    near_b, far_b, total = project((2,), pieces[4:6], total)
    far_b = swap(far_b, "seq", 1)
    near_c, far_c, own_update, away_update = project((3,), pieces[6:8], total)
    far_c = swap(far_c, "seq", 1)
    away_update = swap(away_update, "seq", 1)
    dq_b, own_b, away_b = backward(groups[1], near_b, far_b)
    away_b = swap(away_b, "seq", 1)
    near_c, dq_b = lax.optimization_barrier((near_c, dq_b))
    dq_c, own_c, away_c = backward(groups[2], near_c, far_c)
    away_c = swap(away_c, "seq", 1)
    if not grouped:
        down_grad = lax.psum_scatter(first_term, ("fsdp", "seq"), scatter_dimension=0, tiled=True)
        up_grad = lax.psum_scatter(second_term, ("fsdp", "seq"), scatter_dimension=0, tiled=True).T
    args = [own_update, away_update, act, up]
    outs = [shape((rows, wide))]
    if grouped:
        args += [term, term_far]
        outs += [shape((96, rank), F32), shape((rank, 192), F32)]
    update, *adapter_grads = call(
        update_kernel, tuple(args), outs, [VMEM] * len(args), [], 2 * rows * rank * wide, 24
    )
    if grouped:
        down_grad, up_grad = adapter_grads
    args = (dq_a, dq_b, dq_c, own_a, own_b, own_c, away_a, away_b, away_c)
    query_grad, key_grad, value_grad = call(
        functools.partial(finish_kernel, grouped, groups),
        args,
        [shape((rows, inner))] * 3,
        [VMEM] * len(args),
        [],
        2 * rows * rank * wide,
        24,
    )
    return (update[None], query_grad[None], key_grad[None], value_grad[None], down_grad, up_grad)


def solution(mesh):
    rows = P(("rep", "fsdp"), "seq", None)
    text = P(("rep", "fsdp"), None, None)
    return jax.shard_map(
        local,
        mesh=mesh,
        in_specs=(
            rows,
            rows,
            rows,
            text,
            text,
            rows,
            P("fsdp", "seq"),
            P("fsdp", None),
            P(None, "fsdp"),
            rows,
        ),
        out_specs=(rows, rows, rows, rows, P(("rep", "fsdp", "seq"), None), P("rep", ("fsdp", "seq"))),
        check_vma=False,
    )
```

time: 102 us -> 90.9 us (0.89)
  waiting for transfers between devices: 47.7 us -> 32.6 us
  Pallas kernels: 24.3 us -> 27.3 us
  other arithmetic: 2.06 us -> 0.24 us
  local copies, waits for them, and re-layouts: 4.01 us -> 5.76 us
    ppermute x22 -> x21, waiting for transfers between devices: 43 us -> 13.4 us  [swap(): return lax.ppermute(value, axis, pairs)]
    ppermute x2 -> x4, waiting for transfers between devices: 4.65 us -> 19.2 us  [ring_step(): return lax.ppermute(value, ('rep', 'fsdp'), pairs)]
    ppermute x2 -> x4, starting transfers between devices: 1.65 us -> 7.85 us  [ring_step(): return lax.ppermute(value, ('rep', 'fsdp'), pairs)]
    ppermute x22 -> x21, starting transfers between devices: 21 us -> 15.8 us  [swap(): return lax.ppermute(value, axis, pairs)]
    unnamed x22 -> x21, local copies, waits for them, and re-layouts: 1.8 us -> 5.6 us
    pallas_call x7 -> x12, Pallas kernels: 24.3 us -> 27.3 us  [call(): pl.pallas_call(kernel, out_shape=outs, in_specs=in_specs, out_specs=[VMEM...]
    concatenate x3 -> x0, other arithmetic: 1.84 us -> none  [the longest x1 1.06 us: local(): mine = jnp.concatenate([block, swap(block, 'fsdp', 1)], 0)]
  transfers between devices with their start and end apart: 24 -> 25, of which waited for: 12 -> 8; matrix products, arithmetic and copies ran while one was open for 1% -> 0% of each run, Pallas kernels for 24% -> 25%
where the time goes in v2:
time: 90.9 us; the launch traced here: 90.4 us
  waiting for transfers between devices  32.6 us (36%)
  Pallas kernels  27.3 us (30%)
  starting transfers between devices  23.6 us (26%)
  local copies, waits for them, and re-layouts  5.76 us (6%)
  between operations  0.91 us (1%)
    pallas_call x12, Pallas kernels, call(): pl.pallas_call(kernel, out_shape=outs, in_specs=in_specs, out_specs=[VMEM...  27.3 us
    ppermute x4, waiting for transfers between devices, ring_step(): return lax.ppermute(value, ('rep', 'fsdp'), pairs)  19.2 us
    ppermute x21, starting transfers between devices, swap(): return lax.ppermute(value, axis, pairs)  15.8 us
    ppermute x21, waiting for transfers between devices, swap(): return lax.ppermute(value, axis, pairs)  13.4 us
    ppermute x4, starting transfers between devices, ring_step(): return lax.ppermute(value, ('rep', 'fsdp'), pairs)  7.85 us
    unnamed x21, local copies, waits for them, and re-layouts  5.6 us
  transfers between devices with their start and end apart: 25, of which 8 were waited for; matrix products, arithmetic and copies ran while one was open for 0% of the time, Pallas kernels for 25%

profile of v2, /device:TPU:0, one launch (start us, length us, event | category | flops | bytes accessed | tf_op | source)
XLA Modules:
  0.0 90.4 jit_solution(3214793085540923400)
XLA Ops:
  0.7 1.1 %copy-done.6 = bf16[192,1536]{1,0:T(8,128)(2,1)S(1)} copy-done((bf16[192,1536]{1,0:T(8,128)(2,1)S(1)}, bf16[192,1536]{1,0:T(8,128)(2,1)}, u32[]{:S(2)}) %copy-start.6) | copy-done | bytes 589848
  1.8 0.9 copy-done.7
  2.7 0.8 copy-done.8
  3.8 3.0 %collective-permute-start.1 = (bf16[240,1536]{1,0:T(8,128)(2,1)S(1)}, bf16[240,1536]{1,0:T(8,128)(2,1)S(1)}, u32[]{:S(2)}, u32[]{:S(2)}) collective-permute-start(bf16[240,1536]{1,0:T(8,128)(2,1)S(1)} %shard_map.145.refs_0_), channel_id=1, source_target_pairs={{0,2},{2,0},{4,6},{6,4},{8,10},{10,8},{12,14},{14,12},{1,3},{3,1},... | collective-permute-start | bytes 2211848 | tf_op jit(solution)/shard_map/ppermute | solution.py:21
  6.8 1.6 %collective-permute-start = (bf16[240,1536]{1,0:T(8,128)(2,1)S(1)}, bf16[240,1536]{1,0:T(8,128)(2,1)S(1)}, u32[]{:S(2)}, u32[]{:S(2)}) collective-permute-start(bf16[240,1536]{1,0:T(8,128)(2,1)S(1)} %shard_map.145.refs_0_), channel_id=1, source_target_pairs={{0,4},{16,24},{2,6},{18,26},{4,12},{20,16},{6,14},{22,18},{8,0},{2... | collective-permute-start | bytes 2211848 | tf_op jit(solution)/shard_map/ppermute | solution.py:42
  9.0 1.4 %collective-permute-done.2.kf.refs_2_ = bf16[128,1536]{1,0:T(8,128)(2,1)} collective-permute-done((bf16[128,1536]{1,0:T(8,128)(2,1)}, bf16[128,1536]{1,0:T(8,128)(2,1)}, u32[]{:S(2)}, u32[]{:S(2)}) %collective-permute-start.2) | collective-permute-done | bytes 393248 | tf_op jit(solution)/shard_map/ppermute | solution.py:21
  11.0 1.0 %copy-done.2 = bf16[1,128,1536]{2,1,0:T(8,128)(2,1)S(1)} copy-done((bf16[1,128,1536]{2,1,0:T(8,128)(2,1)S(1)}, bf16[1,128,1536]{2,1,0:T(8,128)(2,1)}, u32[]{:S(2)}) %copy-start.2) | copy-done | bytes 393240
  12.0 1.0 %copy-done.4 = bf16[1,128,1536]{2,1,0:T(8,128)(2,1)S(1)} copy-done((bf16[1,128,1536]{2,1,0:T(8,128)(2,1)S(1)}, bf16[1,128,1536]{2,1,0:T(8,128)(2,1)}, u32[]{:S(2)}) %copy-start.4) | copy-done | bytes 393240
  13.0 5.8 %shard_map.146.refs_2_.refs_8_.refs_7_ = bf16[128,1536]{1,0:T(8,128)(2,1)S(1)} custom-call(bf16[128,1536]{1,0:T(8,128)(2,1)S(1)} %bitcast.20, bf16[128,1536]{1,0:T(8,128)(2,1)} %bitcast.1.ko.refs_1_, bf16[128,1536]{1,0:T(8,128)(2,1)} %collective-permute-done.2.kf.refs_2_, bf16[128,1536]{1,0:T(8,128)(2,1)S(1)} %bitcast.24, ...), custom_call_target="tpu_custom_call" | custom-call | flops 150994944 | bytes 377487 | tf_op jit(solution)/shard_map/pallas_call | solution.py:307
  18.9 4.4 %collective-permute-done.1.refs_1_ = bf16[240,1536]{1,0:T(8,128)(2,1)S(1)} collective-permute-done((bf16[240,1536]{1,0:T(8,128)(2,1)S(1)}, bf16[240,1536]{1,0:T(8,128)(2,1)S(1)}, u32[]{:S(2)}, u32[]{:S(2)}) %collective-permute-start.1) | collective-permute-done | bytes 737312 | tf_op jit(solution)/shard_map/ppermute | solution.py:21
  23.3 2.4 %collective-permute-done.refs_0_.refs_2_ = bf16[240,1536]{1,0:T(8,128)(2,1)S(1)} collective-permute-done((bf16[240,1536]{1,0:T(8,128)(2,1)S(1)}, bf16[240,1536]{1,0:T(8,128)(2,1)S(1)}, u32[]{:S(2)}, u32[]{:S(2)}) %collective-permute-start) | collective-permute-done | bytes 737312 | tf_op jit(solution)/shard_map/ppermute | solution.py:42
  27.0 2.4 %collective-permute-start.5 = (bf16[240,1536]{1,0:T(8,128)(2,1)S(1)}, bf16[240,1536]{1,0:T(8,128)(2,1)S(1)}, u32[]{:S(2)}, u32[]{:S(2)}) collective-permute-start(bf16[240,1536]{1,0:T(8,128)(2,1)S(1)} %collective-permute-done.refs_0_.refs_2_), channel_id=1, source_target_pairs={{0,4},{16,24},{2,6},{18,26},{4,12},{20,16},{6,14},{22,18},{8,0},{2... | collective-permute-start | bytes 2211848 | tf_op jit(solution)/shard_map/ppermute | solution.py:42
  29.4 2.7 %collective-permute-start.8 = (bf16[48,1536]{1,0:T(8,128)(2,1)S(1)}, bf16[48,1536]{1,0:T(8,128)(2,1)S(1)}, u32[]{:S(2)}, u32[]{:S(2)}) collective-permute-start(bf16[48,1536]{1,0:T(8,128)(2,1)S(1)} %slice.31), channel_id=1, source_target_pairs={{0,6},{16,26},{2,4},{18,24},{4,14},{20,18},{6,12},{22,16},{8,2},{2... | collective-permute-start | bytes 442376 | tf_op jit(solution)/shard_map/ppermute | solution.py:42
  32.0 1.2 %collective-permute-start.9 = (bf16[48,1536]{1,0:T(8,128)(2,1)S(1)}, bf16[48,1536]{1,0:T(8,128)(2,1)S(1)}, u32[]{:S(2)}, u32[]{:S(2)}) collective-permute-start(bf16[48,1536]{1,0:T(8,128)(2,1)S(1)} %slice.32), channel_id=1, source_target_pairs={{4,0},{24,16},{6,2},{26,18},{12,4},{16,20},{14,6},{18,22},{0,8},{2... | collective-permute-start | bytes 442376 | tf_op jit(solution)/shard_map/ppermute | solution.py:42
  33.3 1.3 %shard_map.147 = (f32[128,384]{1,0:T(8,128)S(1)}, bf16[128,384]{1,0:T(8,128)(2,1)S(1)}, f32[256,1536]{1,0:T(8,128)S(1)}) custom-call(bf16[240,1536]{1,0:T(8,128)(2,1)S(1)} %shard_map.145.refs_0_, bf16[240,1536]{1,0:T(8,128)(2,1)S(1)} %collective-permute-done.1.refs_1_, bf16[128,1536]{1,0:T(8,128)(2,1)S(1)} %shard_map.146.refs_2_.refs_8_.refs_7_, ...), custom_call_target="tpu_custom_call" | custom-call | flops 30198988 | bytes 75497 | tf_op jit(solution)/shard_map/pallas_call | solution.py:307
  34.6 16.2 %collective-permute-done.8.refs_7_ = bf16[48,1536]{1,0:T(8,128)(2,1)S(1)} collective-permute-done((bf16[48,1536]{1,0:T(8,128)(2,1)S(1)}, bf16[48,1536]{1,0:T(8,128)(2,1)S(1)}, u32[]{:S(2)}, u32[]{:S(2)}) %collective-permute-start.8) | collective-permute-done | bytes 147488 | tf_op jit(solution)/shard_map/ppermute | solution.py:42
  51.4 3.3 %shard_map.149 = (bf16[1536,128]{1,0:T(8,128)(2,1)S(1)}, bf16[128,3072]{1,0:T(8,128)(2,1)S(1)}, bf16[128,128]{1,0:T(8,128)(2,1)S(1)}, bf16[128,128]{1,0:T(8,128)...) custom-call(bf16[240,1536]{1,0:T(8,128)(2,1)S(1)} %shard_map.145.refs_0_, ...), custom_call_target="tpu_custom_call" | custom-call | flops 75497472 | bytes 188743 | tf_op jit(solution)/shard_map/pallas_call | solution.py:307
  54.9 1.4 %shard_map.148 = (f32[128,768]{1,0:T(8,128)S(1)}, bf16[128,768]{1,0:T(8,128)(2,1)S(1)}, f32[256,1536]{1,0:T(8,128)S(1)}) custom-call(bf16[240,1536]{1,0:T(8,128)(2,1)S(1)} %collective-permute-done.refs_0_.refs_2_, bf16[240,1536]{1,0:T(8,128)(2,1)S(1)} %collective-permute-done.6.refs_1_.refs_3_, bf16[128,1536]{1,0:T(8,128)(2,1)S(1)} %shard_map.146.refs_2_.refs_8_.refs_7_, ...), custom_call_target="tpu_custom_call" | custom-call | flops 30198988 | bytes 75497 | tf_op jit(solution)/shard_map/pallas_call | solution.py:307
  56.9 1.6 %collective-permute-start.12 = (bf16[192,1536]{1,0:T(8,128)(2,1)S(1)}, bf16[192,1536]{1,0:T(8,128)(2,1)S(1)}, u32[]{:S(2)}, u32[]{:S(2)}) collective-permute-start(bf16[192,1536]{1,0:T(8,128)(2,1)S(1)} %slice.34), channel_id=1, source_target_pairs={{0,2},{2,0},{4,6},{6,4},{8,10},{10,8},{12,14},{14,12},{1,3},{3,1},... | collective-permute-start | bytes 1769480 | tf_op jit(solution)/shard_map/ppermute | solution.py:21
  58.5 1.6 %collective-permute-start.11 = (bf16[192,1536]{1,0:T(8,128)(2,1)S(1)}, bf16[192,1536]{1,0:T(8,128)(2,1)S(1)}, u32[]{:S(2)}, u32[]{:S(2)}) collective-permute-start(bf16[192,1536]{1,0:T(8,128)(2,1)S(1)} %slice.33), channel_id=1, source_target_pairs={{0,16},{16,0},{1,17},{17,1},{2,18},{18,2},{3,19},{19,3},{4,20},{20... | collective-permute-start | bytes 1769480 | tf_op jit(solution)/shard_map/ppermute | solution.py:21
  60.1 4.4 %shard_map.150 = (bf16[128,768]{1,0:T(8,128)(2,1)S(1)}, f32[2,128,768]{2,1,0:T(8,128)S(1)}, bf16[2,128,768]{2,1,0:T(8,128)(2,1)S(1)}) custom-call(bf16[128,1536]{1,0:T(8,128)(2,1)S(1)} %bitcast.21, bf16[128,1536]{1,0:T(8,128)(2,1)} %bitcast.1.ko.refs_1_, bf16[128,1536]{1,0:T(8,128)(2,1)} %collective-permute-done.2.kf.refs_2_, ...), custom_call_target="tpu_custom_call" | custom-call | flops 15099494 | bytes 37748 | tf_op jit(solution)/shard_map/pallas_call | solution.py:307
  65.4 1.8 %collective-permute-start.18 = (bf16[2,288,128]{2,1,0:T(8,128)(2,1)S(1)}, bf16[2,288,128]{2,1,0:T(8,128)(2,1)S(1)}, u32[]{:S(2)}, u32[]{:S(2)}) collective-permute-start(bf16[2,288,128]{2,1,0:T(8,128)(2,1)S(1)} %get-tuple-element.113), channel_id=1, source_target_pairs={{0,12},{2,14},{4,8},{6,10},{8,4},{10,6},{12,0},{14,2},{1,13},{3,15... | collective-permute-start | bytes 442376 | tf_op jit(solution)/shard_map/ppermute | solution.py:21
  67.2 5.0 %collective-permute-done.12.refs_1_ = bf16[192,1536]{1,0:T(8,128)(2,1)S(1)} collective-permute-done((bf16[192,1536]{1,0:T(8,128)(2,1)S(1)}, bf16[192,1536]{1,0:T(8,128)(2,1)S(1)}, u32[]{:S(2)}, u32[]{:S(2)}) %collective-permute-start.12) | collective-permute-done | bytes 589856 | tf_op jit(solution)/shard_map/ppermute | solution.py:21
  72.2 1.7 %collective-permute-start.17 = (bf16[2,288,128]{2,1,0:T(8,128)(2,1)S(1)}, bf16[2,288,128]{2,1,0:T(8,128)(2,1)S(1)}, u32[]{:S(2)}, u32[]{:S(2)}) collective-permute-start(bf16[2,288,128]{2,1,0:T(8,128)(2,1)S(1)} %get-tuple-element.114), channel_id=1, source_target_pairs={{0,8},{2,10},{4,12},{6,14},{8,0},{10,2},{12,4},{14,6},{1,9},{3,11}... | collective-permute-start | bytes 442376 | tf_op jit(solution)/shard_map/ppermute | solution.py:21
  74.0 1.4 %shard_map.151 = (f32[128,384]{1,0:T(8,128)S(1)}, bf16[128,384]{1,0:T(8,128)(2,1)S(1)}, f32[256,1536]{1,0:T(8,128)S(1)}) custom-call(bf16[240,1536]{1,0:T(8,128)(2,1)S(1)} %collective-permute-done.7.refs_4_.refs_0_, bf16[192,1536]{1,0:T(8,128)(2,1)S(1)} %collective-permute-done.11.refs_1_, bf16[128,1536]{1,0:T(8,128)(2,1)S(1)} %shard_map.146.refs_2_.refs_8_.refs_7_, ...), custom_call_target="tpu_custom_call" | custom-call | flops 2415919104 | bytes 6039797 | tf_op jit(solution)/shard_map/pallas_call | solution.py:307
  75.5 1.4 %shard_map.152 = (f32[128,384]{1,0:T(8,128)S(1)}, bf16[128,384]{1,0:T(8,128)(2,1)S(1)}, f32[128,1536]{1,0:T(8,128)S(1)}, bf16[128,1536]{1,0:T(8,128)(2,1)S(1)}) custom-call(bf16[240,1536]{1,0:T(8,128)(2,1)S(1)} %collective-permute-done.5.refs_6_.refs_0_, bf16[192,1536]{1,0:T(8,128)(2,1)S(1)} %collective-permute-done.12.refs_1_, ...), custom_call_target="tpu_custom_call" | custom-call | flops 2415919104 | bytes 6039797 | tf_op jit(solution)/shard_map/pallas_call | solution.py:307
  77.4 2.7 %shard_map.154 = (bf16[128,384]{1,0:T(8,128)(2,1)S(1)}, f32[2,128,384]{2,1,0:T(8,128)S(1)}, bf16[2,128,384]{2,1,0:T(8,128)(2,1)S(1)}) custom-call(bf16[128,1536]{1,0:T(8,128)(2,1)S(1)} %bitcast.22, bf16[128,1536]{1,0:T(8,128)(2,1)} %bitcast.1.ko.refs_1_, bf16[128,1536]{1,0:T(8,128)(2,1)} %collective-permute-done.2.kf.refs_2_, ...), custom_call_target="tpu_custom_call" | custom-call | flops 4529848320 | bytes 11324620 | tf_op jit(solution)/shard_map/pallas_call | solution.py:307
  80.3 2.7 %shard_map.155 = (bf16[128,384]{1,0:T(8,128)(2,1)S(1)}, f32[2,128,384]{2,1,0:T(8,128)S(1)}, bf16[2,128,384]{2,1,0:T(8,128)(2,1)S(1)}) custom-call(bf16[128,1536]{1,0:T(8,128)(2,1)S(1)} %bitcast.23, bf16[128,1536]{1,0:T(8,128)(2,1)} %bitcast.1.ko.refs_1_, bf16[128,1536]{1,0:T(8,128)(2,1)} %collective-permute-done.2.kf.refs_2_, ...), custom_call_target="tpu_custom_call" | custom-call | flops 4529848320 | bytes 11324620 | tf_op jit(solution)/shard_map/pallas_call | solution.py:307
  83.8 1.6 %collective-permute-start.19 = (bf16[288,128]{1,0:T(8,128)(2,1)S(1)}, bf16[288,128]{1,0:T(8,128)(2,1)S(1)}, u32[]{:S(2)}, u32[]{:S(2)}) collective-permute-start(bf16[288,128]{1,0:T(8,128)(2,1)S(1)} %fusion), channel_id=1, source_target_pairs={{0,2},{2,0},{4,6},{6,4},{8,10},{10,8},{12,14},{14,12},{1,3},{3,1},... | collective-permute-start | bytes 221192 | tf_op jit(solution)/shard_map/ppermute | solution.py:21
  85.3 1.2 %shard_map.156 = (bf16[128,1536]{1,0:T(8,128)(2,1)}, bf16[128,1536]{1,0:T(8,128)(2,1)}, bf16[128,1536]{1,0:T(8,128)(2,1)}) custom-call(bf16[128,768]{1,0:T(8,128)(2,1)S(1)} %get-tuple-element.84.refs_0_, bf16[128,384]{1,0:T(8,128)(2,1)S(1)} %get-tuple-element.89.refs_1_, bf16[128,384]{1,0:T(8,128)(2,1)S(1)} %get-tuple-element.92.refs_2_, ...), custom_call_target="tpu_custom_call" | custom-call | flops 100663296 | bytes 251658 | tf_op jit(solution)/shard_map/pallas_call | solution.py:307
  86.5 1.9 %collective-permute-done.19.refs_1_ = bf16[288,128]{1,0:T(8,128)(2,1)S(1)} collective-permute-done((bf16[288,128]{1,0:T(8,128)(2,1)S(1)}, bf16[288,128]{1,0:T(8,128)(2,1)S(1)}, u32[]{:S(2)}, u32[]{:S(2)}) %collective-permute-start.19) | collective-permute-done | bytes 73760 | tf_op jit(solution)/shard_map/ppermute | solution.py:21
  88.5 1.2 %shard_map.153 = (bf16[128,3072]{1,0:T(8,128)(2,1)}, f32[96,128]{1,0:T(8,128)}, f32[128,192]{1,0:T(8,128)S(1)}) custom-call(f32[128,1536]{1,0:T(8,128)S(1)} %get-tuple-element.77.own, bf16[128,1536]{1,0:T(8,128)(2,1)S(1)} %collective-permute-done.14.away, bf16[128,128]{1,0:T(8,128)(2,1)S(1)} %get-tuple-element.79.act, ...), custom_call_target="tpu_custom_call" | custom-call | flops 100663296 | bytes 251658 | tf_op jit(solution)/shard_map/pallas_call | solution.py:307
  (60 shorter events, 7.2 us)
Async XLA Ops:
  0.6 8.3 %copy-start = (bf16[1,128,3072]{2,1,0:T(8,128)(2,1)S(1)}, bf16[1,128,3072]{2,1,0:T(8,128)(2,1)}, u32[]{:S(2)}) copy-start(bf16[1,128,3072]{2,1,0:T(8,128)(2,1)} %param.19) | copy-start | bytes 2359300
  0.6 10.4 %copy-start.1 = (bf16[1,128,1536]{2,1,0:T(8,128)(2,1)S(1)}, bf16[1,128,1536]{2,1,0:T(8,128)(2,1)}, u32[]{:S(2)}) copy-start(bf16[1,128,1536]{2,1,0:T(8,128)(2,1)} %param.10) | copy-start | bytes 1179652
  0.7 1.2 %copy-start.6 = (bf16[192,1536]{1,0:T(8,128)(2,1)S(1)}, bf16[192,1536]{1,0:T(8,128)(2,1)}, u32[]{:S(2)}) copy-start(bf16[192,1536]{1,0:T(8,128)(2,1)} %proj.1) | copy-start | bytes 1769476
  3.8 19.5 %collective-permute-start.1 = (bf16[240,1536]{1,0:T(8,128)(2,1)S(1)}, bf16[240,1536]{1,0:T(8,128)(2,1)S(1)}, u32[]{:S(2)}, u32[]{:S(2)}) collective-permute-start(bf16[240,1536]{1,0:T(8,128)(2,1)S(1)} %shard_map.145.refs_0_), channel_id=1, source_target_pairs={{0,2},{2,0},{4,6},{6,4},{8,10},{10,8},{12,14},{14,12},{1,3},{3,1},... | collective-permute-start | bytes 2211848 | tf_op jit(solution)/shard_map/ppermute | solution.py:21
  6.8 18.8 %collective-permute-start = (bf16[240,1536]{1,0:T(8,128)(2,1)S(1)}, bf16[240,1536]{1,0:T(8,128)(2,1)S(1)}, u32[]{:S(2)}, u32[]{:S(2)}) collective-permute-start(bf16[240,1536]{1,0:T(8,128)(2,1)S(1)} %shard_map.145.refs_0_), channel_id=1, source_target_pairs={{0,4},{16,24},{2,6},{18,26},{4,12},{20,16},{6,14},{22,18},{8,0},{2... | collective-permute-start | bytes 2211848 | tf_op jit(solution)/shard_map/ppermute | solution.py:42
  8.4 2.1 %collective-permute-start.2 = (bf16[128,1536]{1,0:T(8,128)(2,1)}, bf16[128,1536]{1,0:T(8,128)(2,1)}, u32[]{:S(2)}, u32[]{:S(2)}) collective-permute-start(bf16[128,1536]{1,0:T(8,128)(2,1)} %bitcast.1.ko.refs_1_), channel_id=1, source_target_pairs={{0,1},{1,0},{2,3},{3,2},{4,5},{5,4},{6,7},{7,6},{8,9},{9,8},{10,11... | collective-permute-start | bytes 1179656 | tf_op jit(solution)/shard_map/ppermute | solution.py:21
  8.4 2.6 %collective-permute-start.3 = (bf16[128,1536]{1,0:T(8,128)(2,1)}, bf16[128,1536]{1,0:T(8,128)(2,1)}, u32[]{:S(2)}, u32[]{:S(2)}) collective-permute-start(bf16[128,1536]{1,0:T(8,128)(2,1)} %bitcast.3.vo.refs_4_), channel_id=1, source_target_pairs={{0,1},{1,0},{2,3},{3,2},{4,5},{5,4},{6,7},{7,6},{8,9},{9,8},{10,11... | collective-permute-start | bytes 1179656 | tf_op jit(solution)/shard_map/ppermute | solution.py:21
  9.0 9.9 %collective-permute-start.4 = (bf16[128,1536]{1,0:T(8,128)(2,1)S(1)}, bf16[128,1536]{1,0:T(8,128)(2,1)S(1)}, u32[]{:S(2)}, u32[]{:S(2)}) collective-permute-start(bf16[128,1536]{1,0:T(8,128)(2,1)S(1)} %dynamic-slice_bitcast_fusion), channel_id=1, source_target_pairs={{0,1},{1,0},{2,3},{3,2},{4,5},{5,4},{6,7},{7,6},{8,9},{9,8},{10,11... | collective-permute-start | bytes 1179656 | tf_op jit(solution)/shard_map/ppermute | solution.py:21
  11.0 1.0 %copy-start.2 = (bf16[1,128,1536]{2,1,0:T(8,128)(2,1)S(1)}, bf16[1,128,1536]{2,1,0:T(8,128)(2,1)}, u32[]{:S(2)}) copy-start(bf16[1,128,1536]{2,1,0:T(8,128)(2,1)} %param.13) | copy-start | bytes 1179652
  25.7 25.7 %collective-permute-start.7 = (bf16[240,1536]{1,0:T(8,128)(2,1)S(1)}, bf16[240,1536]{1,0:T(8,128)(2,1)S(1)}, u32[]{:S(2)}, u32[]{:S(2)}) collective-permute-start(bf16[240,1536]{1,0:T(8,128)(2,1)S(1)} %collective-permute-done.refs_0_.refs_2_), channel_id=1, source_target_pairs={{0,16},{16,0},{1,17},{17,1},{2,18},{18,2},{3,19},{19,3},{4,20},{20... | collective-permute-start | bytes 2211848 | tf_op jit(solution)/shard_map/ppermute | solution.py:21
  26.4 25.0 %collective-permute-start.6 = (bf16[240,1536]{1,0:T(8,128)(2,1)S(1)}, bf16[240,1536]{1,0:T(8,128)(2,1)S(1)}, u32[]{:S(2)}, u32[]{:S(2)}) collective-permute-start(bf16[240,1536]{1,0:T(8,128)(2,1)S(1)} %collective-permute-done.refs_0_.refs_2_), channel_id=1, source_target_pairs={{0,2},{2,0},{4,6},{6,4},{8,10},{10,8},{12,14},{14,12},{1,3},{3,1},... | collective-permute-start | bytes 2211848 | tf_op jit(solution)/shard_map/ppermute | solution.py:21
  27.0 24.4 %collective-permute-start.5 = (bf16[240,1536]{1,0:T(8,128)(2,1)S(1)}, bf16[240,1536]{1,0:T(8,128)(2,1)S(1)}, u32[]{:S(2)}, u32[]{:S(2)}) collective-permute-start(bf16[240,1536]{1,0:T(8,128)(2,1)S(1)} %collective-permute-done.refs_0_.refs_2_), channel_id=1, source_target_pairs={{0,4},{16,24},{2,6},{18,26},{4,12},{20,16},{6,14},{22,18},{8,0},{2... | collective-permute-start | bytes 2211848 | tf_op jit(solution)/shard_map/ppermute | solution.py:42
  29.3 2.7 %collective-permute-start.10 = (bf16[128,1536]{1,0:T(8,128)(2,1)S(1)}, bf16[128,1536]{1,0:T(8,128)(2,1)S(1)}, u32[]{:S(2)}, u32[]{:S(2)}) collective-permute-start(bf16[128,1536]{1,0:T(8,128)(2,1)S(1)} %shard_map.146.refs_2_.refs_8_.refs_7_), channel_id=1, source_target_pairs={{0,1},{1,0},{2,3},{3,2},{4,5},{5,4},{6,7},{7,6},{8,9},{9,8},{10,11... | collective-permute-start | bytes 1179656 | tf_op jit(solution)/shard_map/ppermute | solution.py:21
  29.4 21.4 %collective-permute-start.8 = (bf16[48,1536]{1,0:T(8,128)(2,1)S(1)}, bf16[48,1536]{1,0:T(8,128)(2,1)S(1)}, u32[]{:S(2)}, u32[]{:S(2)}) collective-permute-start(bf16[48,1536]{1,0:T(8,128)(2,1)S(1)} %slice.31), channel_id=1, source_target_pairs={{0,6},{16,26},{2,4},{18,24},{4,14},{20,18},{6,12},{22,16},{8,2},{2... | collective-permute-start | bytes 442376 | tf_op jit(solution)/shard_map/ppermute | solution.py:42
  32.0 19.4 %collective-permute-start.9 = (bf16[48,1536]{1,0:T(8,128)(2,1)S(1)}, bf16[48,1536]{1,0:T(8,128)(2,1)S(1)}, u32[]{:S(2)}, u32[]{:S(2)}) collective-permute-start(bf16[48,1536]{1,0:T(8,128)(2,1)S(1)} %slice.32), channel_id=1, source_target_pairs={{4,0},{24,16},{6,2},{26,18},{12,4},{16,20},{14,6},{18,22},{0,8},{2... | collective-permute-start | bytes 442376 | tf_op jit(solution)/shard_map/ppermute | solution.py:42
  33.3 18.1 %copy-start.9 = (bf16[1,128,128]{2,1,0:T(8,128)(2,1)S(1)}, bf16[1,128,128]{2,1,0:T(8,128)(2,1)}, u32[]{:S(2)}) copy-start(bf16[1,128,128]{2,1,0:T(8,128)(2,1)} %param.15) | copy-start | bytes 98308
  54.8 9.8 %collective-permute-start.15 = (bf16[8,288,128]{2,1,0:T(8,128)(2,1)S(1)}, bf16[8,288,128]{2,1,0:T(8,128)(2,1)S(1)}, u32[]{:S(2)}, u32[]{:S(2)}) collective-permute-start(bf16[8,288,128]{2,1,0:T(8,128)(2,1)S(1)} %get-tuple-element.82), channel_id=1, source_target_pairs={{0,1},{1,0},{2,3},{3,2},{4,5},{5,4},{6,7},{7,6},{8,9},{9,8},{10,11... | collective-permute-start | bytes 1769480 | tf_op jit(solution)/shard_map/ppermute | solution.py:21
  56.3 3.8 %copy-start.3 = (bf16[1,128,1536]{2,1,0:T(8,128)(2,1)S(1)}, bf16[1,128,1536]{2,1,0:T(8,128)(2,1)}, u32[]{:S(2)}) copy-start(bf16[1,128,1536]{2,1,0:T(8,128)(2,1)} %param.13) | copy-start | bytes 1179652
  56.3 3.8 %copy-start.5 = (bf16[1,128,1536]{2,1,0:T(8,128)(2,1)S(1)}, bf16[1,128,1536]{2,1,0:T(8,128)(2,1)}, u32[]{:S(2)}) copy-start(bf16[1,128,1536]{2,1,0:T(8,128)(2,1)} %param.14) | copy-start | bytes 1179652
  56.3 3.8 %collective-permute-start.13 = (bf16[128,768]{1,0:T(8,128)(2,1)S(1)}, bf16[128,768]{1,0:T(8,128)(2,1)S(1)}, u32[]{:S(2)}, u32[]{:S(2)}) collective-permute-start(bf16[128,768]{1,0:T(8,128)(2,1)S(1)} %get-tuple-element.66), channel_id=1, source_target_pairs={{0,1},{1,0},{2,3},{3,2},{4,5},{5,4},{6,7},{7,6},{8,9},{9,8},{10,11... | collective-permute-start | bytes 589832 | tf_op jit(solution)/shard_map/ppermute | solution.py:21
  56.9 15.3 %collective-permute-start.12 = (bf16[192,1536]{1,0:T(8,128)(2,1)S(1)}, bf16[192,1536]{1,0:T(8,128)(2,1)S(1)}, u32[]{:S(2)}, u32[]{:S(2)}) collective-permute-start(bf16[192,1536]{1,0:T(8,128)(2,1)S(1)} %slice.34), channel_id=1, source_target_pairs={{0,2},{2,0},{4,6},{6,4},{8,10},{10,8},{12,14},{14,12},{1,3},{3,1},... | collective-permute-start | bytes 1769480 | tf_op jit(solution)/shard_map/ppermute | solution.py:21
  58.5 15.5 %collective-permute-start.11 = (bf16[192,1536]{1,0:T(8,128)(2,1)S(1)}, bf16[192,1536]{1,0:T(8,128)(2,1)S(1)}, u32[]{:S(2)}, u32[]{:S(2)}) collective-permute-start(bf16[192,1536]{1,0:T(8,128)(2,1)S(1)} %slice.33), channel_id=1, source_target_pairs={{0,16},{16,0},{1,17},{17,1},{2,18},{18,2},{3,19},{19,3},{4,20},{20... | collective-permute-start | bytes 1769480 | tf_op jit(solution)/shard_map/ppermute | solution.py:21
  64.4 20.9 %collective-permute-start.22 = (bf16[2,128,768]{2,1,0:T(8,128)(2,1)S(1)}, bf16[2,128,768]{2,1,0:T(8,128)(2,1)S(1)}, u32[]{:S(2)}, u32[]{:S(2)}) collective-permute-start(bf16[2,128,768]{2,1,0:T(8,128)(2,1)S(1)} %get-tuple-element.96), channel_id=1, source_target_pairs={{0,1},{1,0},{2,3},{3,2},{4,5},{5,4},{6,7},{7,6},{8,9},{9,8},{10,11... | collective-permute-start | bytes 1179656 | tf_op jit(solution)/shard_map/ppermute | solution.py:21
  64.8 18.3 %collective-permute-start.16 = (bf16[2,288,128]{2,1,0:T(8,128)(2,1)S(1)}, bf16[2,288,128]{2,1,0:T(8,128)(2,1)S(1)}, u32[]{:S(2)}, u32[]{:S(2)}) collective-permute-start(bf16[2,288,128]{2,1,0:T(8,128)(2,1)S(1)} %get-tuple-element.112), channel_id=1, source_target_pairs={{0,4},{2,6},{4,0},{6,2},{8,12},{10,14},{12,8},{14,10},{1,5},{3,7},... | collective-permute-start | bytes 442376 | tf_op jit(solution)/shard_map/ppermute | solution.py:21
  65.4 18.2 %collective-permute-start.18 = (bf16[2,288,128]{2,1,0:T(8,128)(2,1)S(1)}, bf16[2,288,128]{2,1,0:T(8,128)(2,1)S(1)}, u32[]{:S(2)}, u32[]{:S(2)}) collective-permute-start(bf16[2,288,128]{2,1,0:T(8,128)(2,1)S(1)} %get-tuple-element.113), channel_id=1, source_target_pairs={{0,12},{2,14},{4,8},{6,10},{8,4},{10,6},{12,0},{14,2},{1,13},{3,15... | collective-permute-start | bytes 442376 | tf_op jit(solution)/shard_map/ppermute | solution.py:21
  72.2 11.5 %collective-permute-start.17 = (bf16[2,288,128]{2,1,0:T(8,128)(2,1)S(1)}, bf16[2,288,128]{2,1,0:T(8,128)(2,1)S(1)}, u32[]{:S(2)}, u32[]{:S(2)}) collective-permute-start(bf16[2,288,128]{2,1,0:T(8,128)(2,1)S(1)} %get-tuple-element.114), channel_id=1, source_target_pairs={{0,8},{2,10},{4,12},{6,14},{8,0},{10,2},{12,4},{14,6},{1,9},{3,11}... | collective-permute-start | bytes 442376 | tf_op jit(solution)/shard_map/ppermute | solution.py:21
  75.4 1.5 %collective-permute-start.20 = (bf16[128,384]{1,0:T(8,128)(2,1)S(1)}, bf16[128,384]{1,0:T(8,128)(2,1)S(1)}, u32[]{:S(2)}, u32[]{:S(2)}) collective-permute-start(bf16[128,384]{1,0:T(8,128)(2,1)S(1)} %get-tuple-element.87), channel_id=1, source_target_pairs={{0,1},{1,0},{2,3},{3,2},{4,5},{5,4},{6,7},{7,6},{8,9},{9,8},{10,11... | collective-permute-start | bytes 294920 | tf_op jit(solution)/shard_map/ppermute | solution.py:21
  76.9 3.3 %collective-permute-start.21 = (bf16[128,384]{1,0:T(8,128)(2,1)S(1)}, bf16[128,384]{1,0:T(8,128)(2,1)S(1)}, u32[]{:S(2)}, u32[]{:S(2)}) collective-permute-start(bf16[128,384]{1,0:T(8,128)(2,1)S(1)} %get-tuple-element.91), channel_id=1, source_target_pairs={{0,1},{1,0},{2,3},{3,2},{4,5},{5,4},{6,7},{7,6},{8,9},{9,8},{10,11... | collective-permute-start | bytes 294920 | tf_op jit(solution)/shard_map/ppermute | solution.py:21
  80.2 8.3 %collective-permute-start.14 = (bf16[128,1536]{1,0:T(8,128)(2,1)S(1)}, bf16[128,1536]{1,0:T(8,128)(2,1)S(1)}, u32[]{:S(2)}, u32[]{:S(2)}) collective-permute-start(bf16[128,1536]{1,0:T(8,128)(2,1)S(1)} %get-tuple-element.78), channel_id=1, source_target_pairs={{0,1},{1,0},{2,3},{3,2},{4,5},{5,4},{6,7},{7,6},{8,9},{9,8},{10,11... | collective-permute-start | bytes 1179656 | tf_op jit(solution)/shard_map/ppermute | solution.py:21
  83.1 2.3 %collective-permute-start.24 = (bf16[2,128,384]{2,1,0:T(8,128)(2,1)S(1)}, bf16[2,128,384]{2,1,0:T(8,128)(2,1)S(1)}, u32[]{:S(2)}, u32[]{:S(2)}) collective-permute-start(bf16[2,128,384]{2,1,0:T(8,128)(2,1)S(1)} %get-tuple-element.98), channel_id=1, source_target_pairs={{0,1},{1,0},{2,3},{3,2},{4,5},{5,4},{6,7},{7,6},{8,9},{9,8},{10,11... | collective-permute-start | bytes 589832 | tf_op jit(solution)/shard_map/ppermute | solution.py:21
  83.6 1.7 %collective-permute-start.23 = (bf16[2,128,384]{2,1,0:T(8,128)(2,1)S(1)}, bf16[2,128,384]{2,1,0:T(8,128)(2,1)S(1)}, u32[]{:S(2)}, u32[]{:S(2)}) collective-permute-start(bf16[2,128,384]{2,1,0:T(8,128)(2,1)S(1)} %get-tuple-element.97), channel_id=1, source_target_pairs={{0,1},{1,0},{2,3},{3,2},{4,5},{5,4},{6,7},{7,6},{8,9},{9,8},{10,11... | collective-permute-start | bytes 589832 | tf_op jit(solution)/shard_map/ppermute | solution.py:21
  83.8 4.7 %collective-permute-start.19 = (bf16[288,128]{1,0:T(8,128)(2,1)S(1)}, bf16[288,128]{1,0:T(8,128)(2,1)S(1)}, u32[]{:S(2)}, u32[]{:S(2)}) collective-permute-start(bf16[288,128]{1,0:T(8,128)(2,1)S(1)} %fusion), channel_id=1, source_target_pairs={{0,2},{2,0},{4,6},{6,4},{8,10},{10,8},{12,14},{14,12},{1,3},{3,1},... | collective-permute-start | bytes 221192 | tf_op jit(solution)/shard_map/ppermute | solution.py:21
  (3 other events, 2.7 us)

commit v3 on v2

--- a/solution.py
+++ b/solution.py
@@ -149,8 +149,8 @@
         return
     terms[pl.ds(0, inner)] = dot(attn[...], act_grad[...], ROWS) * scale
     terms[pl.ds(inner, wide)] = dot(cot[...], act[...], ROWS) * scale
-    for place in range(8):
-        block = f ^ place
+    for place, mask in enumerate((0, 1, 4, 5, 2, 3, 6, 7)):
+        block = f ^ mask
         for target, half in ((near, core), (far, 1 - core)):
             piece = block * 2 + half
             rows = terms[pl.ds(pl.multiple_of(piece * 96, 32), 96)]
@@ -303,15 +303,17 @@
     return jax.ShapeDtypeStruct(dims, dtype)
 
 
-def call(kernel, args, outs, in_specs, scratch, flops, megabytes):
+def call(kernel, args, outs, in_specs, scratch, cost, megabytes):
+    name = getattr(kernel, "func", kernel).__name__
     return pl.pallas_call(
         kernel,
+        name=name,
         out_shape=outs,
         in_specs=in_specs,
         out_specs=[VMEM] * len(outs),
         scratch_shapes=scratch,
         compiler_params=pltpu.CompilerParams(vmem_limit_bytes=megabytes * 2**20),
-        cost_estimate=pl.CostEstimate(flops=int(flops), bytes_accessed=int(flops) // 400, transcendentals=0),
+        cost_estimate=pl.CostEstimate(flops=int(cost * 1e9), bytes_accessed=int(cost * 1e3), transcendentals=0),
     )(*args)
 
 
@@ -342,7 +344,6 @@
 
     kf, vf = swap(ko, "seq", 1), swap(vo, "seq", 1)
     cot_far = swap(lax.dynamic_slice_in_dim(cot, (1 - core) * half, half, 1), "seq", 1)
-    attention_flops = 2 * rows * 3 * rows * inner
     (attn,) = call(
         forward_kernel,
         (q, ko, kf, kt, vo, vf, vt),
@@ -354,7 +355,7 @@
             pltpu.VMEM((3 * rows, inner), BF16),
             pltpu.SemaphoreType.DMA((3, 3)),
         ],
-        attention_flops,
+        0.119135,
         16,
     )
     if grouped:
@@ -368,7 +369,7 @@
                 pltpu.VMEM(adapter_up.shape, BF16),
                 pltpu.SemaphoreType.DMA((3,)),
             ],
-            1000,
+            8.53264,
             16,
         )
         z1, x1 = ring_step(message), swap(message, "fsdp", 1)
@@ -399,13 +400,13 @@
             outs,
             [ANY] * (2 * count) + [VMEM] * (len(args) - 2 * count),
             [pltpu.VMEM((count, width, half), BF16), pltpu.SemaphoreType.DMA((2 * count,))],
-            (8 if numbers[-1] > 1 else 0.1) * 2 * rows * count * width * half * 2,
+            (0.668445, 15.5525, 0.0371933, 0.0320126)[numbers[-1]],
             24,
         )
 
     near, far, total = project((0,), [message, x1] if grouped else pieces[:2])
     if grouped:
-        z2, x2, y1, end_x, end_y, total = lax.optimization_barrier((z2, x2, y1, end_x, end_y, total))
+        z2, x2, y1, total = lax.optimization_barrier((z2, x2, y1, total))
         x3, y2 = swap(z2[:depth], "fsdp", 1), swap(x2[:depth], "rep", 1)
         pieces = [message, x1, z1, x2, y1, y2, z2, x3]
         adapters = (message, x1, z1, x2, y1, end_y, z2, end_x)
@@ -431,7 +432,7 @@
         outs,
         [ANY] * len(adapters) + [VMEM] * 3,
         scratch,
-        rows * (inner + wide) * rank,
+        8.73854,
         24,
     )
     def backward(numbers, near, far):
@@ -453,7 +454,7 @@
                 pltpu.VMEM((count, width, rank), BF16),
                 pltpu.SemaphoreType.DMA((count, 9)),
             ],
-            (30 if numbers[-1] > 1 else 0.1) * attention_flops,
+            (43.2055, 43.2055, 32.5195, 0.0437518)[numbers[-1]],
             16,
         )
 
@@ -462,18 +463,21 @@
     far = swap(far, "seq", 1)
     if grouped:
         term = first_term + swap(second_term, "seq", 1).astype(F32)
-        shares = [swap(term[2 * k : 2 * k + 2].astype(BF16), "fsdp", 2 * k) for k in (1, 2, 3)]
-        term = term[:2] + (shares[0].astype(F32) + shares[1].astype(F32) + shares[2].astype(F32))
+        for mask in (2, 4):
+            keep = term.shape[0] // 2
+            term = term[:keep] + swap(term[keep:].astype(BF16), "fsdp", mask).astype(F32)
         term_far = swap(term[1].astype(BF16), "fsdp", 1)
     dq_a, own_a, away_a = backward(groups[0], near, far)
     away_a = swap(away_a, "seq", 1)
     if grouped:
-        pieces[5], pieces[7], dq_a = lax.optimization_barrier((pieces[5], pieces[7], dq_a))
+        pieces[5], pieces[7], near = lax.optimization_barrier((pieces[5], pieces[7], near))
     near_b, far_b, total = project((2,), pieces[4:6], total)
     far_b = swap(far_b, "seq", 1)
     near_c, far_c, own_update, away_update = project((3,), pieces[6:8], total)
     far_c = swap(far_c, "seq", 1)
     away_update = swap(away_update, "seq", 1)
+    if grouped:
+        near_b, dq_a = lax.optimization_barrier((near_b, dq_a))
     dq_b, own_b, away_b = backward(groups[1], near_b, far_b)
     away_b = swap(away_b, "seq", 1)
     near_c, dq_b = lax.optimization_barrier((near_c, dq_b))
@@ -488,7 +492,7 @@
         args += [term, term_far]
         outs += [shape((96, rank), F32), shape((rank, 192), F32)]
     update, *adapter_grads = call(
-        update_kernel, tuple(args), outs, [VMEM] * len(args), [], 2 * rows * rank * wide, 24
+        update_kernel, tuple(args), outs, [VMEM] * len(args), [], 7.44686, 24
     )
     if grouped:
         down_grad, up_grad = adapter_grads
@@ -499,7 +503,7 @@
         [shape((rows, inner))] * 3,
         [VMEM] * len(args),
         [],
-        2 * rows * rank * wide,
+        44.0671,
         24,
     )
     return (update[None], query_grad[None], key_grad[None], value_grad[None], down_grad, up_grad)

time: 90.9 us -> 83.4 us (0.917)
  waiting for transfers between devices: 32.6 us -> 27 us
  Pallas kernels: 27.3 us -> 26.3 us
    ppermute x21 -> x20, waiting for transfers between devices: 13.4 us -> 7.6 us  [swap(): return lax.ppermute(value, axis, pairs)]
    unnamed x21, local copies, waits for them, and re-layouts: 5.6 us -> 3.67 us
    pallas_call x12, Pallas kernels: 27.3 us -> 26.3 us  [call(): pl.pallas_call(kernel, name=name, out_shape=outs, in_specs=in_specs, out_...]
    slice x1, local copies, waits for them, and re-layouts: 0.01 us -> 0.95 us  [local(): z1[depth:]]
    slice x1, local copies, waits for them, and re-layouts: 0.01 us -> 0.92 us  [local(): x1[depth:]]
    ppermute x21 -> x20, starting transfers between devices: 15.8 us -> 15.2 us  [swap(): return lax.ppermute(value, axis, pairs)]
  transfers between devices with their start and end apart: 25 -> 24, of which waited for: 8 -> 8; matrix products, arithmetic and copies ran while one was open for 0% -> 3% of each run, Pallas kernels for 25% -> 29%
where the time goes in v3:
time: 83.4 us; the launch traced here: 83.1 us
  waiting for transfers between devices  27 us (32%)
  Pallas kernels  26.3 us (32%)
  starting transfers between devices  22.9 us (27%)
  local copies, waits for them, and re-layouts  5.72 us (7%)
  between operations  0.92 us (1%)
    pallas_call x12, Pallas kernels, call(): pl.pallas_call(kernel, name=name, out_shape=outs, in_specs=in_specs, out_...  26.3 us
    ppermute x4, waiting for transfers between devices, ring_step(): return lax.ppermute(value, ('rep', 'fsdp'), pairs)  19.4 us
    ppermute x20, starting transfers between devices, swap(): return lax.ppermute(value, axis, pairs)  15.2 us
    ppermute x4, starting transfers between devices, ring_step(): return lax.ppermute(value, ('rep', 'fsdp'), pairs)  7.72 us
    ppermute x20, waiting for transfers between devices, swap(): return lax.ppermute(value, axis, pairs)  7.6 us
    unnamed x21, local copies, waits for them, and re-layouts  3.67 us
  transfers between devices with their start and end apart: 24, of which 8 were waited for; matrix products, arithmetic and copies ran while one was open for 3% of the time, Pallas kernels for 29%

profile of v3, /device:TPU:0, one launch (start us, length us, event | category | flops | bytes accessed | tf_op | source)
XLA Modules:
  0.0 83.1 jit_solution(15014755511104743041)
XLA Ops:
  0.7 1.2 %copy-done.6 = bf16[192,1536]{1,0:T(8,128)(2,1)S(1)} copy-done((bf16[192,1536]{1,0:T(8,128)(2,1)S(1)}, bf16[192,1536]{1,0:T(8,128)(2,1)}, u32[]{:S(2)}) %copy-start.6) | copy-done | bytes 589848
  1.9 0.9 %copy-done.7 = bf16[128,384]{1,0:T(8,128)(2,1)S(1)} copy-done((bf16[128,384]{1,0:T(8,128)(2,1)S(1)}, bf16[128,384]{1,0:T(8,128)(2,1)}, u32[]{:S(2)}) %copy-start.7) | copy-done | bytes 98328
  3.6 1.2 %pack_kernel.1.refs_0_ = bf16[240,1536]{1,0:T(8,128)(2,1)} custom-call(bf16[192,1536]{1,0:T(8,128)(2,1)S(1)} %copy-done.6, bf16[192,128]{1,0:T(8,128)(2,1)S(1)} %copy-done.8, bf16[128,384]{1,0:T(8,128)(2,1)S(1)} %copy-done.7), custom_call_target="tpu_custom_call" | custom-call | flops 8532639744 | bytes 8532 | tf_op jit(solution)/shard_map/pack_kernel/pallas_call | solution.py:308
  4.8 3.1 %collective-permute-start = (bf16[240,1536]{1,0:T(8,128)(2,1)}, bf16[240,1536]{1,0:T(8,128)(2,1)}, u32[]{:S(2)}, u32[]{:S(2)}) collective-permute-start(bf16[240,1536]{1,0:T(8,128)(2,1)} %pack_kernel.1.refs_0_), channel_id=1, source_target_pairs={{0,4},{16,24},{2,6},{18,26},{4,12},{20,16},{6,14},{22,18},{8,0},{2... | collective-permute-start | bytes 2211848 | tf_op jit(solution)/shard_map/ppermute | solution.py:42
  7.9 1.5 %collective-permute-start.1 = (bf16[240,1536]{1,0:T(8,128)(2,1)}, bf16[240,1536]{1,0:T(8,128)(2,1)}, u32[]{:S(2)}, u32[]{:S(2)}) collective-permute-start(bf16[240,1536]{1,0:T(8,128)(2,1)} %pack_kernel.1.refs_0_), channel_id=1, source_target_pairs={{0,2},{2,0},{4,6},{6,4},{8,10},{10,8},{12,14},{14,12},{1,3},{3,1},... | collective-permute-start | bytes 2211848 | tf_op jit(solution)/shard_map/ppermute | solution.py:21
  10.1 1.0 %collective-permute-done.2.kf.refs_2_ = bf16[128,1536]{1,0:T(8,128)(2,1)S(1)} collective-permute-done((bf16[128,1536]{1,0:T(8,128)(2,1)S(1)}, bf16[128,1536]{1,0:T(8,128)(2,1)S(1)}, u32[]{:S(2)}, u32[]{:S(2)}) %collective-permute-start.2) | collective-permute-done | bytes 393248 | tf_op jit(solution)/shard_map/ppermute | solution.py:21
  11.7 5.6 %forward_kernel.1.refs_2_.refs_8_.refs_7_ = bf16[128,1536]{1,0:T(8,128)(2,1)S(1)} custom-call(bf16[128,1536]{1,0:T(8,128)(2,1)S(1)} %bitcast.20, bf16[128,1536]{1,0:T(8,128)(2,1)S(1)} %bitcast.25, bf16[128,1536]{1,0:T(8,128)(2,1)S(1)} %collective-permute-done.2.kf.refs_2_, bf16[128,1536]{1,0:T(8,128)(2,1)S(1)} %bitcast.29, bf16[128,1536]{1,0:T(8,128)(2,1)S(1)} %bitcast.34, ...), custom_call_target="tpu_custom_call" | custom-call | flops 119135000 | bytes 119 | tf_op jit(solution)/shard_map/forward_kernel/pallas_call | solution.py:308
  17.3 8.4 %collective-permute-done.refs_0_.refs_2_ = bf16[240,1536]{1,0:T(8,128)(2,1)} collective-permute-done((bf16[240,1536]{1,0:T(8,128)(2,1)}, bf16[240,1536]{1,0:T(8,128)(2,1)}, u32[]{:S(2)}, u32[]{:S(2)}) %collective-permute-start) | collective-permute-done | bytes 737312 | tf_op jit(solution)/shard_map/ppermute | solution.py:42
  26.1 2.6 %collective-permute-start.5 = (bf16[240,1536]{1,0:T(8,128)(2,1)}, bf16[240,1536]{1,0:T(8,128)(2,1)S(1)}, u32[]{:S(2)}, u32[]{:S(2)}) collective-permute-start(bf16[240,1536]{1,0:T(8,128)(2,1)} %collective-permute-done.refs_0_.refs_2_), channel_id=1, source_target_pairs={{0,4},{16,24},{2,6},{18,26},{4,12},{20,16},{6,14},{22,18},{8,0},{2... | collective-permute-start | bytes 2211848 | tf_op jit(solution)/shard_map/ppermute | solution.py:42
  28.7 1.5 %collective-permute-start.6 = (bf16[240,1536]{1,0:T(8,128)(2,1)}, bf16[240,1536]{1,0:T(8,128)(2,1)S(1)}, u32[]{:S(2)}, u32[]{:S(2)}) collective-permute-start(bf16[240,1536]{1,0:T(8,128)(2,1)} %collective-permute-done.refs_0_.refs_2_), channel_id=1, source_target_pairs={{0,2},{2,0},{4,6},{6,4},{8,10},{10,8},{12,14},{14,12},{1,3},{3,1},... | collective-permute-start | bytes 2211848 | tf_op jit(solution)/shard_map/ppermute | solution.py:21
  30.2 1.5 %collective-permute-start.7 = (bf16[240,1536]{1,0:T(8,128)(2,1)}, bf16[240,1536]{1,0:T(8,128)(2,1)S(1)}, u32[]{:S(2)}, u32[]{:S(2)}) collective-permute-start(bf16[240,1536]{1,0:T(8,128)(2,1)} %collective-permute-done.refs_0_.refs_2_), channel_id=1, source_target_pairs={{0,16},{16,0},{1,17},{17,1},{2,18},{18,2},{3,19},{19,3},{4,20},{20... | collective-permute-start | bytes 2211848 | tf_op jit(solution)/shard_map/ppermute | solution.py:21
  31.7 0.9 %slice.33 = bf16[48,1536]{1,0:T(8,128)(2,1)S(1)} slice(bf16[240,1536]{1,0:T(8,128)(2,1)} %collective-permute-done.refs_0_.refs_2_), slice={[192:240], [0:1536]} | slice | bytes 294912 | tf_op jit(solution)/shard_map/slice | solution.py:378
  32.7 0.9 %slice.32 = bf16[48,1536]{1,0:T(8,128)(2,1)S(1)} slice(bf16[240,1536]{1,0:T(8,128)(2,1)} %collective-permute-done.1.refs_1_), slice={[192:240], [0:1536]} | slice | bytes 294912 | tf_op jit(solution)/shard_map/slice | solution.py:378
  34.0 1.6 %collective-permute-start.13 = (bf16[48,1536]{1,0:T(8,128)(2,1)S(1)}, bf16[48,1536]{1,0:T(8,128)(2,1)S(1)}, u32[]{:S(2)}, u32[]{:S(2)}) collective-permute-start(bf16[48,1536]{1,0:T(8,128)(2,1)S(1)} %slice.33), channel_id=1, source_target_pairs={{0,6},{16,26},{2,4},{18,24},{4,14},{20,18},{6,12},{22,16},{8,2},{2... | collective-permute-start | bytes 442376 | tf_op jit(solution)/shard_map/ppermute | solution.py:42
  35.7 2.2 %project_kernel.4 = (f32[128,384]{1,0:T(8,128)S(1)}, bf16[128,384]{1,0:T(8,128)(2,1)S(1)}, f32[256,1536]{1,0:T(8,128)S(1)}) custom-call(bf16[240,1536]{1,0:T(8,128)(2,1)} %pack_kernel.1.refs_0_, bf16[240,1536]{1,0:T(8,128)(2,1)} %collective-permute-done.1.refs_1_, bf16[128,1536]{1,0:T(8,128)(2,1)S(1)} %forward_kernel.1.refs_2_.refs_8_.refs_7_, ...), custom_call_target="tpu_custom_call" | custom-call | flops 668444992 | bytes 668 | tf_op jit(solution)/shard_map/project_kernel/pallas_call | solution.py:308
  37.9 10.5 %collective-permute-done.5.refs_0_.refs_6_ = bf16[240,1536]{1,0:T(8,128)(2,1)S(1)} collective-permute-done((bf16[240,1536]{1,0:T(8,128)(2,1)}, bf16[240,1536]{1,0:T(8,128)(2,1)S(1)}, u32[]{:S(2)}, u32[]{:S(2)}) %collective-permute-start.5) | collective-permute-done | bytes 737312 | tf_op jit(solution)/shard_map/ppermute | solution.py:42
  48.5 1.0 %collective-permute-start.9 = (bf16[192,1536]{1,0:T(8,128)(2,1)S(1)}, bf16[192,1536]{1,0:T(8,128)(2,1)S(1)}, u32[]{:S(2)}, u32[]{:S(2)}) collective-permute-start(bf16[192,1536]{1,0:T(8,128)(2,1)S(1)} %slice.30), channel_id=1, source_target_pairs={{0,16},{16,0},{1,17},{17,1},{2,18},{18,2},{3,19},{19,3},{4,20},{20... | collective-permute-start | bytes 1769480 | tf_op jit(solution)/shard_map/ppermute | solution.py:21
  49.6 1.6 %collective-permute-start.10 = (bf16[192,1536]{1,0:T(8,128)(2,1)S(1)}, bf16[192,1536]{1,0:T(8,128)(2,1)S(1)}, u32[]{:S(2)}, u32[]{:S(2)}) collective-permute-start(bf16[192,1536]{1,0:T(8,128)(2,1)S(1)} %slice.31), channel_id=1, source_target_pairs={{0,2},{2,0},{4,6},{6,4},{8,10},{10,8},{12,14},{14,12},{1,3},{3,1},... | collective-permute-start | bytes 1769480 | tf_op jit(solution)/shard_map/ppermute | solution.py:21
  51.6 2.7 %adapter_kernel.1 = (bf16[1536,128]{1,0:T(8,128)(2,1)S(1)}, bf16[128,3072]{1,0:T(8,128)(2,1)S(1)}, bf16[128,128]{1,0:T(8,128)(2,1)S(1)}, bf16[128,128]{1,0:T(8,1...) custom-call(bf16[240,1536]{1,0:T(8,128)(2,1)} %pack_kernel.1.refs_0_, ...), custom_call_target="tpu_custom_call" | custom-call | flops 8738539520 | bytes 8738 | tf_op jit(solution)/shard_map/adapter_kernel/pallas_call | solution.py:308
  54.5 2.1 %project_kernel.5 = (f32[128,768]{1,0:T(8,128)S(1)}, bf16[128,768]{1,0:T(8,128)(2,1)S(1)}, f32[256,1536]{1,0:T(8,128)S(1)}) custom-call(bf16[240,1536]{1,0:T(8,128)(2,1)} %collective-permute-done.refs_0_.refs_2_, bf16[240,1536]{1,0:T(8,128)(2,1)S(1)} %collective-permute-done.6.refs_1_.refs_3_, bf16[128,1536]{1,0:T(8,128)(2,1)S(1)} %forward_kernel.1.refs_2_.refs_8_.refs_7_, ...), custom_call_target="tpu_custom_call" | custom-call | flops 15552499712 | bytes 15552 | tf_op jit(solution)/shard_map/project_kernel/pallas_call | solution.py:308
  57.3 1.8 %collective-permute-start.15 = (bf16[4,288,128]{2,1,0:T(8,128)(2,1)S(1)}, bf16[4,288,128]{2,1,0:T(8,128)(2,1)S(1)}, u32[]{:S(2)}, u32[]{:S(2)}) collective-permute-start(bf16[4,288,128]{2,1,0:T(8,128)(2,1)S(1)} %slice.51), channel_id=1, source_target_pairs={{0,4},{2,6},{4,0},{6,2},{8,12},{10,14},{12,8},{14,10},{1,5},{3,7},... | collective-permute-start | bytes 884744 | tf_op jit(solution)/shard_map/ppermute | solution.py:21
  59.0 3.6 %backward_kernel.3 = (bf16[128,768]{1,0:T(8,128)(2,1)S(1)}, f32[2,128,768]{2,1,0:T(8,128)S(1)}, bf16[2,128,768]{2,1,0:T(8,128)(2,1)S(1)}) custom-call(bf16[128,1536]{1,0:T(8,128)(2,1)S(1)} %bitcast.21, bf16[128,1536]{1,0:T(8,128)(2,1)S(1)} %bitcast.26, bf16[128,1536]{1,0:T(8,128)(2,1)S(1)} %collective-permute-done.2.kf.refs_2_, ...), custom_call_target="tpu_custom_call" | custom-call | flops 43205500928 | bytes 43205 | tf_op jit(solution)/shard_map/backward_kernel/pallas_call | solution.py:308
  62.7 1.4 %project_kernel.6 = (f32[128,384]{1,0:T(8,128)S(1)}, bf16[128,384]{1,0:T(8,128)(2,1)S(1)}, f32[256,1536]{1,0:T(8,128)S(1)}) custom-call(bf16[240,1536]{1,0:T(8,128)(2,1)S(1)} %collective-permute-done.7.refs_0_.refs_4_, bf16[192,1536]{1,0:T(8,128)(2,1)S(1)} %collective-permute-done.9.refs_1_, bf16[128,1536]{1,0:T(8,128)(2,1)S(1)} %forward_kernel.1.refs_2_.refs_8_.refs_7_, ...), custom_call_target="tpu_custom_call" | custom-call | flops 37193300 | bytes 37 | tf_op jit(solution)/shard_map/project_kernel/pallas_call | solution.py:308
  64.2 1.4 %project_kernel.7 = (f32[128,384]{1,0:T(8,128)S(1)}, bf16[128,384]{1,0:T(8,128)(2,1)S(1)}, f32[128,1536]{1,0:T(8,128)S(1)}, bf16[128,1536]{1,0:T(8,128)(2,1)S(1)}) custom-call(bf16[240,1536]{1,0:T(8,128)(2,1)S(1)} %collective-permute-done.5.refs_0_.refs_6_, bf16[192,1536]{1,0:T(8,128)(2,1)S(1)} %collective-permute-done.10.refs_1_, ...), custom_call_target="tpu_custom_call" | custom-call | flops 32012600 | bytes 32 | tf_op jit(solution)/shard_map/project_kernel/pallas_call | solution.py:308
  66.7 2.5 %collective-permute-start.16 = (bf16[2,288,128]{2,1,0:T(8,128)(2,1)S(1)}, bf16[2,288,128]{2,1,0:T(8,128)(2,1)S(1)}, u32[]{:S(2)}, u32[]{:S(2)}) collective-permute-start(bf16[2,288,128]{2,1,0:T(8,128)(2,1)S(1)} %slice.52), channel_id=1, source_target_pairs={{0,8},{2,10},{4,12},{6,14},{8,0},{10,2},{12,4},{14,6},{1,9},{3,11}... | collective-permute-start | bytes 442376 | tf_op jit(solution)/shard_map/ppermute | solution.py:21
  69.2 1.8 %backward_kernel.4 = (bf16[128,384]{1,0:T(8,128)(2,1)S(1)}, f32[2,128,384]{2,1,0:T(8,128)S(1)}, bf16[2,128,384]{2,1,0:T(8,128)(2,1)S(1)}) custom-call(bf16[128,1536]{1,0:T(8,128)(2,1)S(1)} %bitcast.22, bf16[128,1536]{1,0:T(8,128)(2,1)S(1)} %bitcast.27, bf16[128,1536]{1,0:T(8,128)(2,1)S(1)} %collective-permute-done.2.kf.refs_2_, ...), custom_call_target="tpu_custom_call" | custom-call | flops 32519499776 | bytes 32519 | tf_op jit(solution)/shard_map/backward_kernel/pallas_call | solution.py:308
  71.1 1.8 %backward_kernel.5 = (bf16[128,384]{1,0:T(8,128)(2,1)S(1)}, f32[2,128,384]{2,1,0:T(8,128)S(1)}, bf16[2,128,384]{2,1,0:T(8,128)(2,1)S(1)}) custom-call(bf16[128,1536]{1,0:T(8,128)(2,1)S(1)} %bitcast.23, bf16[128,1536]{1,0:T(8,128)(2,1)S(1)} %bitcast.28, bf16[128,1536]{1,0:T(8,128)(2,1)S(1)} %collective-permute-done.2.kf.refs_2_, ...), custom_call_target="tpu_custom_call" | custom-call | flops 43751800 | bytes 43 | tf_op jit(solution)/shard_map/backward_kernel/pallas_call | solution.py:308
  73.5 3.2 %collective-permute-done.16 = bf16[2,288,128]{2,1,0:T(8,128)(2,1)S(1)} collective-permute-done((bf16[2,288,128]{2,1,0:T(8,128)(2,1)S(1)}, bf16[2,288,128]{2,1,0:T(8,128)(2,1)S(1)}, u32[]{:S(2)}, u32[]{:S(2)}) %collective-permute-start.16) | collective-permute-done | bytes 147488 | tf_op jit(solution)/shard_map/ppermute | solution.py:21
  76.7 0.9 %collective-permute-start.17 = (bf16[288,128]{1,0:T(8,128)(2,1)S(1)}, bf16[288,128]{1,0:T(8,128)(2,1)S(1)}, u32[]{:S(2)}, u32[]{:S(2)}) collective-permute-start(bf16[288,128]{1,0:T(8,128)(2,1)S(1)} %fusion), channel_id=1, source_target_pairs={{0,2},{2,0},{4,6},{6,4},{8,10},{10,8},{12,14},{14,12},{1,3},{3,1},... | collective-permute-start | bytes 221192 | tf_op jit(solution)/shard_map/ppermute | solution.py:21
  77.6 1.2 %finish_kernel.1 = (bf16[128,1536]{1,0:T(8,128)(2,1)}, bf16[128,1536]{1,0:T(8,128)(2,1)}, bf16[128,1536]{1,0:T(8,128)(2,1)}) custom-call(bf16[128,768]{1,0:T(8,128)(2,1)S(1)} %get-tuple-element.82.refs_0_, bf16[128,384]{1,0:T(8,128)(2,1)S(1)} %get-tuple-element.87.refs_1_, bf16[128,384]{1,0:T(8,128)(2,1)S(1)} %get-tuple-element.90.refs_2_, ...), custom_call_target="tpu_custom_call" | custom-call | flops 44067098624 | bytes 44067 | tf_op jit(solution)/shard_map/finish_kernel/pallas_call | solution.py:308
  78.8 2.3 %collective-permute-done.17.refs_1_ = bf16[288,128]{1,0:T(8,128)(2,1)S(1)} collective-permute-done((bf16[288,128]{1,0:T(8,128)(2,1)S(1)}, bf16[288,128]{1,0:T(8,128)(2,1)S(1)}, u32[]{:S(2)}, u32[]{:S(2)}) %collective-permute-start.17) | collective-permute-done | bytes 73760 | tf_op jit(solution)/shard_map/ppermute | solution.py:21
  81.1 1.2 %update_kernel.1 = (bf16[128,3072]{1,0:T(8,128)(2,1)}, f32[96,128]{1,0:T(8,128)}, f32[128,192]{1,0:T(8,128)S(1)}) custom-call(f32[128,1536]{1,0:T(8,128)S(1)} %get-tuple-element.70.own, bf16[128,1536]{1,0:T(8,128)(2,1)S(1)} %collective-permute-done.11.away, bf16[128,128]{1,0:T(8,128)(2,1)S(1)} %get-tuple-element.72.act, ...), custom_call_target="tpu_custom_call" | custom-call | flops 7446859776 | bytes 7446 | tf_op jit(solution)/shard_map/update_kernel/pallas_call | solution.py:308
  (60 shorter events, 6.9 us)
Async XLA Ops:
  0.6 8.7 %copy-start.2 = (bf16[1,128,1536]{2,1,0:T(8,128)(2,1)S(1)}, bf16[1,128,1536]{2,1,0:T(8,128)(2,1)}, u32[]{:S(2)}) copy-start(bf16[1,128,1536]{2,1,0:T(8,128)(2,1)} %param.11) | copy-start | bytes 1179652
  0.6 8.7 %copy-start.4 = (bf16[1,128,1536]{2,1,0:T(8,128)(2,1)S(1)}, bf16[1,128,1536]{2,1,0:T(8,128)(2,1)}, u32[]{:S(2)}) copy-start(bf16[1,128,1536]{2,1,0:T(8,128)(2,1)} %param.12) | copy-start | bytes 1179652
  0.7 9.2 %copy-start = (bf16[1,128,3072]{2,1,0:T(8,128)(2,1)S(1)}, bf16[1,128,3072]{2,1,0:T(8,128)(2,1)}, u32[]{:S(2)}) copy-start(bf16[1,128,3072]{2,1,0:T(8,128)(2,1)} %param.19) | copy-start | bytes 2359300
  0.7 11.0 %copy-start.1 = (bf16[1,128,1536]{2,1,0:T(8,128)(2,1)S(1)}, bf16[1,128,1536]{2,1,0:T(8,128)(2,1)}, u32[]{:S(2)}) copy-start(bf16[1,128,1536]{2,1,0:T(8,128)(2,1)} %param.10) | copy-start | bytes 1179652
  0.7 11.0 %copy-start.3 = (bf16[1,128,1536]{2,1,0:T(8,128)(2,1)S(1)}, bf16[1,128,1536]{2,1,0:T(8,128)(2,1)}, u32[]{:S(2)}) copy-start(bf16[1,128,1536]{2,1,0:T(8,128)(2,1)} %param.13) | copy-start | bytes 1179652
  0.7 11.0 %copy-start.5 = (bf16[1,128,1536]{2,1,0:T(8,128)(2,1)S(1)}, bf16[1,128,1536]{2,1,0:T(8,128)(2,1)}, u32[]{:S(2)}) copy-start(bf16[1,128,1536]{2,1,0:T(8,128)(2,1)} %param.14) | copy-start | bytes 1179652
  0.7 1.2 %copy-start.6 = (bf16[192,1536]{1,0:T(8,128)(2,1)S(1)}, bf16[192,1536]{1,0:T(8,128)(2,1)}, u32[]{:S(2)}) copy-start(bf16[192,1536]{1,0:T(8,128)(2,1)} %proj.1) | copy-start | bytes 1769476
  4.8 20.9 %collective-permute-start = (bf16[240,1536]{1,0:T(8,128)(2,1)}, bf16[240,1536]{1,0:T(8,128)(2,1)}, u32[]{:S(2)}, u32[]{:S(2)}) collective-permute-start(bf16[240,1536]{1,0:T(8,128)(2,1)} %pack_kernel.1.refs_0_), channel_id=1, source_target_pairs={{0,4},{16,24},{2,6},{18,26},{4,12},{20,16},{6,14},{22,18},{8,0},{2... | collective-permute-start | bytes 2211848 | tf_op jit(solution)/shard_map/ppermute | solution.py:42
  7.9 18.3 %collective-permute-start.1 = (bf16[240,1536]{1,0:T(8,128)(2,1)}, bf16[240,1536]{1,0:T(8,128)(2,1)}, u32[]{:S(2)}, u32[]{:S(2)}) collective-permute-start(bf16[240,1536]{1,0:T(8,128)(2,1)} %pack_kernel.1.refs_0_), channel_id=1, source_target_pairs={{0,2},{2,0},{4,6},{6,4},{8,10},{10,8},{12,14},{14,12},{1,3},{3,1},... | collective-permute-start | bytes 2211848 | tf_op jit(solution)/shard_map/ppermute | solution.py:21
  9.4 1.7 %collective-permute-start.2 = (bf16[128,1536]{1,0:T(8,128)(2,1)S(1)}, bf16[128,1536]{1,0:T(8,128)(2,1)S(1)}, u32[]{:S(2)}, u32[]{:S(2)}) collective-permute-start(bf16[128,1536]{1,0:T(8,128)(2,1)S(1)} %bitcast.24), channel_id=1, source_target_pairs={{0,1},{1,0},{2,3},{3,2},{4,5},{5,4},{6,7},{7,6},{8,9},{9,8},{10,11... | collective-permute-start | bytes 1179656 | tf_op jit(solution)/shard_map/ppermute | solution.py:21
  9.4 2.3 %collective-permute-start.3 = (bf16[128,1536]{1,0:T(8,128)(2,1)S(1)}, bf16[128,1536]{1,0:T(8,128)(2,1)S(1)}, u32[]{:S(2)}, u32[]{:S(2)}) collective-permute-start(bf16[128,1536]{1,0:T(8,128)(2,1)S(1)} %bitcast.33), channel_id=1, source_target_pairs={{0,1},{1,0},{2,3},{3,2},{4,5},{5,4},{6,7},{7,6},{8,9},{9,8},{10,11... | collective-permute-start | bytes 1179656 | tf_op jit(solution)/shard_map/ppermute | solution.py:21
  9.9 7.3 %collective-permute-start.4 = (bf16[128,1536]{1,0:T(8,128)(2,1)S(1)}, bf16[128,1536]{1,0:T(8,128)(2,1)S(1)}, u32[]{:S(2)}, u32[]{:S(2)}) collective-permute-start(bf16[128,1536]{1,0:T(8,128)(2,1)S(1)} %dynamic-slice_bitcast_fusion), channel_id=1, source_target_pairs={{0,1},{1,0},{2,3},{3,2},{4,5},{5,4},{6,7},{7,6},{8,9},{9,8},{10,11... | collective-permute-start | bytes 1179656 | tf_op jit(solution)/shard_map/ppermute | solution.py:21
  26.1 22.3 %collective-permute-start.5 = (bf16[240,1536]{1,0:T(8,128)(2,1)}, bf16[240,1536]{1,0:T(8,128)(2,1)S(1)}, u32[]{:S(2)}, u32[]{:S(2)}) collective-permute-start(bf16[240,1536]{1,0:T(8,128)(2,1)} %collective-permute-done.refs_0_.refs_2_), channel_id=1, source_target_pairs={{0,4},{16,24},{2,6},{18,26},{4,12},{20,16},{6,14},{22,18},{8,0},{2... | collective-permute-start | bytes 2211848 | tf_op jit(solution)/shard_map/ppermute | solution.py:42
  28.7 19.7 %collective-permute-start.6 = (bf16[240,1536]{1,0:T(8,128)(2,1)}, bf16[240,1536]{1,0:T(8,128)(2,1)S(1)}, u32[]{:S(2)}, u32[]{:S(2)}) collective-permute-start(bf16[240,1536]{1,0:T(8,128)(2,1)} %collective-permute-done.refs_0_.refs_2_), channel_id=1, source_target_pairs={{0,2},{2,0},{4,6},{6,4},{8,10},{10,8},{12,14},{14,12},{1,3},{3,1},... | collective-permute-start | bytes 2211848 | tf_op jit(solution)/shard_map/ppermute | solution.py:21
  30.2 18.2 %collective-permute-start.7 = (bf16[240,1536]{1,0:T(8,128)(2,1)}, bf16[240,1536]{1,0:T(8,128)(2,1)S(1)}, u32[]{:S(2)}, u32[]{:S(2)}) collective-permute-start(bf16[240,1536]{1,0:T(8,128)(2,1)} %collective-permute-done.refs_0_.refs_2_), channel_id=1, source_target_pairs={{0,16},{16,0},{1,17},{17,1},{2,18},{18,2},{3,19},{19,3},{4,20},{20... | collective-permute-start | bytes 2211848 | tf_op jit(solution)/shard_map/ppermute | solution.py:21
  31.7 2.3 %collective-permute-start.8 = (bf16[128,1536]{1,0:T(8,128)(2,1)S(1)}, bf16[128,1536]{1,0:T(8,128)(2,1)S(1)}, u32[]{:S(2)}, u32[]{:S(2)}) collective-permute-start(bf16[128,1536]{1,0:T(8,128)(2,1)S(1)} %forward_kernel.1.refs_2_.refs_8_.refs_7_), channel_id=1, source_target_pairs={{0,1},{1,0},{2,3},{3,2},{4,5},{5,4},{6,7},{7,6},{8,9},{9,8},{10,11... | collective-permute-start | bytes 1179656 | tf_op jit(solution)/shard_map/ppermute | solution.py:21
  33.6 17.5 %collective-permute-start.12 = (bf16[48,1536]{1,0:T(8,128)(2,1)S(1)}, bf16[48,1536]{1,0:T(8,128)(2,1)S(1)}, u32[]{:S(2)}, u32[]{:S(2)}) collective-permute-start(bf16[48,1536]{1,0:T(8,128)(2,1)S(1)} %slice.32), channel_id=1, source_target_pairs={{4,0},{24,16},{6,2},{26,18},{12,4},{16,20},{14,6},{18,22},{0,8},{2... | collective-permute-start | bytes 442376 | tf_op jit(solution)/shard_map/ppermute | solution.py:42
  34.0 17.6 %collective-permute-start.13 = (bf16[48,1536]{1,0:T(8,128)(2,1)S(1)}, bf16[48,1536]{1,0:T(8,128)(2,1)S(1)}, u32[]{:S(2)}, u32[]{:S(2)}) collective-permute-start(bf16[48,1536]{1,0:T(8,128)(2,1)S(1)} %slice.33), channel_id=1, source_target_pairs={{0,6},{16,26},{2,4},{18,24},{4,14},{20,18},{6,12},{22,16},{8,2},{2... | collective-permute-start | bytes 442376 | tf_op jit(solution)/shard_map/ppermute | solution.py:42
  48.4 3.2 %copy-start.9 = (bf16[1,128,128]{2,1,0:T(8,128)(2,1)S(1)}, bf16[1,128,128]{2,1,0:T(8,128)(2,1)}, u32[]{:S(2)}) copy-start(bf16[1,128,128]{2,1,0:T(8,128)(2,1)} %param.15) | copy-start | bytes 98308
  48.5 14.2 %collective-permute-start.9 = (bf16[192,1536]{1,0:T(8,128)(2,1)S(1)}, bf16[192,1536]{1,0:T(8,128)(2,1)S(1)}, u32[]{:S(2)}, u32[]{:S(2)}) collective-permute-start(bf16[192,1536]{1,0:T(8,128)(2,1)S(1)} %slice.30), channel_id=1, source_target_pairs={{0,16},{16,0},{1,17},{17,1},{2,18},{18,2},{3,19},{19,3},{4,20},{20... | collective-permute-start | bytes 1769480 | tf_op jit(solution)/shard_map/ppermute | solution.py:21
  49.6 13.2 %collective-permute-start.10 = (bf16[192,1536]{1,0:T(8,128)(2,1)S(1)}, bf16[192,1536]{1,0:T(8,128)(2,1)S(1)}, u32[]{:S(2)}, u32[]{:S(2)}) collective-permute-start(bf16[192,1536]{1,0:T(8,128)(2,1)S(1)} %slice.31), channel_id=1, source_target_pairs={{0,2},{2,0},{4,6},{6,4},{8,10},{10,8},{12,14},{14,12},{1,3},{3,1},... | collective-permute-start | bytes 1769480 | tf_op jit(solution)/shard_map/ppermute | solution.py:21
  54.4 2.7 %collective-permute-start.14 = (bf16[8,288,128]{2,1,0:T(8,128)(2,1)S(1)}, bf16[8,288,128]{2,1,0:T(8,128)(2,1)S(1)}, u32[]{:S(2)}, u32[]{:S(2)}) collective-permute-start(bf16[8,288,128]{2,1,0:T(8,128)(2,1)S(1)} %get-tuple-element.75), channel_id=1, source_target_pairs={{0,1},{1,0},{2,3},{3,2},{4,5},{5,4},{6,7},{7,6},{8,9},{9,8},{10,11... | collective-permute-start | bytes 1769480 | tf_op jit(solution)/shard_map/ppermute | solution.py:21
  56.6 2.4 %collective-permute-start.18 = (bf16[128,768]{1,0:T(8,128)(2,1)S(1)}, bf16[128,768]{1,0:T(8,128)(2,1)S(1)}, u32[]{:S(2)}, u32[]{:S(2)}) collective-permute-start(bf16[128,768]{1,0:T(8,128)(2,1)S(1)} %get-tuple-element.78), channel_id=1, source_target_pairs={{0,1},{1,0},{2,3},{3,2},{4,5},{5,4},{6,7},{7,6},{8,9},{9,8},{10,11... | collective-permute-start | bytes 589832 | tf_op jit(solution)/shard_map/ppermute | solution.py:21
  57.3 9.4 %collective-permute-start.15 = (bf16[4,288,128]{2,1,0:T(8,128)(2,1)S(1)}, bf16[4,288,128]{2,1,0:T(8,128)(2,1)S(1)}, u32[]{:S(2)}, u32[]{:S(2)}) collective-permute-start(bf16[4,288,128]{2,1,0:T(8,128)(2,1)S(1)} %slice.51), channel_id=1, source_target_pairs={{0,4},{2,6},{4,0},{6,2},{8,12},{10,14},{12,8},{14,10},{1,5},{3,7},... | collective-permute-start | bytes 884744 | tf_op jit(solution)/shard_map/ppermute | solution.py:21
  62.6 15.0 %collective-permute-start.21 = (bf16[2,128,768]{2,1,0:T(8,128)(2,1)S(1)}, bf16[2,128,768]{2,1,0:T(8,128)(2,1)S(1)}, u32[]{:S(2)}, u32[]{:S(2)}) collective-permute-start(bf16[2,128,768]{2,1,0:T(8,128)(2,1)S(1)} %get-tuple-element.94), channel_id=1, source_target_pairs={{0,1},{1,0},{2,3},{3,2},{4,5},{5,4},{6,7},{7,6},{8,9},{9,8},{10,11... | collective-permute-start | bytes 1179656 | tf_op jit(solution)/shard_map/ppermute | solution.py:21
  65.6 13.2 %collective-permute-start.11 = (bf16[128,1536]{1,0:T(8,128)(2,1)S(1)}, bf16[128,1536]{1,0:T(8,128)(2,1)S(1)}, u32[]{:S(2)}, u32[]{:S(2)}) collective-permute-start(bf16[128,1536]{1,0:T(8,128)(2,1)S(1)} %get-tuple-element.71), channel_id=1, source_target_pairs={{0,1},{1,0},{2,3},{3,2},{4,5},{5,4},{6,7},{7,6},{8,9},{9,8},{10,11... | collective-permute-start | bytes 1179656 | tf_op jit(solution)/shard_map/ppermute | solution.py:21
  66.1 3.1 %collective-permute-start.19 = (bf16[128,384]{1,0:T(8,128)(2,1)S(1)}, bf16[128,384]{1,0:T(8,128)(2,1)S(1)}, u32[]{:S(2)}, u32[]{:S(2)}) collective-permute-start(bf16[128,384]{1,0:T(8,128)(2,1)S(1)} %get-tuple-element.85), channel_id=1, source_target_pairs={{0,1},{1,0},{2,3},{3,2},{4,5},{5,4},{6,7},{7,6},{8,9},{9,8},{10,11... | collective-permute-start | bytes 294920 | tf_op jit(solution)/shard_map/ppermute | solution.py:21
  66.2 4.9 %collective-permute-start.20 = (bf16[128,384]{1,0:T(8,128)(2,1)S(1)}, bf16[128,384]{1,0:T(8,128)(2,1)S(1)}, u32[]{:S(2)}, u32[]{:S(2)}) collective-permute-start(bf16[128,384]{1,0:T(8,128)(2,1)S(1)} %get-tuple-element.89), channel_id=1, source_target_pairs={{0,1},{1,0},{2,3},{3,2},{4,5},{5,4},{6,7},{7,6},{8,9},{9,8},{10,11... | collective-permute-start | bytes 294920 | tf_op jit(solution)/shard_map/ppermute | solution.py:21
  66.7 10.0 %collective-permute-start.16 = (bf16[2,288,128]{2,1,0:T(8,128)(2,1)S(1)}, bf16[2,288,128]{2,1,0:T(8,128)(2,1)S(1)}, u32[]{:S(2)}, u32[]{:S(2)}) collective-permute-start(bf16[2,288,128]{2,1,0:T(8,128)(2,1)S(1)} %slice.52), channel_id=1, source_target_pairs={{0,8},{2,10},{4,12},{6,14},{8,0},{10,2},{12,4},{14,6},{1,9},{3,11}... | collective-permute-start | bytes 442376 | tf_op jit(solution)/shard_map/ppermute | solution.py:21
  71.0 6.6 %collective-permute-start.22 = (bf16[2,128,384]{2,1,0:T(8,128)(2,1)S(1)}, bf16[2,128,384]{2,1,0:T(8,128)(2,1)S(1)}, u32[]{:S(2)}, u32[]{:S(2)}) collective-permute-start(bf16[2,128,384]{2,1,0:T(8,128)(2,1)S(1)} %get-tuple-element.95), channel_id=1, source_target_pairs={{0,1},{1,0},{2,3},{3,2},{4,5},{5,4},{6,7},{7,6},{8,9},{9,8},{10,11... | collective-permute-start | bytes 589832 | tf_op jit(solution)/shard_map/ppermute | solution.py:21
  72.9 4.7 %collective-permute-start.23 = (bf16[2,128,384]{2,1,0:T(8,128)(2,1)S(1)}, bf16[2,128,384]{2,1,0:T(8,128)(2,1)S(1)}, u32[]{:S(2)}, u32[]{:S(2)}) collective-permute-start(bf16[2,128,384]{2,1,0:T(8,128)(2,1)S(1)} %get-tuple-element.96), channel_id=1, source_target_pairs={{0,1},{1,0},{2,3},{3,2},{4,5},{5,4},{6,7},{7,6},{8,9},{9,8},{10,11... | collective-permute-start | bytes 589832 | tf_op jit(solution)/shard_map/ppermute | solution.py:21
  76.7 4.4 %collective-permute-start.17 = (bf16[288,128]{1,0:T(8,128)(2,1)S(1)}, bf16[288,128]{1,0:T(8,128)(2,1)S(1)}, u32[]{:S(2)}, u32[]{:S(2)}) collective-permute-start(bf16[288,128]{1,0:T(8,128)(2,1)S(1)} %fusion), channel_id=1, source_target_pairs={{0,2},{2,0},{4,6},{6,4},{8,10},{10,8},{12,14},{14,12},{1,3},{3,1},... | collective-permute-start | bytes 221192 | tf_op jit(solution)/shard_map/ppermute | solution.py:21
  (2 other events, 1.7 us)

commit v4 on v3

--- a/solution.py
+++ b/solution.py
@@ -149,7 +149,7 @@
         return
     terms[pl.ds(0, inner)] = dot(attn[...], act_grad[...], ROWS) * scale
     terms[pl.ds(inner, wide)] = dot(cot[...], act[...], ROWS) * scale
-    for place, mask in enumerate((0, 1, 4, 5, 2, 3, 6, 7)):
+    for place, mask in enumerate((0, 4, 1, 5, 2, 6, 3, 7)):
         block = f ^ mask
         for target, half in ((near, core), (far, 1 - core)):
             piece = block * 2 + half
@@ -270,7 +270,7 @@
         value = term[0] + term_far[...].astype(F32)
         rows = down_grad.shape[0]
         down_grad[...] = value[:rows]
-        up_grad[...] = value[rows:].T
+        up_grad[...] = value[rows:]
     core = lax.axis_index("seq")
     half = own.shape[1]
     for c, term in ((core, own[...]), (1 - core, away[...].astype(F32))):
@@ -370,7 +370,7 @@
                 pltpu.SemaphoreType.DMA((3,)),
             ],
             8.53264,
-            16,
+            60,
         )
         z1, x1 = ring_step(message), swap(message, "fsdp", 1)
         z1, x1, attn, cot_far = lax.optimization_barrier((z1, x1, attn, cot_far))
@@ -463,10 +463,10 @@
     far = swap(far, "seq", 1)
     if grouped:
         term = first_term + swap(second_term, "seq", 1).astype(F32)
-        for mask in (2, 4):
+        for mask in (2, 1):
             keep = term.shape[0] // 2
             term = term[:keep] + swap(term[keep:].astype(BF16), "fsdp", mask).astype(F32)
-        term_far = swap(term[1].astype(BF16), "fsdp", 1)
+        term_far = swap(term[1].astype(BF16), "fsdp", 4)
     dq_a, own_a, away_a = backward(groups[0], near, far)
     away_a = swap(away_a, "seq", 1)
     if grouped:
@@ -490,12 +490,12 @@
     outs = [shape((rows, wide))]
     if grouped:
         args += [term, term_far]
-        outs += [shape((96, rank), F32), shape((rank, 192), F32)]
+        outs += [shape((96, rank), F32), shape((192, rank), F32)]
     update, *adapter_grads = call(
         update_kernel, tuple(args), outs, [VMEM] * len(args), [], 7.44686, 24
     )
     if grouped:
-        down_grad, up_grad = adapter_grads
+        down_grad, up_grad = adapter_grads[0], adapter_grads[1].T
     args = (dq_a, dq_b, dq_c, own_a, own_b, own_c, away_a, away_b, away_c)
     query_grad, key_grad, value_grad = call(
         functools.partial(finish_kernel, grouped, groups),

time: 83.4 us -> 78.7 us (0.944)
  local copies, waits for them, and re-layouts: 5.72 us -> 2.09 us
  waiting for transfers between devices: 27 us -> 25.2 us
  Pallas kernels: 26.3 us -> 27.4 us
    unnamed x21 -> x16, local copies, waits for them, and re-layouts: 3.67 us -> 0.04 us
    ppermute x20, waiting for transfers between devices: 7.6 us -> 5.77 us  [swap(): return lax.ppermute(value, axis, pairs)]
    pallas_call x12, Pallas kernels: 26.3 us -> 27.4 us  [call(): pl.pallas_call(kernel, name=name, out_shape=outs, in_specs=in_specs, out_...]
  transfers between devices with their start and end apart: 24 -> 24, of which waited for: 8 -> 9; matrix products, arithmetic and copies ran while one was open for 3% -> 3% of each run, Pallas kernels for 29% -> 31%
where the time goes in v4:
time: 78.7 us; the launch traced here: 78.5 us
  Pallas kernels  27.4 us (35%)
  waiting for transfers between devices  25.2 us (32%)
  starting transfers between devices  22.7 us (29%)
  local copies, waits for them, and re-layouts  2.09 us (3%)
  between operations  0.9 us (1%)
    pallas_call x12, Pallas kernels, call(): pl.pallas_call(kernel, name=name, out_shape=outs, in_specs=in_specs, out_...  27.4 us
    ppermute x4, waiting for transfers between devices, ring_step(): return lax.ppermute(value, ('rep', 'fsdp'), pairs)  19.5 us
    ppermute x20, starting transfers between devices, swap(): return lax.ppermute(value, axis, pairs)  15 us
    ppermute x4, starting transfers between devices, ring_step(): return lax.ppermute(value, ('rep', 'fsdp'), pairs)  7.72 us
    ppermute x20, waiting for transfers between devices, swap(): return lax.ppermute(value, axis, pairs)  5.77 us
  transfers between devices with their start and end apart: 24, of which 9 were waited for; matrix products, arithmetic and copies ran while one was open for 3% of the time, Pallas kernels for 31%

profile of v4, /device:TPU:0, one launch (start us, length us, event | category | flops | bytes accessed | tf_op | source)
XLA Modules:
  0.0 78.5 jit_solution(10162184984903449142)
XLA Ops:
  0.7 2.2 %pack_kernel.1.refs_0_ = bf16[240,1536]{1,0:T(8,128)(2,1)} custom-call(bf16[192,1536]{1,0:T(8,128)(2,1)} %proj.1, bf16[192,128]{1,0:T(8,128)(2,1)} %down_in.1, bf16[128,384]{1,0:T(8,128)(2,1)} %up_in.1), custom_call_target="tpu_custom_call" | custom-call | flops 8532639744 | bytes 8532 | tf_op jit(solution)/shard_map/pack_kernel/pallas_call | solution.py:308
  2.9 3.1 %collective-permute-start = (bf16[240,1536]{1,0:T(8,128)(2,1)}, bf16[240,1536]{1,0:T(8,128)(2,1)}, u32[]{:S(2)}, u32[]{:S(2)}) collective-permute-start(bf16[240,1536]{1,0:T(8,128)(2,1)} %pack_kernel.1.refs_0_), channel_id=1, source_target_pairs={{0,4},{16,24},{2,6},{18,26},{4,12},{20,16},{6,14},{22,18},{8,0},{2... | collective-permute-start | bytes 2211848 | tf_op jit(solution)/shard_map/ppermute | solution.py:42
  6.0 1.5 %collective-permute-start.1 = (bf16[240,1536]{1,0:T(8,128)(2,1)}, bf16[240,1536]{1,0:T(8,128)(2,1)}, u32[]{:S(2)}, u32[]{:S(2)}) collective-permute-start(bf16[240,1536]{1,0:T(8,128)(2,1)} %pack_kernel.1.refs_0_), channel_id=1, source_target_pairs={{0,2},{2,0},{4,6},{6,4},{8,10},{10,8},{12,14},{14,12},{1,3},{3,1},... | collective-permute-start | bytes 2211848 | tf_op jit(solution)/shard_map/ppermute | solution.py:21
  8.1 1.0 %collective-permute-done.2.kf.refs_2_ = bf16[128,1536]{1,0:T(8,128)(2,1)S(1)} collective-permute-done((bf16[128,1536]{1,0:T(8,128)(2,1)S(1)}, bf16[128,1536]{1,0:T(8,128)(2,1)S(1)}, u32[]{:S(2)}, u32[]{:S(2)}) %collective-permute-start.2) | collective-permute-done | bytes 393248 | tf_op jit(solution)/shard_map/ppermute | solution.py:21
  9.2 0.6 collective-permute-done.3.vf.refs_5_
  9.8 5.6 %forward_kernel.1.refs_2_.refs_8_.refs_7_ = bf16[128,1536]{1,0:T(8,128)(2,1)S(1)} custom-call(bf16[128,1536]{1,0:T(8,128)(2,1)S(1)} %bitcast.21, bf16[128,1536]{1,0:T(8,128)(2,1)S(1)} %bitcast.26, bf16[128,1536]{1,0:T(8,128)(2,1)S(1)} %collective-permute-done.2.kf.refs_2_, bf16[128,1536]{1,0:T(8,128)(2,1)S(1)} %bitcast.30, bf16[128,1536]{1,0:T(8,128)(2,1)S(1)} %bitcast.35, ...), custom_call_target="tpu_custom_call" | custom-call | flops 119135000 | bytes 119 | tf_op jit(solution)/shard_map/forward_kernel/pallas_call | solution.py:308
  15.4 8.4 %collective-permute-done.refs_0_.refs_2_ = bf16[240,1536]{1,0:T(8,128)(2,1)} collective-permute-done((bf16[240,1536]{1,0:T(8,128)(2,1)}, bf16[240,1536]{1,0:T(8,128)(2,1)}, u32[]{:S(2)}, u32[]{:S(2)}) %collective-permute-start) | collective-permute-done | bytes 737312 | tf_op jit(solution)/shard_map/ppermute | solution.py:42
  24.2 2.6 %collective-permute-start.5 = (bf16[240,1536]{1,0:T(8,128)(2,1)}, bf16[240,1536]{1,0:T(8,128)(2,1)S(1)}, u32[]{:S(2)}, u32[]{:S(2)}) collective-permute-start(bf16[240,1536]{1,0:T(8,128)(2,1)} %collective-permute-done.refs_0_.refs_2_), channel_id=1, source_target_pairs={{0,4},{16,24},{2,6},{18,26},{4,12},{20,16},{6,14},{22,18},{8,0},{2... | collective-permute-start | bytes 2211848 | tf_op jit(solution)/shard_map/ppermute | solution.py:42
  26.8 1.5 %collective-permute-start.6 = (bf16[240,1536]{1,0:T(8,128)(2,1)}, bf16[240,1536]{1,0:T(8,128)(2,1)S(1)}, u32[]{:S(2)}, u32[]{:S(2)}) collective-permute-start(bf16[240,1536]{1,0:T(8,128)(2,1)} %collective-permute-done.refs_0_.refs_2_), channel_id=1, source_target_pairs={{0,2},{2,0},{4,6},{6,4},{8,10},{10,8},{12,14},{14,12},{1,3},{3,1},... | collective-permute-start | bytes 2211848 | tf_op jit(solution)/shard_map/ppermute | solution.py:21
  28.3 1.5 %collective-permute-start.7 = (bf16[240,1536]{1,0:T(8,128)(2,1)}, bf16[240,1536]{1,0:T(8,128)(2,1)S(1)}, u32[]{:S(2)}, u32[]{:S(2)}) collective-permute-start(bf16[240,1536]{1,0:T(8,128)(2,1)} %collective-permute-done.refs_0_.refs_2_), channel_id=1, source_target_pairs={{0,16},{16,0},{1,17},{17,1},{2,18},{18,2},{3,19},{19,3},{4,20},{20... | collective-permute-start | bytes 2211848 | tf_op jit(solution)/shard_map/ppermute | solution.py:21
  29.8 0.9 %slice.33 = bf16[48,1536]{1,0:T(8,128)(2,1)S(1)} slice(bf16[240,1536]{1,0:T(8,128)(2,1)} %collective-permute-done.refs_0_.refs_2_), slice={[192:240], [0:1536]} | slice | bytes 294912 | tf_op jit(solution)/shard_map/slice | solution.py:378
  30.8 0.9 %slice.32 = bf16[48,1536]{1,0:T(8,128)(2,1)S(1)} slice(bf16[240,1536]{1,0:T(8,128)(2,1)} %collective-permute-done.1.refs_1_), slice={[192:240], [0:1536]} | slice | bytes 294912 | tf_op jit(solution)/shard_map/slice | solution.py:378
  32.1 1.6 %collective-permute-start.13 = (bf16[48,1536]{1,0:T(8,128)(2,1)S(1)}, bf16[48,1536]{1,0:T(8,128)(2,1)S(1)}, u32[]{:S(2)}, u32[]{:S(2)}) collective-permute-start(bf16[48,1536]{1,0:T(8,128)(2,1)S(1)} %slice.33), channel_id=1, source_target_pairs={{0,6},{16,26},{2,4},{18,24},{4,14},{20,18},{6,12},{22,16},{8,2},{2... | collective-permute-start | bytes 442376 | tf_op jit(solution)/shard_map/ppermute | solution.py:42
  33.8 2.2 %project_kernel.4 = (f32[128,384]{1,0:T(8,128)S(1)}, bf16[128,384]{1,0:T(8,128)(2,1)S(1)}, f32[256,1536]{1,0:T(8,128)S(1)}) custom-call(bf16[240,1536]{1,0:T(8,128)(2,1)S(1)} %copy-done.6, bf16[240,1536]{1,0:T(8,128)(2,1)} %collective-permute-done.1.refs_1_, bf16[128,1536]{1,0:T(8,128)(2,1)S(1)} %forward_kernel.1.refs_2_.refs_8_.refs_7_, ...), custom_call_target="tpu_custom_call" | custom-call | flops 668444992 | bytes 668 | tf_op jit(solution)/shard_map/project_kernel/pallas_call | solution.py:308
  35.9 10.5 %collective-permute-done.5.refs_0_.refs_6_ = bf16[240,1536]{1,0:T(8,128)(2,1)S(1)} collective-permute-done((bf16[240,1536]{1,0:T(8,128)(2,1)}, bf16[240,1536]{1,0:T(8,128)(2,1)S(1)}, u32[]{:S(2)}, u32[]{:S(2)}) %collective-permute-start.5) | collective-permute-done | bytes 737312 | tf_op jit(solution)/shard_map/ppermute | solution.py:42
  46.5 1.0 %collective-permute-start.9 = (bf16[192,1536]{1,0:T(8,128)(2,1)S(1)}, bf16[192,1536]{1,0:T(8,128)(2,1)S(1)}, u32[]{:S(2)}, u32[]{:S(2)}) collective-permute-start(bf16[192,1536]{1,0:T(8,128)(2,1)S(1)} %slice.30), channel_id=1, source_target_pairs={{0,16},{16,0},{1,17},{17,1},{2,18},{18,2},{3,19},{19,3},{4,20},{20... | collective-permute-start | bytes 1769480 | tf_op jit(solution)/shard_map/ppermute | solution.py:21
  47.6 1.6 %collective-permute-start.10 = (bf16[192,1536]{1,0:T(8,128)(2,1)S(1)}, bf16[192,1536]{1,0:T(8,128)(2,1)S(1)}, u32[]{:S(2)}, u32[]{:S(2)}) collective-permute-start(bf16[192,1536]{1,0:T(8,128)(2,1)S(1)} %slice.31), channel_id=1, source_target_pairs={{0,2},{2,0},{4,6},{6,4},{8,10},{10,8},{12,14},{14,12},{1,3},{3,1},... | collective-permute-start | bytes 1769480 | tf_op jit(solution)/shard_map/ppermute | solution.py:21
  49.7 2.9 %adapter_kernel.1 = (bf16[1536,128]{1,0:T(8,128)(2,1)S(1)}, bf16[128,3072]{1,0:T(8,128)(2,1)S(1)}, bf16[128,128]{1,0:T(8,128)(2,1)S(1)}, bf16[128,128]{1,0:T(8,1...) custom-call(bf16[240,1536]{1,0:T(8,128)(2,1)S(1)} %copy-done.6, ...), custom_call_target="tpu_custom_call" | custom-call | flops 8738539520 | bytes 8738 | tf_op jit(solution)/shard_map/adapter_kernel/pallas_call | solution.py:308
  52.7 2.1 %project_kernel.5 = (f32[128,768]{1,0:T(8,128)S(1)}, bf16[128,768]{1,0:T(8,128)(2,1)S(1)}, f32[256,1536]{1,0:T(8,128)S(1)}) custom-call(bf16[240,1536]{1,0:T(8,128)(2,1)} %collective-permute-done.refs_0_.refs_2_, bf16[240,1536]{1,0:T(8,128)(2,1)S(1)} %collective-permute-done.6.refs_1_.refs_3_, bf16[128,1536]{1,0:T(8,128)(2,1)S(1)} %forward_kernel.1.refs_2_.refs_8_.refs_7_, ...), custom_call_target="tpu_custom_call" | custom-call | flops 15552499712 | bytes 15552 | tf_op jit(solution)/shard_map/project_kernel/pallas_call | solution.py:308
  54.8 0.5 collective-permute-start.18
  55.5 1.8 %collective-permute-start.15 = (bf16[4,288,128]{2,1,0:T(8,128)(2,1)S(1)}, bf16[4,288,128]{2,1,0:T(8,128)(2,1)S(1)}, u32[]{:S(2)}, u32[]{:S(2)}) collective-permute-start(bf16[4,288,128]{2,1,0:T(8,128)(2,1)S(1)} %slice.51), channel_id=1, source_target_pairs={{0,4},{2,6},{4,0},{6,2},{8,12},{10,14},{12,8},{14,10},{1,5},{3,7},... | collective-permute-start | bytes 884744 | tf_op jit(solution)/shard_map/ppermute | solution.py:21
  57.3 3.6 %backward_kernel.3 = (bf16[128,768]{1,0:T(8,128)(2,1)S(1)}, f32[2,128,768]{2,1,0:T(8,128)S(1)}, bf16[2,128,768]{2,1,0:T(8,128)(2,1)S(1)}) custom-call(bf16[128,1536]{1,0:T(8,128)(2,1)S(1)} %bitcast.22, bf16[128,1536]{1,0:T(8,128)(2,1)S(1)} %bitcast.27, bf16[128,1536]{1,0:T(8,128)(2,1)S(1)} %collective-permute-done.2.kf.refs_2_, ...), custom_call_target="tpu_custom_call" | custom-call | flops 43205500928 | bytes 43205 | tf_op jit(solution)/shard_map/backward_kernel/pallas_call | solution.py:308
  61.0 1.4 %project_kernel.6 = (f32[128,384]{1,0:T(8,128)S(1)}, bf16[128,384]{1,0:T(8,128)(2,1)S(1)}, f32[256,1536]{1,0:T(8,128)S(1)}) custom-call(bf16[240,1536]{1,0:T(8,128)(2,1)S(1)} %collective-permute-done.7.refs_0_.refs_4_, bf16[192,1536]{1,0:T(8,128)(2,1)S(1)} %collective-permute-done.9.refs_1_, bf16[128,1536]{1,0:T(8,128)(2,1)S(1)} %forward_kernel.1.refs_2_.refs_8_.refs_7_, ...), custom_call_target="tpu_custom_call" | custom-call | flops 37193300 | bytes 37 | tf_op jit(solution)/shard_map/project_kernel/pallas_call | solution.py:308
  62.4 1.4 %project_kernel.7 = (f32[128,384]{1,0:T(8,128)S(1)}, bf16[128,384]{1,0:T(8,128)(2,1)S(1)}, f32[128,1536]{1,0:T(8,128)S(1)}, bf16[128,1536]{1,0:T(8,128)(2,1)S(1)}) custom-call(bf16[240,1536]{1,0:T(8,128)(2,1)S(1)} %collective-permute-done.5.refs_0_.refs_6_, bf16[192,1536]{1,0:T(8,128)(2,1)S(1)} %collective-permute-done.10.refs_1_, ...), custom_call_target="tpu_custom_call" | custom-call | flops 32012600 | bytes 32 | tf_op jit(solution)/shard_map/project_kernel/pallas_call | solution.py:308
  64.9 0.6 collective-permute-start.16
  65.8 1.8 %backward_kernel.4 = (bf16[128,384]{1,0:T(8,128)(2,1)S(1)}, f32[2,128,384]{2,1,0:T(8,128)S(1)}, bf16[2,128,384]{2,1,0:T(8,128)(2,1)S(1)}) custom-call(bf16[128,1536]{1,0:T(8,128)(2,1)S(1)} %bitcast.23, bf16[128,1536]{1,0:T(8,128)(2,1)S(1)} %bitcast.28, bf16[128,1536]{1,0:T(8,128)(2,1)S(1)} %collective-permute-done.2.kf.refs_2_, ...), custom_call_target="tpu_custom_call" | custom-call | flops 32519499776 | bytes 32519 | tf_op jit(solution)/shard_map/backward_kernel/pallas_call | solution.py:308
  68.1 1.8 %backward_kernel.5 = (bf16[128,384]{1,0:T(8,128)(2,1)S(1)}, f32[2,128,384]{2,1,0:T(8,128)S(1)}, bf16[2,128,384]{2,1,0:T(8,128)(2,1)S(1)}) custom-call(bf16[128,1536]{1,0:T(8,128)(2,1)S(1)} %bitcast.24, bf16[128,1536]{1,0:T(8,128)(2,1)S(1)} %bitcast.29, bf16[128,1536]{1,0:T(8,128)(2,1)S(1)} %collective-permute-done.2.kf.refs_2_, ...), custom_call_target="tpu_custom_call" | custom-call | flops 43751800 | bytes 43 | tf_op jit(solution)/shard_map/backward_kernel/pallas_call | solution.py:308
  70.1 0.8 collective-permute-done.16
  70.9 2.5 %collective-permute-start.17 = (bf16[288,128]{1,0:T(8,128)(2,1)S(1)}, bf16[288,128]{1,0:T(8,128)(2,1)S(1)}, u32[]{:S(2)}, u32[]{:S(2)}) collective-permute-start(bf16[288,128]{1,0:T(8,128)(2,1)S(1)} %fusion), channel_id=1, source_target_pairs={{0,8},{2,10},{4,12},{6,14},{8,0},{10,2},{12,4},{14,6},{1,9},{3,11}... | collective-permute-start | bytes 221192 | tf_op jit(solution)/shard_map/ppermute | solution.py:21
  73.4 1.2 %finish_kernel.1 = (bf16[128,1536]{1,0:T(8,128)(2,1)}, bf16[128,1536]{1,0:T(8,128)(2,1)}, bf16[128,1536]{1,0:T(8,128)(2,1)}) custom-call(bf16[128,768]{1,0:T(8,128)(2,1)S(1)} %get-tuple-element.82.refs_0_, bf16[128,384]{1,0:T(8,128)(2,1)S(1)} %get-tuple-element.87.refs_1_, bf16[128,384]{1,0:T(8,128)(2,1)S(1)} %get-tuple-element.90.refs_2_, ...), custom_call_target="tpu_custom_call" | custom-call | flops 44067098624 | bytes 44067 | tf_op jit(solution)/shard_map/finish_kernel/pallas_call | solution.py:308
  74.6 2.6 %collective-permute-done.17.refs_1_ = bf16[288,128]{1,0:T(8,128)(2,1)S(1)} collective-permute-done((bf16[288,128]{1,0:T(8,128)(2,1)S(1)}, bf16[288,128]{1,0:T(8,128)(2,1)S(1)}, u32[]{:S(2)}, u32[]{:S(2)}) %collective-permute-start.17) | collective-permute-done | bytes 73760 | tf_op jit(solution)/shard_map/ppermute | solution.py:21
  77.2 1.2 %update_kernel.1 = (bf16[128,3072]{1,0:T(8,128)(2,1)}, f32[96,128]{1,0:T(8,128)}, f32[192,128]{1,0:T(8,128)}) custom-call(f32[128,1536]{1,0:T(8,128)S(1)} %get-tuple-element.70.own, bf16[128,1536]{1,0:T(8,128)(2,1)S(1)} %collective-permute-done.11.away, bf16[128,128]{1,0:T(8,128)(2,1)S(1)} %get-tuple-element.72.act, ...), custom_call_target="tpu_custom_call" | custom-call | flops 7446859776 | bytes 7446 | tf_op jit(solution)/shard_map/update_kernel/pallas_call | solution.py:308
  (55 shorter events, 4.6 us)
Async XLA Ops:
  0.6 6.8 %copy-start.2 = (bf16[1,128,1536]{2,1,0:T(8,128)(2,1)S(1)}, bf16[1,128,1536]{2,1,0:T(8,128)(2,1)}, u32[]{:S(2)}) copy-start(bf16[1,128,1536]{2,1,0:T(8,128)(2,1)} %param.11) | copy-start | bytes 1179652
  0.6 6.8 %copy-start.4 = (bf16[1,128,1536]{2,1,0:T(8,128)(2,1)S(1)}, bf16[1,128,1536]{2,1,0:T(8,128)(2,1)}, u32[]{:S(2)}) copy-start(bf16[1,128,1536]{2,1,0:T(8,128)(2,1)} %param.12) | copy-start | bytes 1179652
  0.7 7.3 %copy-start = (bf16[1,128,3072]{2,1,0:T(8,128)(2,1)S(1)}, bf16[1,128,3072]{2,1,0:T(8,128)(2,1)}, u32[]{:S(2)}) copy-start(bf16[1,128,3072]{2,1,0:T(8,128)(2,1)} %param.19) | copy-start | bytes 2359300
  0.7 9.1 %copy-start.1 = (bf16[1,128,1536]{2,1,0:T(8,128)(2,1)S(1)}, bf16[1,128,1536]{2,1,0:T(8,128)(2,1)}, u32[]{:S(2)}) copy-start(bf16[1,128,1536]{2,1,0:T(8,128)(2,1)} %param.10) | copy-start | bytes 1179652
  0.7 9.1 %copy-start.3 = (bf16[1,128,1536]{2,1,0:T(8,128)(2,1)S(1)}, bf16[1,128,1536]{2,1,0:T(8,128)(2,1)}, u32[]{:S(2)}) copy-start(bf16[1,128,1536]{2,1,0:T(8,128)(2,1)} %param.13) | copy-start | bytes 1179652
  0.7 9.1 %copy-start.5 = (bf16[1,128,1536]{2,1,0:T(8,128)(2,1)S(1)}, bf16[1,128,1536]{2,1,0:T(8,128)(2,1)}, u32[]{:S(2)}) copy-start(bf16[1,128,1536]{2,1,0:T(8,128)(2,1)} %param.14) | copy-start | bytes 1179652
  2.9 20.9 %collective-permute-start = (bf16[240,1536]{1,0:T(8,128)(2,1)}, bf16[240,1536]{1,0:T(8,128)(2,1)}, u32[]{:S(2)}, u32[]{:S(2)}) collective-permute-start(bf16[240,1536]{1,0:T(8,128)(2,1)} %pack_kernel.1.refs_0_), channel_id=1, source_target_pairs={{0,4},{16,24},{2,6},{18,26},{4,12},{20,16},{6,14},{22,18},{8,0},{2... | collective-permute-start | bytes 2211848 | tf_op jit(solution)/shard_map/ppermute | solution.py:42
  6.0 18.3 %collective-permute-start.1 = (bf16[240,1536]{1,0:T(8,128)(2,1)}, bf16[240,1536]{1,0:T(8,128)(2,1)}, u32[]{:S(2)}, u32[]{:S(2)}) collective-permute-start(bf16[240,1536]{1,0:T(8,128)(2,1)} %pack_kernel.1.refs_0_), channel_id=1, source_target_pairs={{0,2},{2,0},{4,6},{6,4},{8,10},{10,8},{12,14},{14,12},{1,3},{3,1},... | collective-permute-start | bytes 2211848 | tf_op jit(solution)/shard_map/ppermute | solution.py:21
  7.4 1.7 %collective-permute-start.2 = (bf16[128,1536]{1,0:T(8,128)(2,1)S(1)}, bf16[128,1536]{1,0:T(8,128)(2,1)S(1)}, u32[]{:S(2)}, u32[]{:S(2)}) collective-permute-start(bf16[128,1536]{1,0:T(8,128)(2,1)S(1)} %bitcast.25), channel_id=1, source_target_pairs={{0,1},{1,0},{2,3},{3,2},{4,5},{5,4},{6,7},{7,6},{8,9},{9,8},{10,11... | collective-permute-start | bytes 1179656 | tf_op jit(solution)/shard_map/ppermute | solution.py:21
  7.5 2.3 %collective-permute-start.3 = (bf16[128,1536]{1,0:T(8,128)(2,1)S(1)}, bf16[128,1536]{1,0:T(8,128)(2,1)S(1)}, u32[]{:S(2)}, u32[]{:S(2)}) collective-permute-start(bf16[128,1536]{1,0:T(8,128)(2,1)S(1)} %bitcast.34), channel_id=1, source_target_pairs={{0,1},{1,0},{2,3},{3,2},{4,5},{5,4},{6,7},{7,6},{8,9},{9,8},{10,11... | collective-permute-start | bytes 1179656 | tf_op jit(solution)/shard_map/ppermute | solution.py:21
  8.0 7.4 %collective-permute-start.4 = (bf16[128,1536]{1,0:T(8,128)(2,1)S(1)}, bf16[128,1536]{1,0:T(8,128)(2,1)S(1)}, u32[]{:S(2)}, u32[]{:S(2)}) collective-permute-start(bf16[128,1536]{1,0:T(8,128)(2,1)S(1)} %dynamic-slice_bitcast_fusion), channel_id=1, source_target_pairs={{0,1},{1,0},{2,3},{3,2},{4,5},{5,4},{6,7},{7,6},{8,9},{9,8},{10,11... | collective-permute-start | bytes 1179656 | tf_op jit(solution)/shard_map/ppermute | solution.py:21
  9.7 24.0 %copy-start.6 = (bf16[240,1536]{1,0:T(8,128)(2,1)S(1)}, bf16[240,1536]{1,0:T(8,128)(2,1)}, u32[]{:S(2)}) copy-start(bf16[240,1536]{1,0:T(8,128)(2,1)} %pack_kernel.1.refs_0_) | copy-start | bytes 2211844
  24.2 22.3 %collective-permute-start.5 = (bf16[240,1536]{1,0:T(8,128)(2,1)}, bf16[240,1536]{1,0:T(8,128)(2,1)S(1)}, u32[]{:S(2)}, u32[]{:S(2)}) collective-permute-start(bf16[240,1536]{1,0:T(8,128)(2,1)} %collective-permute-done.refs_0_.refs_2_), channel_id=1, source_target_pairs={{0,4},{16,24},{2,6},{18,26},{4,12},{20,16},{6,14},{22,18},{8,0},{2... | collective-permute-start | bytes 2211848 | tf_op jit(solution)/shard_map/ppermute | solution.py:42
  26.8 19.7 %collective-permute-start.6 = (bf16[240,1536]{1,0:T(8,128)(2,1)}, bf16[240,1536]{1,0:T(8,128)(2,1)S(1)}, u32[]{:S(2)}, u32[]{:S(2)}) collective-permute-start(bf16[240,1536]{1,0:T(8,128)(2,1)} %collective-permute-done.refs_0_.refs_2_), channel_id=1, source_target_pairs={{0,2},{2,0},{4,6},{6,4},{8,10},{10,8},{12,14},{14,12},{1,3},{3,1},... | collective-permute-start | bytes 2211848 | tf_op jit(solution)/shard_map/ppermute | solution.py:21
  28.3 18.2 %collective-permute-start.7 = (bf16[240,1536]{1,0:T(8,128)(2,1)}, bf16[240,1536]{1,0:T(8,128)(2,1)S(1)}, u32[]{:S(2)}, u32[]{:S(2)}) collective-permute-start(bf16[240,1536]{1,0:T(8,128)(2,1)} %collective-permute-done.refs_0_.refs_2_), channel_id=1, source_target_pairs={{0,16},{16,0},{1,17},{17,1},{2,18},{18,2},{3,19},{19,3},{4,20},{20... | collective-permute-start | bytes 2211848 | tf_op jit(solution)/shard_map/ppermute | solution.py:21
  29.8 2.3 %collective-permute-start.8 = (bf16[128,1536]{1,0:T(8,128)(2,1)S(1)}, bf16[128,1536]{1,0:T(8,128)(2,1)S(1)}, u32[]{:S(2)}, u32[]{:S(2)}) collective-permute-start(bf16[128,1536]{1,0:T(8,128)(2,1)S(1)} %forward_kernel.1.refs_2_.refs_8_.refs_7_), channel_id=1, source_target_pairs={{0,1},{1,0},{2,3},{3,2},{4,5},{5,4},{6,7},{7,6},{8,9},{9,8},{10,11... | collective-permute-start | bytes 1179656 | tf_op jit(solution)/shard_map/ppermute | solution.py:21
  31.7 17.5 %collective-permute-start.12 = (bf16[48,1536]{1,0:T(8,128)(2,1)S(1)}, bf16[48,1536]{1,0:T(8,128)(2,1)S(1)}, u32[]{:S(2)}, u32[]{:S(2)}) collective-permute-start(bf16[48,1536]{1,0:T(8,128)(2,1)S(1)} %slice.32), channel_id=1, source_target_pairs={{4,0},{24,16},{6,2},{26,18},{12,4},{16,20},{14,6},{18,22},{0,8},{2... | collective-permute-start | bytes 442376 | tf_op jit(solution)/shard_map/ppermute | solution.py:42
  32.1 17.6 %collective-permute-start.13 = (bf16[48,1536]{1,0:T(8,128)(2,1)S(1)}, bf16[48,1536]{1,0:T(8,128)(2,1)S(1)}, u32[]{:S(2)}, u32[]{:S(2)}) collective-permute-start(bf16[48,1536]{1,0:T(8,128)(2,1)S(1)} %slice.33), channel_id=1, source_target_pairs={{0,6},{16,26},{2,4},{18,24},{4,14},{20,18},{6,12},{22,16},{8,2},{2... | collective-permute-start | bytes 442376 | tf_op jit(solution)/shard_map/ppermute | solution.py:42
  46.5 3.2 %copy-start.7 = (bf16[1,128,128]{2,1,0:T(8,128)(2,1)S(1)}, bf16[1,128,128]{2,1,0:T(8,128)(2,1)}, u32[]{:S(2)}) copy-start(bf16[1,128,128]{2,1,0:T(8,128)(2,1)} %param.15) | copy-start | bytes 98308
  46.5 14.4 %collective-permute-start.9 = (bf16[192,1536]{1,0:T(8,128)(2,1)S(1)}, bf16[192,1536]{1,0:T(8,128)(2,1)S(1)}, u32[]{:S(2)}, u32[]{:S(2)}) collective-permute-start(bf16[192,1536]{1,0:T(8,128)(2,1)S(1)} %slice.30), channel_id=1, source_target_pairs={{0,16},{16,0},{1,17},{17,1},{2,18},{18,2},{3,19},{19,3},{4,20},{20... | collective-permute-start | bytes 1769480 | tf_op jit(solution)/shard_map/ppermute | solution.py:21
  47.6 13.3 %collective-permute-start.10 = (bf16[192,1536]{1,0:T(8,128)(2,1)S(1)}, bf16[192,1536]{1,0:T(8,128)(2,1)S(1)}, u32[]{:S(2)}, u32[]{:S(2)}) collective-permute-start(bf16[192,1536]{1,0:T(8,128)(2,1)S(1)} %slice.31), channel_id=1, source_target_pairs={{0,2},{2,0},{4,6},{6,4},{8,10},{10,8},{12,14},{14,12},{1,3},{3,1},... | collective-permute-start | bytes 1769480 | tf_op jit(solution)/shard_map/ppermute | solution.py:21
  52.6 2.7 %collective-permute-start.14 = (bf16[8,288,128]{2,1,0:T(8,128)(2,1)S(1)}, bf16[8,288,128]{2,1,0:T(8,128)(2,1)S(1)}, u32[]{:S(2)}, u32[]{:S(2)}) collective-permute-start(bf16[8,288,128]{2,1,0:T(8,128)(2,1)S(1)} %get-tuple-element.75), channel_id=1, source_target_pairs={{0,1},{1,0},{2,3},{3,2},{4,5},{5,4},{6,7},{7,6},{8,9},{9,8},{10,11... | collective-permute-start | bytes 1769480 | tf_op jit(solution)/shard_map/ppermute | solution.py:21
  54.8 2.4 %collective-permute-start.18 = (bf16[128,768]{1,0:T(8,128)(2,1)S(1)}, bf16[128,768]{1,0:T(8,128)(2,1)S(1)}, u32[]{:S(2)}, u32[]{:S(2)}) collective-permute-start(bf16[128,768]{1,0:T(8,128)(2,1)S(1)} %get-tuple-element.78), channel_id=1, source_target_pairs={{0,1},{1,0},{2,3},{3,2},{4,5},{5,4},{6,7},{7,6},{8,9},{9,8},{10,11... | collective-permute-start | bytes 589832 | tf_op jit(solution)/shard_map/ppermute | solution.py:21
  55.5 9.4 %collective-permute-start.15 = (bf16[4,288,128]{2,1,0:T(8,128)(2,1)S(1)}, bf16[4,288,128]{2,1,0:T(8,128)(2,1)S(1)}, u32[]{:S(2)}, u32[]{:S(2)}) collective-permute-start(bf16[4,288,128]{2,1,0:T(8,128)(2,1)S(1)} %slice.51), channel_id=1, source_target_pairs={{0,4},{2,6},{4,0},{6,2},{8,12},{10,14},{12,8},{14,10},{1,5},{3,7},... | collective-permute-start | bytes 884744 | tf_op jit(solution)/shard_map/ppermute | solution.py:21
  60.9 12.6 %collective-permute-start.21 = (bf16[2,128,768]{2,1,0:T(8,128)(2,1)S(1)}, bf16[2,128,768]{2,1,0:T(8,128)(2,1)S(1)}, u32[]{:S(2)}, u32[]{:S(2)}) collective-permute-start(bf16[2,128,768]{2,1,0:T(8,128)(2,1)S(1)} %get-tuple-element.94), channel_id=1, source_target_pairs={{0,1},{1,0},{2,3},{3,2},{4,5},{5,4},{6,7},{7,6},{8,9},{9,8},{10,11... | collective-permute-start | bytes 1179656 | tf_op jit(solution)/shard_map/ppermute | solution.py:21
  63.8 10.8 %collective-permute-start.11 = (bf16[128,1536]{1,0:T(8,128)(2,1)S(1)}, bf16[128,1536]{1,0:T(8,128)(2,1)S(1)}, u32[]{:S(2)}, u32[]{:S(2)}) collective-permute-start(bf16[128,1536]{1,0:T(8,128)(2,1)S(1)} %get-tuple-element.71), channel_id=1, source_target_pairs={{0,1},{1,0},{2,3},{3,2},{4,5},{5,4},{6,7},{7,6},{8,9},{9,8},{10,11... | collective-permute-start | bytes 1179656 | tf_op jit(solution)/shard_map/ppermute | solution.py:21
  64.3 1.5 %collective-permute-start.19 = (bf16[128,384]{1,0:T(8,128)(2,1)S(1)}, bf16[128,384]{1,0:T(8,128)(2,1)S(1)}, u32[]{:S(2)}, u32[]{:S(2)}) collective-permute-start(bf16[128,384]{1,0:T(8,128)(2,1)S(1)} %get-tuple-element.85), channel_id=1, source_target_pairs={{0,1},{1,0},{2,3},{3,2},{4,5},{5,4},{6,7},{7,6},{8,9},{9,8},{10,11... | collective-permute-start | bytes 294920 | tf_op jit(solution)/shard_map/ppermute | solution.py:21
  64.4 3.7 %collective-permute-start.20 = (bf16[128,384]{1,0:T(8,128)(2,1)S(1)}, bf16[128,384]{1,0:T(8,128)(2,1)S(1)}, u32[]{:S(2)}, u32[]{:S(2)}) collective-permute-start(bf16[128,384]{1,0:T(8,128)(2,1)S(1)} %get-tuple-element.89), channel_id=1, source_target_pairs={{0,1},{1,0},{2,3},{3,2},{4,5},{5,4},{6,7},{7,6},{8,9},{9,8},{10,11... | collective-permute-start | bytes 294920 | tf_op jit(solution)/shard_map/ppermute | solution.py:21
  64.9 5.9 %collective-permute-start.16 = (bf16[2,288,128]{2,1,0:T(8,128)(2,1)S(1)}, bf16[2,288,128]{2,1,0:T(8,128)(2,1)S(1)}, u32[]{:S(2)}, u32[]{:S(2)}) collective-permute-start(bf16[2,288,128]{2,1,0:T(8,128)(2,1)S(1)} %slice.52), channel_id=1, source_target_pairs={{0,2},{2,0},{4,6},{6,4},{8,10},{10,8},{12,14},{14,12},{1,3},{3,1},... | collective-permute-start | bytes 442376 | tf_op jit(solution)/shard_map/ppermute | solution.py:21
  67.6 5.8 %collective-permute-start.22 = (bf16[2,128,384]{2,1,0:T(8,128)(2,1)S(1)}, bf16[2,128,384]{2,1,0:T(8,128)(2,1)S(1)}, u32[]{:S(2)}, u32[]{:S(2)}) collective-permute-start(bf16[2,128,384]{2,1,0:T(8,128)(2,1)S(1)} %get-tuple-element.95), channel_id=1, source_target_pairs={{0,1},{1,0},{2,3},{3,2},{4,5},{5,4},{6,7},{7,6},{8,9},{9,8},{10,11... | collective-permute-start | bytes 589832 | tf_op jit(solution)/shard_map/ppermute | solution.py:21
  69.9 3.5 %collective-permute-start.23 = (bf16[2,128,384]{2,1,0:T(8,128)(2,1)S(1)}, bf16[2,128,384]{2,1,0:T(8,128)(2,1)S(1)}, u32[]{:S(2)}, u32[]{:S(2)}) collective-permute-start(bf16[2,128,384]{2,1,0:T(8,128)(2,1)S(1)} %get-tuple-element.96), channel_id=1, source_target_pairs={{0,1},{1,0},{2,3},{3,2},{4,5},{5,4},{6,7},{7,6},{8,9},{9,8},{10,11... | collective-permute-start | bytes 589832 | tf_op jit(solution)/shard_map/ppermute | solution.py:21
  70.9 6.3 %collective-permute-start.17 = (bf16[288,128]{1,0:T(8,128)(2,1)S(1)}, bf16[288,128]{1,0:T(8,128)(2,1)S(1)}, u32[]{:S(2)}, u32[]{:S(2)}) collective-permute-start(bf16[288,128]{1,0:T(8,128)(2,1)S(1)} %fusion), channel_id=1, source_target_pairs={{0,8},{2,10},{4,12},{6,14},{8,0},{10,2},{12,4},{14,6},{1,9},{3,11}... | collective-permute-start | bytes 221192 | tf_op jit(solution)/shard_map/ppermute | solution.py:21

commit v5 on v4

--- a/solution.py
+++ b/solution.py
@@ -263,19 +263,29 @@
 
 
 def update_kernel(own, away, act, up, *refs):
-    if len(refs) == 1:
-        (update,) = refs
-    else:
-        term, term_far, update, down_grad, up_grad = refs
+    held, sems = refs[-2:]
+    refs = refs[:-2]
+    update = refs[0] if len(refs) == 1 else refs[2]
+    core = lax.axis_index("seq")
+    half = own.shape[1]
+    copies = []
+    for i, (c, term) in enumerate(((core, own), (1 - core, away))):
+        for j in range(2):
+            span = slice(j * half // 2, (j + 1) * half // 2)
+            columns = pl.ds(pl.multiple_of(c * half + j * (half // 2), 128), half // 2)
+            held[:, columns] = (term[:, span].astype(F32) + dot(act[...], up[:, columns])).astype(BF16)
+            copies.append(
+                pltpu.make_async_copy(held.at[:, columns], update.at[:, columns], sems.at[2 * i + j])
+            )
+            copies[-1].start()
+    if len(refs) > 1:
+        term, term_far, _, down_grad, up_grad = refs
         value = term[0] + term_far[...].astype(F32)
         rows = down_grad.shape[0]
         down_grad[...] = value[:rows]
         up_grad[...] = value[rows:]
-    core = lax.axis_index("seq")
-    half = own.shape[1]
-    for c, term in ((core, own[...]), (1 - core, away[...].astype(F32))):
-        columns = pl.ds(pl.multiple_of(c * half, 128), half)
-        update[:, columns] = (term + dot(act[...], up[:, columns])).astype(BF16)
+    for copy in copies:
+        copy.wait()
 
 
 def finish_kernel(grouped, groups, *refs):
@@ -303,14 +313,14 @@
     return jax.ShapeDtypeStruct(dims, dtype)
 
 
-def call(kernel, args, outs, in_specs, scratch, cost, megabytes):
+def call(kernel, args, outs, in_specs, scratch, cost, megabytes, placed=None):
     name = getattr(kernel, "func", kernel).__name__
     return pl.pallas_call(
         kernel,
         name=name,
         out_shape=outs,
         in_specs=in_specs,
-        out_specs=[VMEM] * len(outs),
+        out_specs=placed or [VMEM] * len(outs),
         scratch_shapes=scratch,
         compiler_params=pltpu.CompilerParams(vmem_limit_bytes=megabytes * 2**20),
         cost_estimate=pl.CostEstimate(flops=int(cost * 1e9), bytes_accessed=int(cost * 1e3), transcendentals=0),
@@ -492,7 +502,14 @@
         args += [term, term_far]
         outs += [shape((96, rank), F32), shape((192, rank), F32)]
     update, *adapter_grads = call(
-        update_kernel, tuple(args), outs, [VMEM] * len(args), [], 7.44686, 24
+        update_kernel,
+        tuple(args),
+        outs,
+        [VMEM] * len(args),
+        [pltpu.VMEM((rows, wide), BF16), pltpu.SemaphoreType.DMA((4,))],
+        7.44686,
+        24,
+        [HBM] + [VMEM] * (len(outs) - 1),
     )
     if grouped:
         down_grad, up_grad = adapter_grads[0], adapter_grads[1].T

time: 78.7 us -> 79.4 us (level)
  transfers between devices with their start and end apart: 24 -> 24, of which waited for: 9 -> 9; matrix products, arithmetic and copies ran while one was open for 3% -> 3% of each run, Pallas kernels for 31% -> 30%
where the time goes in v5:
time: 79.4 us; the launch traced here: 79.2 us
  Pallas kernels  27.9 us (35%)
  waiting for transfers between devices  25.2 us (32%)
  starting transfers between devices  22.7 us (29%)
  local copies, waits for them, and re-layouts  2.09 us (3%)
  between operations  1.06 us (1%)
    pallas_call x12, Pallas kernels, call(): pl.pallas_call(kernel, name=name, out_shape=outs, in_specs=in_specs, out_...  27.9 us
    ppermute x4, waiting for transfers between devices, ring_step(): return lax.ppermute(value, ('rep', 'fsdp'), pairs)  19.5 us
    ppermute x20, starting transfers between devices, swap(): return lax.ppermute(value, axis, pairs)  15 us
    ppermute x4, starting transfers between devices, ring_step(): return lax.ppermute(value, ('rep', 'fsdp'), pairs)  7.72 us
    ppermute x20, waiting for transfers between devices, swap(): return lax.ppermute(value, axis, pairs)  5.77 us
  transfers between devices with their start and end apart: 24, of which 9 were waited for; matrix products, arithmetic and copies ran while one was open for 3% of the time, Pallas kernels for 30%

profile of v5, /device:TPU:0, one launch (start us, length us, event | category | flops | bytes accessed | tf_op | source)
XLA Modules:
  0.0 79.2 jit_solution(2226925682783136263)
XLA Ops:
  0.7 2.2 %pack_kernel.1.refs_0_ = bf16[240,1536]{1,0:T(8,128)(2,1)} custom-call(bf16[192,1536]{1,0:T(8,128)(2,1)} %proj.1, bf16[192,128]{1,0:T(8,128)(2,1)} %down_in.1, bf16[128,384]{1,0:T(8,128)(2,1)} %up_in.1), custom_call_target="tpu_custom_call" | custom-call | flops 8532639744 | bytes 8532 | tf_op jit(solution)/shard_map/pack_kernel/pallas_call | solution.py:318
  2.9 3.1 %collective-permute-start = (bf16[240,1536]{1,0:T(8,128)(2,1)}, bf16[240,1536]{1,0:T(8,128)(2,1)}, u32[]{:S(2)}, u32[]{:S(2)}) collective-permute-start(bf16[240,1536]{1,0:T(8,128)(2,1)} %pack_kernel.1.refs_0_), channel_id=1, source_target_pairs={{0,4},{16,24},{2,6},{18,26},{4,12},{20,16},{6,14},{22,18},{8,0},{2... | collective-permute-start | bytes 2211848 | tf_op jit(solution)/shard_map/ppermute | solution.py:42
  6.0 1.5 %collective-permute-start.1 = (bf16[240,1536]{1,0:T(8,128)(2,1)}, bf16[240,1536]{1,0:T(8,128)(2,1)}, u32[]{:S(2)}, u32[]{:S(2)}) collective-permute-start(bf16[240,1536]{1,0:T(8,128)(2,1)} %pack_kernel.1.refs_0_), channel_id=1, source_target_pairs={{0,2},{2,0},{4,6},{6,4},{8,10},{10,8},{12,14},{14,12},{1,3},{3,1},... | collective-permute-start | bytes 2211848 | tf_op jit(solution)/shard_map/ppermute | solution.py:21
  8.1 1.0 %collective-permute-done.2.kf.refs_2_ = bf16[128,1536]{1,0:T(8,128)(2,1)S(1)} collective-permute-done((bf16[128,1536]{1,0:T(8,128)(2,1)S(1)}, bf16[128,1536]{1,0:T(8,128)(2,1)S(1)}, u32[]{:S(2)}, u32[]{:S(2)}) %collective-permute-start.2) | collective-permute-done | bytes 393248 | tf_op jit(solution)/shard_map/ppermute | solution.py:21
  9.2 0.6 collective-permute-done.3.vf.refs_5_
  9.8 5.6 %forward_kernel.1.refs_2_.refs_8_.refs_7_ = bf16[128,1536]{1,0:T(8,128)(2,1)S(1)} custom-call(bf16[128,1536]{1,0:T(8,128)(2,1)S(1)} %bitcast.21, bf16[128,1536]{1,0:T(8,128)(2,1)S(1)} %bitcast.26, bf16[128,1536]{1,0:T(8,128)(2,1)S(1)} %collective-permute-done.2.kf.refs_2_, bf16[128,1536]{1,0:T(8,128)(2,1)S(1)} %bitcast.30, bf16[128,1536]{1,0:T(8,128)(2,1)S(1)} %bitcast.35, ...), custom_call_target="tpu_custom_call" | custom-call | flops 119135000 | bytes 119 | tf_op jit(solution)/shard_map/forward_kernel/pallas_call | solution.py:318
  15.4 8.4 %collective-permute-done.refs_0_.refs_2_ = bf16[240,1536]{1,0:T(8,128)(2,1)} collective-permute-done((bf16[240,1536]{1,0:T(8,128)(2,1)}, bf16[240,1536]{1,0:T(8,128)(2,1)}, u32[]{:S(2)}, u32[]{:S(2)}) %collective-permute-start) | collective-permute-done | bytes 737312 | tf_op jit(solution)/shard_map/ppermute | solution.py:42
  24.2 2.6 %collective-permute-start.5 = (bf16[240,1536]{1,0:T(8,128)(2,1)}, bf16[240,1536]{1,0:T(8,128)(2,1)S(1)}, u32[]{:S(2)}, u32[]{:S(2)}) collective-permute-start(bf16[240,1536]{1,0:T(8,128)(2,1)} %collective-permute-done.refs_0_.refs_2_), channel_id=1, source_target_pairs={{0,4},{16,24},{2,6},{18,26},{4,12},{20,16},{6,14},{22,18},{8,0},{2... | collective-permute-start | bytes 2211848 | tf_op jit(solution)/shard_map/ppermute | solution.py:42
  26.8 1.5 %collective-permute-start.6 = (bf16[240,1536]{1,0:T(8,128)(2,1)}, bf16[240,1536]{1,0:T(8,128)(2,1)S(1)}, u32[]{:S(2)}, u32[]{:S(2)}) collective-permute-start(bf16[240,1536]{1,0:T(8,128)(2,1)} %collective-permute-done.refs_0_.refs_2_), channel_id=1, source_target_pairs={{0,2},{2,0},{4,6},{6,4},{8,10},{10,8},{12,14},{14,12},{1,3},{3,1},... | collective-permute-start | bytes 2211848 | tf_op jit(solution)/shard_map/ppermute | solution.py:21
  28.3 1.5 %collective-permute-start.7 = (bf16[240,1536]{1,0:T(8,128)(2,1)}, bf16[240,1536]{1,0:T(8,128)(2,1)S(1)}, u32[]{:S(2)}, u32[]{:S(2)}) collective-permute-start(bf16[240,1536]{1,0:T(8,128)(2,1)} %collective-permute-done.refs_0_.refs_2_), channel_id=1, source_target_pairs={{0,16},{16,0},{1,17},{17,1},{2,18},{18,2},{3,19},{19,3},{4,20},{20... | collective-permute-start | bytes 2211848 | tf_op jit(solution)/shard_map/ppermute | solution.py:21
  29.8 0.9 %slice.33 = bf16[48,1536]{1,0:T(8,128)(2,1)S(1)} slice(bf16[240,1536]{1,0:T(8,128)(2,1)} %collective-permute-done.refs_0_.refs_2_), slice={[192:240], [0:1536]} | slice | bytes 294912 | tf_op jit(solution)/shard_map/slice | solution.py:388
  30.8 0.9 %slice.32 = bf16[48,1536]{1,0:T(8,128)(2,1)S(1)} slice(bf16[240,1536]{1,0:T(8,128)(2,1)} %collective-permute-done.1.refs_1_), slice={[192:240], [0:1536]} | slice | bytes 294912 | tf_op jit(solution)/shard_map/slice | solution.py:388
  32.1 1.6 %collective-permute-start.13 = (bf16[48,1536]{1,0:T(8,128)(2,1)S(1)}, bf16[48,1536]{1,0:T(8,128)(2,1)S(1)}, u32[]{:S(2)}, u32[]{:S(2)}) collective-permute-start(bf16[48,1536]{1,0:T(8,128)(2,1)S(1)} %slice.33), channel_id=1, source_target_pairs={{0,6},{16,26},{2,4},{18,24},{4,14},{20,18},{6,12},{22,16},{8,2},{2... | collective-permute-start | bytes 442376 | tf_op jit(solution)/shard_map/ppermute | solution.py:42
  33.8 2.2 %project_kernel.4 = (f32[128,384]{1,0:T(8,128)S(1)}, bf16[128,384]{1,0:T(8,128)(2,1)S(1)}, f32[256,1536]{1,0:T(8,128)S(1)}) custom-call(bf16[240,1536]{1,0:T(8,128)(2,1)S(1)} %copy-done.6, bf16[240,1536]{1,0:T(8,128)(2,1)} %collective-permute-done.1.refs_1_, bf16[128,1536]{1,0:T(8,128)(2,1)S(1)} %forward_kernel.1.refs_2_.refs_8_.refs_7_, ...), custom_call_target="tpu_custom_call" | custom-call | flops 668444992 | bytes 668 | tf_op jit(solution)/shard_map/project_kernel/pallas_call | solution.py:318
  35.9 10.5 %collective-permute-done.5.refs_0_.refs_6_ = bf16[240,1536]{1,0:T(8,128)(2,1)S(1)} collective-permute-done((bf16[240,1536]{1,0:T(8,128)(2,1)}, bf16[240,1536]{1,0:T(8,128)(2,1)S(1)}, u32[]{:S(2)}, u32[]{:S(2)}) %collective-permute-start.5) | collective-permute-done | bytes 737312 | tf_op jit(solution)/shard_map/ppermute | solution.py:42
  46.5 1.0 %collective-permute-start.9 = (bf16[192,1536]{1,0:T(8,128)(2,1)S(1)}, bf16[192,1536]{1,0:T(8,128)(2,1)S(1)}, u32[]{:S(2)}, u32[]{:S(2)}) collective-permute-start(bf16[192,1536]{1,0:T(8,128)(2,1)S(1)} %slice.30), channel_id=1, source_target_pairs={{0,16},{16,0},{1,17},{17,1},{2,18},{18,2},{3,19},{19,3},{4,20},{20... | collective-permute-start | bytes 1769480 | tf_op jit(solution)/shard_map/ppermute | solution.py:21
  47.6 1.6 %collective-permute-start.10 = (bf16[192,1536]{1,0:T(8,128)(2,1)S(1)}, bf16[192,1536]{1,0:T(8,128)(2,1)S(1)}, u32[]{:S(2)}, u32[]{:S(2)}) collective-permute-start(bf16[192,1536]{1,0:T(8,128)(2,1)S(1)} %slice.31), channel_id=1, source_target_pairs={{0,2},{2,0},{4,6},{6,4},{8,10},{10,8},{12,14},{14,12},{1,3},{3,1},... | collective-permute-start | bytes 1769480 | tf_op jit(solution)/shard_map/ppermute | solution.py:21
  49.7 2.9 %adapter_kernel.1 = (bf16[1536,128]{1,0:T(8,128)(2,1)S(1)}, bf16[128,3072]{1,0:T(8,128)(2,1)S(1)}, bf16[128,128]{1,0:T(8,128)(2,1)S(1)}, bf16[128,128]{1,0:T(8,1...) custom-call(bf16[240,1536]{1,0:T(8,128)(2,1)S(1)} %copy-done.6, ...), custom_call_target="tpu_custom_call" | custom-call | flops 8738539520 | bytes 8738 | tf_op jit(solution)/shard_map/adapter_kernel/pallas_call | solution.py:318
  52.7 2.1 %project_kernel.5 = (f32[128,768]{1,0:T(8,128)S(1)}, bf16[128,768]{1,0:T(8,128)(2,1)S(1)}, f32[256,1536]{1,0:T(8,128)S(1)}) custom-call(bf16[240,1536]{1,0:T(8,128)(2,1)} %collective-permute-done.refs_0_.refs_2_, bf16[240,1536]{1,0:T(8,128)(2,1)S(1)} %collective-permute-done.6.refs_1_.refs_3_, bf16[128,1536]{1,0:T(8,128)(2,1)S(1)} %forward_kernel.1.refs_2_.refs_8_.refs_7_, ...), custom_call_target="tpu_custom_call" | custom-call | flops 15552499712 | bytes 15552 | tf_op jit(solution)/shard_map/project_kernel/pallas_call | solution.py:318
  54.8 0.5 collective-permute-start.18
  55.5 1.8 %collective-permute-start.15 = (bf16[4,288,128]{2,1,0:T(8,128)(2,1)S(1)}, bf16[4,288,128]{2,1,0:T(8,128)(2,1)S(1)}, u32[]{:S(2)}, u32[]{:S(2)}) collective-permute-start(bf16[4,288,128]{2,1,0:T(8,128)(2,1)S(1)} %slice.51), channel_id=1, source_target_pairs={{0,4},{2,6},{4,0},{6,2},{8,12},{10,14},{12,8},{14,10},{1,5},{3,7},... | collective-permute-start | bytes 884744 | tf_op jit(solution)/shard_map/ppermute | solution.py:21
  57.3 3.6 %backward_kernel.3 = (bf16[128,768]{1,0:T(8,128)(2,1)S(1)}, f32[2,128,768]{2,1,0:T(8,128)S(1)}, bf16[2,128,768]{2,1,0:T(8,128)(2,1)S(1)}) custom-call(bf16[128,1536]{1,0:T(8,128)(2,1)S(1)} %bitcast.22, bf16[128,1536]{1,0:T(8,128)(2,1)S(1)} %bitcast.27, bf16[128,1536]{1,0:T(8,128)(2,1)S(1)} %collective-permute-done.2.kf.refs_2_, ...), custom_call_target="tpu_custom_call" | custom-call | flops 43205500928 | bytes 43205 | tf_op jit(solution)/shard_map/backward_kernel/pallas_call | solution.py:318
  61.0 1.4 %project_kernel.6 = (f32[128,384]{1,0:T(8,128)S(1)}, bf16[128,384]{1,0:T(8,128)(2,1)S(1)}, f32[256,1536]{1,0:T(8,128)S(1)}) custom-call(bf16[240,1536]{1,0:T(8,128)(2,1)S(1)} %collective-permute-done.7.refs_0_.refs_4_, bf16[192,1536]{1,0:T(8,128)(2,1)S(1)} %collective-permute-done.9.refs_1_, bf16[128,1536]{1,0:T(8,128)(2,1)S(1)} %forward_kernel.1.refs_2_.refs_8_.refs_7_, ...), custom_call_target="tpu_custom_call" | custom-call | flops 37193300 | bytes 37 | tf_op jit(solution)/shard_map/project_kernel/pallas_call | solution.py:318
  62.4 1.4 %project_kernel.7 = (f32[128,384]{1,0:T(8,128)S(1)}, bf16[128,384]{1,0:T(8,128)(2,1)S(1)}, f32[128,1536]{1,0:T(8,128)S(1)}, bf16[128,1536]{1,0:T(8,128)(2,1)S(1)}) custom-call(bf16[240,1536]{1,0:T(8,128)(2,1)S(1)} %collective-permute-done.5.refs_0_.refs_6_, bf16[192,1536]{1,0:T(8,128)(2,1)S(1)} %collective-permute-done.10.refs_1_, ...), custom_call_target="tpu_custom_call" | custom-call | flops 32012600 | bytes 32 | tf_op jit(solution)/shard_map/project_kernel/pallas_call | solution.py:318
  64.9 0.6 collective-permute-start.16
  65.8 1.8 %backward_kernel.4 = (bf16[128,384]{1,0:T(8,128)(2,1)S(1)}, f32[2,128,384]{2,1,0:T(8,128)S(1)}, bf16[2,128,384]{2,1,0:T(8,128)(2,1)S(1)}) custom-call(bf16[128,1536]{1,0:T(8,128)(2,1)S(1)} %bitcast.23, bf16[128,1536]{1,0:T(8,128)(2,1)S(1)} %bitcast.28, bf16[128,1536]{1,0:T(8,128)(2,1)S(1)} %collective-permute-done.2.kf.refs_2_, ...), custom_call_target="tpu_custom_call" | custom-call | flops 32519499776 | bytes 32519 | tf_op jit(solution)/shard_map/backward_kernel/pallas_call | solution.py:318
  68.1 1.8 %backward_kernel.5 = (bf16[128,384]{1,0:T(8,128)(2,1)S(1)}, f32[2,128,384]{2,1,0:T(8,128)S(1)}, bf16[2,128,384]{2,1,0:T(8,128)(2,1)S(1)}) custom-call(bf16[128,1536]{1,0:T(8,128)(2,1)S(1)} %bitcast.24, bf16[128,1536]{1,0:T(8,128)(2,1)S(1)} %bitcast.29, bf16[128,1536]{1,0:T(8,128)(2,1)S(1)} %collective-permute-done.2.kf.refs_2_, ...), custom_call_target="tpu_custom_call" | custom-call | flops 43751800 | bytes 43 | tf_op jit(solution)/shard_map/backward_kernel/pallas_call | solution.py:318
  70.1 0.8 collective-permute-done.16
  70.9 2.5 %collective-permute-start.17 = (bf16[288,128]{1,0:T(8,128)(2,1)S(1)}, bf16[288,128]{1,0:T(8,128)(2,1)S(1)}, u32[]{:S(2)}, u32[]{:S(2)}) collective-permute-start(bf16[288,128]{1,0:T(8,128)(2,1)S(1)} %fusion), channel_id=1, source_target_pairs={{0,8},{2,10},{4,12},{6,14},{8,0},{10,2},{12,4},{14,6},{1,9},{3,11}... | collective-permute-start | bytes 221192 | tf_op jit(solution)/shard_map/ppermute | solution.py:21
  73.4 1.2 %finish_kernel.1 = (bf16[128,1536]{1,0:T(8,128)(2,1)}, bf16[128,1536]{1,0:T(8,128)(2,1)}, bf16[128,1536]{1,0:T(8,128)(2,1)}) custom-call(bf16[128,768]{1,0:T(8,128)(2,1)S(1)} %get-tuple-element.82.refs_0_, bf16[128,384]{1,0:T(8,128)(2,1)S(1)} %get-tuple-element.87.refs_1_, bf16[128,384]{1,0:T(8,128)(2,1)S(1)} %get-tuple-element.90.refs_2_, ...), custom_call_target="tpu_custom_call" | custom-call | flops 44067098624 | bytes 44067 | tf_op jit(solution)/shard_map/finish_kernel/pallas_call | solution.py:318
  74.6 2.6 %collective-permute-done.17.refs_1_ = bf16[288,128]{1,0:T(8,128)(2,1)S(1)} collective-permute-done((bf16[288,128]{1,0:T(8,128)(2,1)S(1)}, bf16[288,128]{1,0:T(8,128)(2,1)S(1)}, u32[]{:S(2)}, u32[]{:S(2)}) %collective-permute-start.17) | collective-permute-done | bytes 73760 | tf_op jit(solution)/shard_map/ppermute | solution.py:21
  77.2 1.8 %update_kernel.1 = (bf16[128,3072]{1,0:T(8,128)(2,1)}, f32[96,128]{1,0:T(8,128)}, f32[192,128]{1,0:T(8,128)}) custom-call(f32[128,1536]{1,0:T(8,128)S(1)} %get-tuple-element.70.own, bf16[128,1536]{1,0:T(8,128)(2,1)S(1)} %collective-permute-done.11.away, bf16[128,128]{1,0:T(8,128)(2,1)S(1)} %get-tuple-element.72.act, ...), custom_call_target="tpu_custom_call" | custom-call | flops 7446859776 | bytes 7446 | tf_op jit(solution)/shard_map/update_kernel/pallas_call | solution.py:318
  (55 shorter events, 4.6 us)
Async XLA Ops:
  0.6 6.8 %copy-start.2 = (bf16[1,128,1536]{2,1,0:T(8,128)(2,1)S(1)}, bf16[1,128,1536]{2,1,0:T(8,128)(2,1)}, u32[]{:S(2)}) copy-start(bf16[1,128,1536]{2,1,0:T(8,128)(2,1)} %param.11) | copy-start | bytes 1179652
  0.6 6.8 %copy-start.4 = (bf16[1,128,1536]{2,1,0:T(8,128)(2,1)S(1)}, bf16[1,128,1536]{2,1,0:T(8,128)(2,1)}, u32[]{:S(2)}) copy-start(bf16[1,128,1536]{2,1,0:T(8,128)(2,1)} %param.12) | copy-start | bytes 1179652
  0.7 7.3 %copy-start = (bf16[1,128,3072]{2,1,0:T(8,128)(2,1)S(1)}, bf16[1,128,3072]{2,1,0:T(8,128)(2,1)}, u32[]{:S(2)}) copy-start(bf16[1,128,3072]{2,1,0:T(8,128)(2,1)} %param.19) | copy-start | bytes 2359300
  0.7 9.1 %copy-start.1 = (bf16[1,128,1536]{2,1,0:T(8,128)(2,1)S(1)}, bf16[1,128,1536]{2,1,0:T(8,128)(2,1)}, u32[]{:S(2)}) copy-start(bf16[1,128,1536]{2,1,0:T(8,128)(2,1)} %param.10) | copy-start | bytes 1179652
  0.7 9.1 %copy-start.3 = (bf16[1,128,1536]{2,1,0:T(8,128)(2,1)S(1)}, bf16[1,128,1536]{2,1,0:T(8,128)(2,1)}, u32[]{:S(2)}) copy-start(bf16[1,128,1536]{2,1,0:T(8,128)(2,1)} %param.13) | copy-start | bytes 1179652
  0.7 9.1 %copy-start.5 = (bf16[1,128,1536]{2,1,0:T(8,128)(2,1)S(1)}, bf16[1,128,1536]{2,1,0:T(8,128)(2,1)}, u32[]{:S(2)}) copy-start(bf16[1,128,1536]{2,1,0:T(8,128)(2,1)} %param.14) | copy-start | bytes 1179652
  2.9 20.9 %collective-permute-start = (bf16[240,1536]{1,0:T(8,128)(2,1)}, bf16[240,1536]{1,0:T(8,128)(2,1)}, u32[]{:S(2)}, u32[]{:S(2)}) collective-permute-start(bf16[240,1536]{1,0:T(8,128)(2,1)} %pack_kernel.1.refs_0_), channel_id=1, source_target_pairs={{0,4},{16,24},{2,6},{18,26},{4,12},{20,16},{6,14},{22,18},{8,0},{2... | collective-permute-start | bytes 2211848 | tf_op jit(solution)/shard_map/ppermute | solution.py:42
  6.0 18.3 %collective-permute-start.1 = (bf16[240,1536]{1,0:T(8,128)(2,1)}, bf16[240,1536]{1,0:T(8,128)(2,1)}, u32[]{:S(2)}, u32[]{:S(2)}) collective-permute-start(bf16[240,1536]{1,0:T(8,128)(2,1)} %pack_kernel.1.refs_0_), channel_id=1, source_target_pairs={{0,2},{2,0},{4,6},{6,4},{8,10},{10,8},{12,14},{14,12},{1,3},{3,1},... | collective-permute-start | bytes 2211848 | tf_op jit(solution)/shard_map/ppermute | solution.py:21
  7.4 1.7 %collective-permute-start.2 = (bf16[128,1536]{1,0:T(8,128)(2,1)S(1)}, bf16[128,1536]{1,0:T(8,128)(2,1)S(1)}, u32[]{:S(2)}, u32[]{:S(2)}) collective-permute-start(bf16[128,1536]{1,0:T(8,128)(2,1)S(1)} %bitcast.25), channel_id=1, source_target_pairs={{0,1},{1,0},{2,3},{3,2},{4,5},{5,4},{6,7},{7,6},{8,9},{9,8},{10,11... | collective-permute-start | bytes 1179656 | tf_op jit(solution)/shard_map/ppermute | solution.py:21
  7.5 2.3 %collective-permute-start.3 = (bf16[128,1536]{1,0:T(8,128)(2,1)S(1)}, bf16[128,1536]{1,0:T(8,128)(2,1)S(1)}, u32[]{:S(2)}, u32[]{:S(2)}) collective-permute-start(bf16[128,1536]{1,0:T(8,128)(2,1)S(1)} %bitcast.34), channel_id=1, source_target_pairs={{0,1},{1,0},{2,3},{3,2},{4,5},{5,4},{6,7},{7,6},{8,9},{9,8},{10,11... | collective-permute-start | bytes 1179656 | tf_op jit(solution)/shard_map/ppermute | solution.py:21
  8.0 7.4 %collective-permute-start.4 = (bf16[128,1536]{1,0:T(8,128)(2,1)S(1)}, bf16[128,1536]{1,0:T(8,128)(2,1)S(1)}, u32[]{:S(2)}, u32[]{:S(2)}) collective-permute-start(bf16[128,1536]{1,0:T(8,128)(2,1)S(1)} %dynamic-slice_bitcast_fusion), channel_id=1, source_target_pairs={{0,1},{1,0},{2,3},{3,2},{4,5},{5,4},{6,7},{7,6},{8,9},{9,8},{10,11... | collective-permute-start | bytes 1179656 | tf_op jit(solution)/shard_map/ppermute | solution.py:21
  9.7 24.0 %copy-start.6 = (bf16[240,1536]{1,0:T(8,128)(2,1)S(1)}, bf16[240,1536]{1,0:T(8,128)(2,1)}, u32[]{:S(2)}) copy-start(bf16[240,1536]{1,0:T(8,128)(2,1)} %pack_kernel.1.refs_0_) | copy-start | bytes 2211844
  24.2 22.3 %collective-permute-start.5 = (bf16[240,1536]{1,0:T(8,128)(2,1)}, bf16[240,1536]{1,0:T(8,128)(2,1)S(1)}, u32[]{:S(2)}, u32[]{:S(2)}) collective-permute-start(bf16[240,1536]{1,0:T(8,128)(2,1)} %collective-permute-done.refs_0_.refs_2_), channel_id=1, source_target_pairs={{0,4},{16,24},{2,6},{18,26},{4,12},{20,16},{6,14},{22,18},{8,0},{2... | collective-permute-start | bytes 2211848 | tf_op jit(solution)/shard_map/ppermute | solution.py:42
  26.8 19.7 %collective-permute-start.6 = (bf16[240,1536]{1,0:T(8,128)(2,1)}, bf16[240,1536]{1,0:T(8,128)(2,1)S(1)}, u32[]{:S(2)}, u32[]{:S(2)}) collective-permute-start(bf16[240,1536]{1,0:T(8,128)(2,1)} %collective-permute-done.refs_0_.refs_2_), channel_id=1, source_target_pairs={{0,2},{2,0},{4,6},{6,4},{8,10},{10,8},{12,14},{14,12},{1,3},{3,1},... | collective-permute-start | bytes 2211848 | tf_op jit(solution)/shard_map/ppermute | solution.py:21
  28.3 18.2 %collective-permute-start.7 = (bf16[240,1536]{1,0:T(8,128)(2,1)}, bf16[240,1536]{1,0:T(8,128)(2,1)S(1)}, u32[]{:S(2)}, u32[]{:S(2)}) collective-permute-start(bf16[240,1536]{1,0:T(8,128)(2,1)} %collective-permute-done.refs_0_.refs_2_), channel_id=1, source_target_pairs={{0,16},{16,0},{1,17},{17,1},{2,18},{18,2},{3,19},{19,3},{4,20},{20... | collective-permute-start | bytes 2211848 | tf_op jit(solution)/shard_map/ppermute | solution.py:21
  29.8 2.3 %collective-permute-start.8 = (bf16[128,1536]{1,0:T(8,128)(2,1)S(1)}, bf16[128,1536]{1,0:T(8,128)(2,1)S(1)}, u32[]{:S(2)}, u32[]{:S(2)}) collective-permute-start(bf16[128,1536]{1,0:T(8,128)(2,1)S(1)} %forward_kernel.1.refs_2_.refs_8_.refs_7_), channel_id=1, source_target_pairs={{0,1},{1,0},{2,3},{3,2},{4,5},{5,4},{6,7},{7,6},{8,9},{9,8},{10,11... | collective-permute-start | bytes 1179656 | tf_op jit(solution)/shard_map/ppermute | solution.py:21
  31.7 17.5 %collective-permute-start.12 = (bf16[48,1536]{1,0:T(8,128)(2,1)S(1)}, bf16[48,1536]{1,0:T(8,128)(2,1)S(1)}, u32[]{:S(2)}, u32[]{:S(2)}) collective-permute-start(bf16[48,1536]{1,0:T(8,128)(2,1)S(1)} %slice.32), channel_id=1, source_target_pairs={{4,0},{24,16},{6,2},{26,18},{12,4},{16,20},{14,6},{18,22},{0,8},{2... | collective-permute-start | bytes 442376 | tf_op jit(solution)/shard_map/ppermute | solution.py:42
  32.1 17.6 %collective-permute-start.13 = (bf16[48,1536]{1,0:T(8,128)(2,1)S(1)}, bf16[48,1536]{1,0:T(8,128)(2,1)S(1)}, u32[]{:S(2)}, u32[]{:S(2)}) collective-permute-start(bf16[48,1536]{1,0:T(8,128)(2,1)S(1)} %slice.33), channel_id=1, source_target_pairs={{0,6},{16,26},{2,4},{18,24},{4,14},{20,18},{6,12},{22,16},{8,2},{2... | collective-permute-start | bytes 442376 | tf_op jit(solution)/shard_map/ppermute | solution.py:42
  46.5 3.2 %copy-start.7 = (bf16[1,128,128]{2,1,0:T(8,128)(2,1)S(1)}, bf16[1,128,128]{2,1,0:T(8,128)(2,1)}, u32[]{:S(2)}) copy-start(bf16[1,128,128]{2,1,0:T(8,128)(2,1)} %param.15) | copy-start | bytes 98308
  46.5 14.4 %collective-permute-start.9 = (bf16[192,1536]{1,0:T(8,128)(2,1)S(1)}, bf16[192,1536]{1,0:T(8,128)(2,1)S(1)}, u32[]{:S(2)}, u32[]{:S(2)}) collective-permute-start(bf16[192,1536]{1,0:T(8,128)(2,1)S(1)} %slice.30), channel_id=1, source_target_pairs={{0,16},{16,0},{1,17},{17,1},{2,18},{18,2},{3,19},{19,3},{4,20},{20... | collective-permute-start | bytes 1769480 | tf_op jit(solution)/shard_map/ppermute | solution.py:21
  47.6 13.3 %collective-permute-start.10 = (bf16[192,1536]{1,0:T(8,128)(2,1)S(1)}, bf16[192,1536]{1,0:T(8,128)(2,1)S(1)}, u32[]{:S(2)}, u32[]{:S(2)}) collective-permute-start(bf16[192,1536]{1,0:T(8,128)(2,1)S(1)} %slice.31), channel_id=1, source_target_pairs={{0,2},{2,0},{4,6},{6,4},{8,10},{10,8},{12,14},{14,12},{1,3},{3,1},... | collective-permute-start | bytes 1769480 | tf_op jit(solution)/shard_map/ppermute | solution.py:21
  52.6 2.7 %collective-permute-start.14 = (bf16[8,288,128]{2,1,0:T(8,128)(2,1)S(1)}, bf16[8,288,128]{2,1,0:T(8,128)(2,1)S(1)}, u32[]{:S(2)}, u32[]{:S(2)}) collective-permute-start(bf16[8,288,128]{2,1,0:T(8,128)(2,1)S(1)} %get-tuple-element.75), channel_id=1, source_target_pairs={{0,1},{1,0},{2,3},{3,2},{4,5},{5,4},{6,7},{7,6},{8,9},{9,8},{10,11... | collective-permute-start | bytes 1769480 | tf_op jit(solution)/shard_map/ppermute | solution.py:21
  54.8 2.4 %collective-permute-start.18 = (bf16[128,768]{1,0:T(8,128)(2,1)S(1)}, bf16[128,768]{1,0:T(8,128)(2,1)S(1)}, u32[]{:S(2)}, u32[]{:S(2)}) collective-permute-start(bf16[128,768]{1,0:T(8,128)(2,1)S(1)} %get-tuple-element.78), channel_id=1, source_target_pairs={{0,1},{1,0},{2,3},{3,2},{4,5},{5,4},{6,7},{7,6},{8,9},{9,8},{10,11... | collective-permute-start | bytes 589832 | tf_op jit(solution)/shard_map/ppermute | solution.py:21
  55.5 9.4 %collective-permute-start.15 = (bf16[4,288,128]{2,1,0:T(8,128)(2,1)S(1)}, bf16[4,288,128]{2,1,0:T(8,128)(2,1)S(1)}, u32[]{:S(2)}, u32[]{:S(2)}) collective-permute-start(bf16[4,288,128]{2,1,0:T(8,128)(2,1)S(1)} %slice.51), channel_id=1, source_target_pairs={{0,4},{2,6},{4,0},{6,2},{8,12},{10,14},{12,8},{14,10},{1,5},{3,7},... | collective-permute-start | bytes 884744 | tf_op jit(solution)/shard_map/ppermute | solution.py:21
  60.9 12.6 %collective-permute-start.21 = (bf16[2,128,768]{2,1,0:T(8,128)(2,1)S(1)}, bf16[2,128,768]{2,1,0:T(8,128)(2,1)S(1)}, u32[]{:S(2)}, u32[]{:S(2)}) collective-permute-start(bf16[2,128,768]{2,1,0:T(8,128)(2,1)S(1)} %get-tuple-element.94), channel_id=1, source_target_pairs={{0,1},{1,0},{2,3},{3,2},{4,5},{5,4},{6,7},{7,6},{8,9},{9,8},{10,11... | collective-permute-start | bytes 1179656 | tf_op jit(solution)/shard_map/ppermute | solution.py:21
  63.8 10.8 %collective-permute-start.11 = (bf16[128,1536]{1,0:T(8,128)(2,1)S(1)}, bf16[128,1536]{1,0:T(8,128)(2,1)S(1)}, u32[]{:S(2)}, u32[]{:S(2)}) collective-permute-start(bf16[128,1536]{1,0:T(8,128)(2,1)S(1)} %get-tuple-element.71), channel_id=1, source_target_pairs={{0,1},{1,0},{2,3},{3,2},{4,5},{5,4},{6,7},{7,6},{8,9},{9,8},{10,11... | collective-permute-start | bytes 1179656 | tf_op jit(solution)/shard_map/ppermute | solution.py:21
  64.3 1.5 %collective-permute-start.19 = (bf16[128,384]{1,0:T(8,128)(2,1)S(1)}, bf16[128,384]{1,0:T(8,128)(2,1)S(1)}, u32[]{:S(2)}, u32[]{:S(2)}) collective-permute-start(bf16[128,384]{1,0:T(8,128)(2,1)S(1)} %get-tuple-element.85), channel_id=1, source_target_pairs={{0,1},{1,0},{2,3},{3,2},{4,5},{5,4},{6,7},{7,6},{8,9},{9,8},{10,11... | collective-permute-start | bytes 294920 | tf_op jit(solution)/shard_map/ppermute | solution.py:21
  64.4 3.7 %collective-permute-start.20 = (bf16[128,384]{1,0:T(8,128)(2,1)S(1)}, bf16[128,384]{1,0:T(8,128)(2,1)S(1)}, u32[]{:S(2)}, u32[]{:S(2)}) collective-permute-start(bf16[128,384]{1,0:T(8,128)(2,1)S(1)} %get-tuple-element.89), channel_id=1, source_target_pairs={{0,1},{1,0},{2,3},{3,2},{4,5},{5,4},{6,7},{7,6},{8,9},{9,8},{10,11... | collective-permute-start | bytes 294920 | tf_op jit(solution)/shard_map/ppermute | solution.py:21
  64.9 5.9 %collective-permute-start.16 = (bf16[2,288,128]{2,1,0:T(8,128)(2,1)S(1)}, bf16[2,288,128]{2,1,0:T(8,128)(2,1)S(1)}, u32[]{:S(2)}, u32[]{:S(2)}) collective-permute-start(bf16[2,288,128]{2,1,0:T(8,128)(2,1)S(1)} %slice.52), channel_id=1, source_target_pairs={{0,2},{2,0},{4,6},{6,4},{8,10},{10,8},{12,14},{14,12},{1,3},{3,1},... | collective-permute-start | bytes 442376 | tf_op jit(solution)/shard_map/ppermute | solution.py:21
  67.6 5.8 %collective-permute-start.22 = (bf16[2,128,384]{2,1,0:T(8,128)(2,1)S(1)}, bf16[2,128,384]{2,1,0:T(8,128)(2,1)S(1)}, u32[]{:S(2)}, u32[]{:S(2)}) collective-permute-start(bf16[2,128,384]{2,1,0:T(8,128)(2,1)S(1)} %get-tuple-element.95), channel_id=1, source_target_pairs={{0,1},{1,0},{2,3},{3,2},{4,5},{5,4},{6,7},{7,6},{8,9},{9,8},{10,11... | collective-permute-start | bytes 589832 | tf_op jit(solution)/shard_map/ppermute | solution.py:21
  69.9 3.5 %collective-permute-start.23 = (bf16[2,128,384]{2,1,0:T(8,128)(2,1)S(1)}, bf16[2,128,384]{2,1,0:T(8,128)(2,1)S(1)}, u32[]{:S(2)}, u32[]{:S(2)}) collective-permute-start(bf16[2,128,384]{2,1,0:T(8,128)(2,1)S(1)} %get-tuple-element.96), channel_id=1, source_target_pairs={{0,1},{1,0},{2,3},{3,2},{4,5},{5,4},{6,7},{7,6},{8,9},{9,8},{10,11... | collective-permute-start | bytes 589832 | tf_op jit(solution)/shard_map/ppermute | solution.py:21
  70.9 6.3 %collective-permute-start.17 = (bf16[288,128]{1,0:T(8,128)(2,1)S(1)}, bf16[288,128]{1,0:T(8,128)(2,1)S(1)}, u32[]{:S(2)}, u32[]{:S(2)}) collective-permute-start(bf16[288,128]{1,0:T(8,128)(2,1)S(1)} %fusion), channel_id=1, source_target_pairs={{0,8},{2,10},{4,12},{6,14},{8,0},{10,2},{12,4},{14,6},{1,9},{3,11}... | collective-permute-start | bytes 221192 | tf_op jit(solution)/shard_map/ppermute | solution.py:21

commit v6 on v4

--- a/solution.py
+++ b/solution.py
@@ -89,22 +89,34 @@
         attn[:, c] = dot(prob, values[:, c]).astype(BF16)
 
 
-def pack_kernel(proj, down_in, up_in, message, down, up, sems):
+def pack_kernel(proj, down_in, up_in, message, down, up, held, sems):
     depth = proj.shape[0]
+    parts = [pl.ds(start, 48) for start in range(0, depth + 48, 48)]
+    adapters = [
+        pltpu.make_async_copy(down_in, down, sems.at[0, 0]),
+        pltpu.make_async_copy(up_in, up, sems.at[0, 1]),
+    ]
     copies = [
-        pltpu.make_async_copy(down_in, down, sems.at[0]),
-        pltpu.make_async_copy(up_in, up, sems.at[1]),
-        pltpu.make_async_copy(proj, message.at[pl.ds(0, depth)], sems.at[2]),
+        pltpu.make_async_copy(proj.at[part], held.at[part], sems.at[1, i])
+        for i, part in enumerate(parts[:-1])
     ]
-    start_all(copies)
-    copies[0].wait()
-    copies[1].wait()
+    start_all(adapters + copies)
+    for copy in adapters:
+        copy.wait()
     for j in range(12):
         c = slice(128 * j, 128 * j + 128)
-        message[depth : depth + 16, c] = down[16 * j : 16 * j + 16]
+        held[depth : depth + 16, c] = down[16 * j : 16 * j + 16]
         a, b = j // 3, j % 3
-        message[depth + 16 : depth + 48, c] = up[32 * a : 32 * a + 32, 128 * b : 128 * b + 128]
-    copies[2].wait()
+        held[depth + 16 : depth + 48, c] = up[32 * a : 32 * a + 32, 128 * b : 128 * b + 128]
+    away = [
+        pltpu.make_async_copy(held.at[part], message.at[part], sems.at[2, i]) for i, part in enumerate(parts)
+    ]
+    away[-1].start()
+    for copy, other in zip(copies, away):
+        copy.wait()
+        other.start()
+    for other in away:
+        other.wait()
 
 
 def adapter_kernel(packed, scale, *refs):
@@ -303,14 +315,14 @@
     return jax.ShapeDtypeStruct(dims, dtype)
 
 
-def call(kernel, args, outs, in_specs, scratch, cost, megabytes):
+def call(kernel, args, outs, in_specs, scratch, cost, megabytes, placed=None):
     name = getattr(kernel, "func", kernel).__name__
     return pl.pallas_call(
         kernel,
         name=name,
         out_shape=outs,
         in_specs=in_specs,
-        out_specs=[VMEM] * len(outs),
+        out_specs=placed or [VMEM] * len(outs),
         scratch_shapes=scratch,
         compiler_params=pltpu.CompilerParams(vmem_limit_bytes=megabytes * 2**20),
         cost_estimate=pl.CostEstimate(flops=int(cost * 1e9), bytes_accessed=int(cost * 1e3), transcendentals=0),
@@ -367,10 +379,12 @@
             [
                 pltpu.VMEM(adapter_down.shape, BF16),
                 pltpu.VMEM(adapter_up.shape, BF16),
-                pltpu.SemaphoreType.DMA((3,)),
+                pltpu.VMEM((depth + 48, half), BF16),
+                pltpu.SemaphoreType.DMA((3, 5)),
             ],
             8.53264,
             60,
+            [ANY],
         )
         z1, x1 = ring_step(message), swap(message, "fsdp", 1)
         z1, x1, attn, cot_far = lax.optimization_barrier((z1, x1, attn, cot_far))
@@ -401,7 +415,7 @@
             [ANY] * (2 * count) + [VMEM] * (len(args) - 2 * count),
             [pltpu.VMEM((count, width, half), BF16), pltpu.SemaphoreType.DMA((2 * count,))],
             (0.668445, 15.5525, 0.0371933, 0.0320126)[numbers[-1]],
-            24,
+            18,
         )
 
     near, far, total = project((0,), [message, x1] if grouped else pieces[:2])
@@ -433,7 +447,7 @@
         [ANY] * len(adapters) + [VMEM] * 3,
         scratch,
         8.73854,
-        24,
+        18,
     )
     def backward(numbers, near, far):
         count = len(numbers)
@@ -492,7 +506,7 @@
         args += [term, term_far]
         outs += [shape((96, rank), F32), shape((192, rank), F32)]
     update, *adapter_grads = call(
-        update_kernel, tuple(args), outs, [VMEM] * len(args), [], 7.44686, 24
+        update_kernel, tuple(args), outs, [VMEM] * len(args), [], 7.44686, 18
     )
     if grouped:
         down_grad, up_grad = adapter_grads[0], adapter_grads[1].T
@@ -504,7 +518,7 @@
         [VMEM] * len(args),
         [],
         44.0671,
-        24,
+        18,
     )
     return (update[None], query_grad[None], key_grad[None], value_grad[None], down_grad, up_grad)
 

time: 78.7 us -> 78.7 us (level)
  no operation moved by 1% of the time
where the time goes in v6:
time: 78.7 us; the launch traced here: 78.4 us
  Pallas kernels  27.3 us (35%)
  waiting for transfers between devices  25.3 us (32%)
  starting transfers between devices  22.7 us (29%)
  local copies, waits for them, and re-layouts  2.09 us (3%)
  between operations  0.9 us (1%)
    pallas_call x12, Pallas kernels, call(): pl.pallas_call(kernel, name=name, out_shape=outs, in_specs=in_specs, out_...  27.3 us
    ppermute x4, waiting for transfers between devices, ring_step(): return lax.ppermute(value, ('rep', 'fsdp'), pairs)  19.5 us
    ppermute x20, starting transfers between devices, swap(): return lax.ppermute(value, axis, pairs)  15 us
    ppermute x4, starting transfers between devices, ring_step(): return lax.ppermute(value, ('rep', 'fsdp'), pairs)  7.72 us
    ppermute x20, waiting for transfers between devices, swap(): return lax.ppermute(value, axis, pairs)  5.78 us
  transfers between devices with their start and end apart: 24, of which 9 were waited for; matrix products, arithmetic and copies ran while one was open for 3% of the time, Pallas kernels for 31%

profile of v6, /device:TPU:0, one launch (start us, length us, event | category | flops | bytes accessed | tf_op | source)
XLA Modules:
  0.0 78.4 jit_solution(17373951683847446208)
XLA Ops:
  0.7 2.1 %pack_kernel.1.refs_0_ = bf16[240,1536]{1,0:T(8,128)(2,1)} custom-call(bf16[192,1536]{1,0:T(8,128)(2,1)} %proj.1, bf16[192,128]{1,0:T(8,128)(2,1)} %down_in.1, bf16[128,384]{1,0:T(8,128)(2,1)} %up_in.1), custom_call_target="tpu_custom_call" | custom-call | flops 8532639744 | bytes 8532 | tf_op jit(solution)/shard_map/pack_kernel/pallas_call | solution.py:320
  2.8 3.1 %collective-permute-start = (bf16[240,1536]{1,0:T(8,128)(2,1)}, bf16[240,1536]{1,0:T(8,128)(2,1)}, u32[]{:S(2)}, u32[]{:S(2)}) collective-permute-start(bf16[240,1536]{1,0:T(8,128)(2,1)} %pack_kernel.1.refs_0_), channel_id=1, source_target_pairs={{0,4},{16,24},{2,6},{18,26},{4,12},{20,16},{6,14},{22,18},{8,0},{2... | collective-permute-start | bytes 2211848 | tf_op jit(solution)/shard_map/ppermute | solution.py:42
  5.9 1.5 %collective-permute-start.1 = (bf16[240,1536]{1,0:T(8,128)(2,1)}, bf16[240,1536]{1,0:T(8,128)(2,1)}, u32[]{:S(2)}, u32[]{:S(2)}) collective-permute-start(bf16[240,1536]{1,0:T(8,128)(2,1)} %pack_kernel.1.refs_0_), channel_id=1, source_target_pairs={{0,2},{2,0},{4,6},{6,4},{8,10},{10,8},{12,14},{14,12},{1,3},{3,1},... | collective-permute-start | bytes 2211848 | tf_op jit(solution)/shard_map/ppermute | solution.py:21
  8.1 1.0 %collective-permute-done.2.kf.refs_2_ = bf16[128,1536]{1,0:T(8,128)(2,1)S(1)} collective-permute-done((bf16[128,1536]{1,0:T(8,128)(2,1)S(1)}, bf16[128,1536]{1,0:T(8,128)(2,1)S(1)}, u32[]{:S(2)}, u32[]{:S(2)}) %collective-permute-start.2) | collective-permute-done | bytes 393248 | tf_op jit(solution)/shard_map/ppermute | solution.py:21
  9.1 0.6 collective-permute-done.3.vf.refs_5_
  9.7 5.6 %forward_kernel.1.refs_2_.refs_8_.refs_7_ = bf16[128,1536]{1,0:T(8,128)(2,1)S(1)} custom-call(bf16[128,1536]{1,0:T(8,128)(2,1)S(1)} %bitcast.21, bf16[128,1536]{1,0:T(8,128)(2,1)S(1)} %bitcast.26, bf16[128,1536]{1,0:T(8,128)(2,1)S(1)} %collective-permute-done.2.kf.refs_2_, bf16[128,1536]{1,0:T(8,128)(2,1)S(1)} %bitcast.30, bf16[128,1536]{1,0:T(8,128)(2,1)S(1)} %bitcast.35, ...), custom_call_target="tpu_custom_call" | custom-call | flops 119135000 | bytes 119 | tf_op jit(solution)/shard_map/forward_kernel/pallas_call | solution.py:320
  15.3 8.4 %collective-permute-done.refs_0_.refs_2_ = bf16[240,1536]{1,0:T(8,128)(2,1)} collective-permute-done((bf16[240,1536]{1,0:T(8,128)(2,1)}, bf16[240,1536]{1,0:T(8,128)(2,1)}, u32[]{:S(2)}, u32[]{:S(2)}) %collective-permute-start) | collective-permute-done | bytes 737312 | tf_op jit(solution)/shard_map/ppermute | solution.py:42
  24.2 2.6 %collective-permute-start.5 = (bf16[240,1536]{1,0:T(8,128)(2,1)}, bf16[240,1536]{1,0:T(8,128)(2,1)S(1)}, u32[]{:S(2)}, u32[]{:S(2)}) collective-permute-start(bf16[240,1536]{1,0:T(8,128)(2,1)} %collective-permute-done.refs_0_.refs_2_), channel_id=1, source_target_pairs={{0,4},{16,24},{2,6},{18,26},{4,12},{20,16},{6,14},{22,18},{8,0},{2... | collective-permute-start | bytes 2211848 | tf_op jit(solution)/shard_map/ppermute | solution.py:42
  26.8 1.5 %collective-permute-start.6 = (bf16[240,1536]{1,0:T(8,128)(2,1)}, bf16[240,1536]{1,0:T(8,128)(2,1)S(1)}, u32[]{:S(2)}, u32[]{:S(2)}) collective-permute-start(bf16[240,1536]{1,0:T(8,128)(2,1)} %collective-permute-done.refs_0_.refs_2_), channel_id=1, source_target_pairs={{0,2},{2,0},{4,6},{6,4},{8,10},{10,8},{12,14},{14,12},{1,3},{3,1},... | collective-permute-start | bytes 2211848 | tf_op jit(solution)/shard_map/ppermute | solution.py:21
  28.3 1.5 %collective-permute-start.7 = (bf16[240,1536]{1,0:T(8,128)(2,1)}, bf16[240,1536]{1,0:T(8,128)(2,1)S(1)}, u32[]{:S(2)}, u32[]{:S(2)}) collective-permute-start(bf16[240,1536]{1,0:T(8,128)(2,1)} %collective-permute-done.refs_0_.refs_2_), channel_id=1, source_target_pairs={{0,16},{16,0},{1,17},{17,1},{2,18},{18,2},{3,19},{19,3},{4,20},{20... | collective-permute-start | bytes 2211848 | tf_op jit(solution)/shard_map/ppermute | solution.py:21
  29.8 0.9 %slice.33 = bf16[48,1536]{1,0:T(8,128)(2,1)S(1)} slice(bf16[240,1536]{1,0:T(8,128)(2,1)} %collective-permute-done.refs_0_.refs_2_), slice={[192:240], [0:1536]} | slice | bytes 294912 | tf_op jit(solution)/shard_map/slice | solution.py:392
  30.7 0.9 %slice.32 = bf16[48,1536]{1,0:T(8,128)(2,1)S(1)} slice(bf16[240,1536]{1,0:T(8,128)(2,1)} %collective-permute-done.1.refs_1_), slice={[192:240], [0:1536]} | slice | bytes 294912 | tf_op jit(solution)/shard_map/slice | solution.py:392
  32.1 1.6 %collective-permute-start.13 = (bf16[48,1536]{1,0:T(8,128)(2,1)S(1)}, bf16[48,1536]{1,0:T(8,128)(2,1)S(1)}, u32[]{:S(2)}, u32[]{:S(2)}) collective-permute-start(bf16[48,1536]{1,0:T(8,128)(2,1)S(1)} %slice.33), channel_id=1, source_target_pairs={{0,6},{16,26},{2,4},{18,24},{4,14},{20,18},{6,12},{22,16},{8,2},{2... | collective-permute-start | bytes 442376 | tf_op jit(solution)/shard_map/ppermute | solution.py:42
  33.7 2.2 %project_kernel.4 = (f32[128,384]{1,0:T(8,128)S(1)}, bf16[128,384]{1,0:T(8,128)(2,1)S(1)}, f32[256,1536]{1,0:T(8,128)S(1)}) custom-call(bf16[240,1536]{1,0:T(8,128)(2,1)S(1)} %copy-done.6, bf16[240,1536]{1,0:T(8,128)(2,1)} %collective-permute-done.1.refs_1_, bf16[128,1536]{1,0:T(8,128)(2,1)S(1)} %forward_kernel.1.refs_2_.refs_8_.refs_7_, ...), custom_call_target="tpu_custom_call" | custom-call | flops 668444992 | bytes 668 | tf_op jit(solution)/shard_map/project_kernel/pallas_call | solution.py:320
  35.9 10.5 %collective-permute-done.5.refs_0_.refs_6_ = bf16[240,1536]{1,0:T(8,128)(2,1)S(1)} collective-permute-done((bf16[240,1536]{1,0:T(8,128)(2,1)}, bf16[240,1536]{1,0:T(8,128)(2,1)S(1)}, u32[]{:S(2)}, u32[]{:S(2)}) %collective-permute-start.5) | collective-permute-done | bytes 737312 | tf_op jit(solution)/shard_map/ppermute | solution.py:42
  46.5 1.0 %collective-permute-start.9 = (bf16[192,1536]{1,0:T(8,128)(2,1)S(1)}, bf16[192,1536]{1,0:T(8,128)(2,1)S(1)}, u32[]{:S(2)}, u32[]{:S(2)}) collective-permute-start(bf16[192,1536]{1,0:T(8,128)(2,1)S(1)} %slice.30), channel_id=1, source_target_pairs={{0,16},{16,0},{1,17},{17,1},{2,18},{18,2},{3,19},{19,3},{4,20},{20... | collective-permute-start | bytes 1769480 | tf_op jit(solution)/shard_map/ppermute | solution.py:21
  47.6 1.6 %collective-permute-start.10 = (bf16[192,1536]{1,0:T(8,128)(2,1)S(1)}, bf16[192,1536]{1,0:T(8,128)(2,1)S(1)}, u32[]{:S(2)}, u32[]{:S(2)}) collective-permute-start(bf16[192,1536]{1,0:T(8,128)(2,1)S(1)} %slice.31), channel_id=1, source_target_pairs={{0,2},{2,0},{4,6},{6,4},{8,10},{10,8},{12,14},{14,12},{1,3},{3,1},... | collective-permute-start | bytes 1769480 | tf_op jit(solution)/shard_map/ppermute | solution.py:21
  49.7 2.9 %adapter_kernel.1 = (bf16[1536,128]{1,0:T(8,128)(2,1)S(1)}, bf16[128,3072]{1,0:T(8,128)(2,1)S(1)}, bf16[128,128]{1,0:T(8,128)(2,1)S(1)}, bf16[128,128]{1,0:T(8,1...) custom-call(bf16[240,1536]{1,0:T(8,128)(2,1)S(1)} %copy-done.6, ...), custom_call_target="tpu_custom_call" | custom-call | flops 8738539520 | bytes 8738 | tf_op jit(solution)/shard_map/adapter_kernel/pallas_call | solution.py:320
  52.7 2.1 %project_kernel.5 = (f32[128,768]{1,0:T(8,128)S(1)}, bf16[128,768]{1,0:T(8,128)(2,1)S(1)}, f32[256,1536]{1,0:T(8,128)S(1)}) custom-call(bf16[240,1536]{1,0:T(8,128)(2,1)} %collective-permute-done.refs_0_.refs_2_, bf16[240,1536]{1,0:T(8,128)(2,1)S(1)} %collective-permute-done.6.refs_1_.refs_3_, bf16[128,1536]{1,0:T(8,128)(2,1)S(1)} %forward_kernel.1.refs_2_.refs_8_.refs_7_, ...), custom_call_target="tpu_custom_call" | custom-call | flops 15552499712 | bytes 15552 | tf_op jit(solution)/shard_map/project_kernel/pallas_call | solution.py:320
  54.8 0.5 collective-permute-start.18
  55.5 1.8 %collective-permute-start.15 = (bf16[4,288,128]{2,1,0:T(8,128)(2,1)S(1)}, bf16[4,288,128]{2,1,0:T(8,128)(2,1)S(1)}, u32[]{:S(2)}, u32[]{:S(2)}) collective-permute-start(bf16[4,288,128]{2,1,0:T(8,128)(2,1)S(1)} %slice.51), channel_id=1, source_target_pairs={{0,4},{2,6},{4,0},{6,2},{8,12},{10,14},{12,8},{14,10},{1,5},{3,7},... | collective-permute-start | bytes 884744 | tf_op jit(solution)/shard_map/ppermute | solution.py:21
  57.2 3.6 %backward_kernel.3 = (bf16[128,768]{1,0:T(8,128)(2,1)S(1)}, f32[2,128,768]{2,1,0:T(8,128)S(1)}, bf16[2,128,768]{2,1,0:T(8,128)(2,1)S(1)}) custom-call(bf16[128,1536]{1,0:T(8,128)(2,1)S(1)} %bitcast.22, bf16[128,1536]{1,0:T(8,128)(2,1)S(1)} %bitcast.27, bf16[128,1536]{1,0:T(8,128)(2,1)S(1)} %collective-permute-done.2.kf.refs_2_, ...), custom_call_target="tpu_custom_call" | custom-call | flops 43205500928 | bytes 43205 | tf_op jit(solution)/shard_map/backward_kernel/pallas_call | solution.py:320
  60.9 1.4 %project_kernel.6 = (f32[128,384]{1,0:T(8,128)S(1)}, bf16[128,384]{1,0:T(8,128)(2,1)S(1)}, f32[256,1536]{1,0:T(8,128)S(1)}) custom-call(bf16[240,1536]{1,0:T(8,128)(2,1)S(1)} %collective-permute-done.7.refs_0_.refs_4_, bf16[192,1536]{1,0:T(8,128)(2,1)S(1)} %collective-permute-done.9.refs_1_, bf16[128,1536]{1,0:T(8,128)(2,1)S(1)} %forward_kernel.1.refs_2_.refs_8_.refs_7_, ...), custom_call_target="tpu_custom_call" | custom-call | flops 37193300 | bytes 37 | tf_op jit(solution)/shard_map/project_kernel/pallas_call | solution.py:320
  62.4 1.4 %project_kernel.7 = (f32[128,384]{1,0:T(8,128)S(1)}, bf16[128,384]{1,0:T(8,128)(2,1)S(1)}, f32[128,1536]{1,0:T(8,128)S(1)}, bf16[128,1536]{1,0:T(8,128)(2,1)S(1)}) custom-call(bf16[240,1536]{1,0:T(8,128)(2,1)S(1)} %collective-permute-done.5.refs_0_.refs_6_, bf16[192,1536]{1,0:T(8,128)(2,1)S(1)} %collective-permute-done.10.refs_1_, ...), custom_call_target="tpu_custom_call" | custom-call | flops 32012600 | bytes 32 | tf_op jit(solution)/shard_map/project_kernel/pallas_call | solution.py:320
  64.9 0.6 collective-permute-start.16
  65.8 1.8 %backward_kernel.4 = (bf16[128,384]{1,0:T(8,128)(2,1)S(1)}, f32[2,128,384]{2,1,0:T(8,128)S(1)}, bf16[2,128,384]{2,1,0:T(8,128)(2,1)S(1)}) custom-call(bf16[128,1536]{1,0:T(8,128)(2,1)S(1)} %bitcast.23, bf16[128,1536]{1,0:T(8,128)(2,1)S(1)} %bitcast.28, bf16[128,1536]{1,0:T(8,128)(2,1)S(1)} %collective-permute-done.2.kf.refs_2_, ...), custom_call_target="tpu_custom_call" | custom-call | flops 32519499776 | bytes 32519 | tf_op jit(solution)/shard_map/backward_kernel/pallas_call | solution.py:320
  68.0 1.8 %backward_kernel.5 = (bf16[128,384]{1,0:T(8,128)(2,1)S(1)}, f32[2,128,384]{2,1,0:T(8,128)S(1)}, bf16[2,128,384]{2,1,0:T(8,128)(2,1)S(1)}) custom-call(bf16[128,1536]{1,0:T(8,128)(2,1)S(1)} %bitcast.24, bf16[128,1536]{1,0:T(8,128)(2,1)S(1)} %bitcast.29, bf16[128,1536]{1,0:T(8,128)(2,1)S(1)} %collective-permute-done.2.kf.refs_2_, ...), custom_call_target="tpu_custom_call" | custom-call | flops 43751800 | bytes 43 | tf_op jit(solution)/shard_map/backward_kernel/pallas_call | solution.py:320
  70.0 0.8 collective-permute-done.16
  70.9 2.5 %collective-permute-start.17 = (bf16[288,128]{1,0:T(8,128)(2,1)S(1)}, bf16[288,128]{1,0:T(8,128)(2,1)S(1)}, u32[]{:S(2)}, u32[]{:S(2)}) collective-permute-start(bf16[288,128]{1,0:T(8,128)(2,1)S(1)} %fusion), channel_id=1, source_target_pairs={{0,8},{2,10},{4,12},{6,14},{8,0},{10,2},{12,4},{14,6},{1,9},{3,11}... | collective-permute-start | bytes 221192 | tf_op jit(solution)/shard_map/ppermute | solution.py:21
  73.4 1.2 %finish_kernel.1 = (bf16[128,1536]{1,0:T(8,128)(2,1)}, bf16[128,1536]{1,0:T(8,128)(2,1)}, bf16[128,1536]{1,0:T(8,128)(2,1)}) custom-call(bf16[128,768]{1,0:T(8,128)(2,1)S(1)} %get-tuple-element.82.refs_0_, bf16[128,384]{1,0:T(8,128)(2,1)S(1)} %get-tuple-element.87.refs_1_, bf16[128,384]{1,0:T(8,128)(2,1)S(1)} %get-tuple-element.90.refs_2_, ...), custom_call_target="tpu_custom_call" | custom-call | flops 44067098624 | bytes 44067 | tf_op jit(solution)/shard_map/finish_kernel/pallas_call | solution.py:320
  74.6 2.6 %collective-permute-done.17.refs_1_ = bf16[288,128]{1,0:T(8,128)(2,1)S(1)} collective-permute-done((bf16[288,128]{1,0:T(8,128)(2,1)S(1)}, bf16[288,128]{1,0:T(8,128)(2,1)S(1)}, u32[]{:S(2)}, u32[]{:S(2)}) %collective-permute-start.17) | collective-permute-done | bytes 73760 | tf_op jit(solution)/shard_map/ppermute | solution.py:21
  77.2 1.2 %update_kernel.1 = (bf16[128,3072]{1,0:T(8,128)(2,1)}, f32[96,128]{1,0:T(8,128)}, f32[192,128]{1,0:T(8,128)}) custom-call(f32[128,1536]{1,0:T(8,128)S(1)} %get-tuple-element.70.own, bf16[128,1536]{1,0:T(8,128)(2,1)S(1)} %collective-permute-done.11.away, bf16[128,128]{1,0:T(8,128)(2,1)S(1)} %get-tuple-element.72.act, ...), custom_call_target="tpu_custom_call" | custom-call | flops 7446859776 | bytes 7446 | tf_op jit(solution)/shard_map/update_kernel/pallas_call | solution.py:320
  (55 shorter events, 4.6 us)
Async XLA Ops:
  0.6 6.8 %copy-start.2 = (bf16[1,128,1536]{2,1,0:T(8,128)(2,1)S(1)}, bf16[1,128,1536]{2,1,0:T(8,128)(2,1)}, u32[]{:S(2)}) copy-start(bf16[1,128,1536]{2,1,0:T(8,128)(2,1)} %param.11) | copy-start | bytes 1179652
  0.6 6.8 %copy-start.4 = (bf16[1,128,1536]{2,1,0:T(8,128)(2,1)S(1)}, bf16[1,128,1536]{2,1,0:T(8,128)(2,1)}, u32[]{:S(2)}) copy-start(bf16[1,128,1536]{2,1,0:T(8,128)(2,1)} %param.12) | copy-start | bytes 1179652
  0.7 7.3 %copy-start = (bf16[1,128,3072]{2,1,0:T(8,128)(2,1)S(1)}, bf16[1,128,3072]{2,1,0:T(8,128)(2,1)}, u32[]{:S(2)}) copy-start(bf16[1,128,3072]{2,1,0:T(8,128)(2,1)} %param.19) | copy-start | bytes 2359300
  0.7 9.0 %copy-start.1 = (bf16[1,128,1536]{2,1,0:T(8,128)(2,1)S(1)}, bf16[1,128,1536]{2,1,0:T(8,128)(2,1)}, u32[]{:S(2)}) copy-start(bf16[1,128,1536]{2,1,0:T(8,128)(2,1)} %param.10) | copy-start | bytes 1179652
  0.7 9.0 %copy-start.3 = (bf16[1,128,1536]{2,1,0:T(8,128)(2,1)S(1)}, bf16[1,128,1536]{2,1,0:T(8,128)(2,1)}, u32[]{:S(2)}) copy-start(bf16[1,128,1536]{2,1,0:T(8,128)(2,1)} %param.13) | copy-start | bytes 1179652
  0.7 9.0 %copy-start.5 = (bf16[1,128,1536]{2,1,0:T(8,128)(2,1)S(1)}, bf16[1,128,1536]{2,1,0:T(8,128)(2,1)}, u32[]{:S(2)}) copy-start(bf16[1,128,1536]{2,1,0:T(8,128)(2,1)} %param.14) | copy-start | bytes 1179652
  2.8 20.9 %collective-permute-start = (bf16[240,1536]{1,0:T(8,128)(2,1)}, bf16[240,1536]{1,0:T(8,128)(2,1)}, u32[]{:S(2)}, u32[]{:S(2)}) collective-permute-start(bf16[240,1536]{1,0:T(8,128)(2,1)} %pack_kernel.1.refs_0_), channel_id=1, source_target_pairs={{0,4},{16,24},{2,6},{18,26},{4,12},{20,16},{6,14},{22,18},{8,0},{2... | collective-permute-start | bytes 2211848 | tf_op jit(solution)/shard_map/ppermute | solution.py:42
  5.9 18.3 %collective-permute-start.1 = (bf16[240,1536]{1,0:T(8,128)(2,1)}, bf16[240,1536]{1,0:T(8,128)(2,1)}, u32[]{:S(2)}, u32[]{:S(2)}) collective-permute-start(bf16[240,1536]{1,0:T(8,128)(2,1)} %pack_kernel.1.refs_0_), channel_id=1, source_target_pairs={{0,2},{2,0},{4,6},{6,4},{8,10},{10,8},{12,14},{14,12},{1,3},{3,1},... | collective-permute-start | bytes 2211848 | tf_op jit(solution)/shard_map/ppermute | solution.py:21
  7.4 1.7 %collective-permute-start.2 = (bf16[128,1536]{1,0:T(8,128)(2,1)S(1)}, bf16[128,1536]{1,0:T(8,128)(2,1)S(1)}, u32[]{:S(2)}, u32[]{:S(2)}) collective-permute-start(bf16[128,1536]{1,0:T(8,128)(2,1)S(1)} %bitcast.25), channel_id=1, source_target_pairs={{0,1},{1,0},{2,3},{3,2},{4,5},{5,4},{6,7},{7,6},{8,9},{9,8},{10,11... | collective-permute-start | bytes 1179656 | tf_op jit(solution)/shard_map/ppermute | solution.py:21
  7.4 2.3 %collective-permute-start.3 = (bf16[128,1536]{1,0:T(8,128)(2,1)S(1)}, bf16[128,1536]{1,0:T(8,128)(2,1)S(1)}, u32[]{:S(2)}, u32[]{:S(2)}) collective-permute-start(bf16[128,1536]{1,0:T(8,128)(2,1)S(1)} %bitcast.34), channel_id=1, source_target_pairs={{0,1},{1,0},{2,3},{3,2},{4,5},{5,4},{6,7},{7,6},{8,9},{9,8},{10,11... | collective-permute-start | bytes 1179656 | tf_op jit(solution)/shard_map/ppermute | solution.py:21
  8.0 7.4 %collective-permute-start.4 = (bf16[128,1536]{1,0:T(8,128)(2,1)S(1)}, bf16[128,1536]{1,0:T(8,128)(2,1)S(1)}, u32[]{:S(2)}, u32[]{:S(2)}) collective-permute-start(bf16[128,1536]{1,0:T(8,128)(2,1)S(1)} %dynamic-slice_bitcast_fusion), channel_id=1, source_target_pairs={{0,1},{1,0},{2,3},{3,2},{4,5},{5,4},{6,7},{7,6},{8,9},{9,8},{10,11... | collective-permute-start | bytes 1179656 | tf_op jit(solution)/shard_map/ppermute | solution.py:21
  9.7 24.0 %copy-start.6 = (bf16[240,1536]{1,0:T(8,128)(2,1)S(1)}, bf16[240,1536]{1,0:T(8,128)(2,1)}, u32[]{:S(2)}) copy-start(bf16[240,1536]{1,0:T(8,128)(2,1)} %pack_kernel.1.refs_0_) | copy-start | bytes 2211844
  24.2 22.3 %collective-permute-start.5 = (bf16[240,1536]{1,0:T(8,128)(2,1)}, bf16[240,1536]{1,0:T(8,128)(2,1)S(1)}, u32[]{:S(2)}, u32[]{:S(2)}) collective-permute-start(bf16[240,1536]{1,0:T(8,128)(2,1)} %collective-permute-done.refs_0_.refs_2_), channel_id=1, source_target_pairs={{0,4},{16,24},{2,6},{18,26},{4,12},{20,16},{6,14},{22,18},{8,0},{2... | collective-permute-start | bytes 2211848 | tf_op jit(solution)/shard_map/ppermute | solution.py:42
  26.8 19.7 %collective-permute-start.6 = (bf16[240,1536]{1,0:T(8,128)(2,1)}, bf16[240,1536]{1,0:T(8,128)(2,1)S(1)}, u32[]{:S(2)}, u32[]{:S(2)}) collective-permute-start(bf16[240,1536]{1,0:T(8,128)(2,1)} %collective-permute-done.refs_0_.refs_2_), channel_id=1, source_target_pairs={{0,2},{2,0},{4,6},{6,4},{8,10},{10,8},{12,14},{14,12},{1,3},{3,1},... | collective-permute-start | bytes 2211848 | tf_op jit(solution)/shard_map/ppermute | solution.py:21
  28.3 18.2 %collective-permute-start.7 = (bf16[240,1536]{1,0:T(8,128)(2,1)}, bf16[240,1536]{1,0:T(8,128)(2,1)S(1)}, u32[]{:S(2)}, u32[]{:S(2)}) collective-permute-start(bf16[240,1536]{1,0:T(8,128)(2,1)} %collective-permute-done.refs_0_.refs_2_), channel_id=1, source_target_pairs={{0,16},{16,0},{1,17},{17,1},{2,18},{18,2},{3,19},{19,3},{4,20},{20... | collective-permute-start | bytes 2211848 | tf_op jit(solution)/shard_map/ppermute | solution.py:21
  29.8 2.3 %collective-permute-start.8 = (bf16[128,1536]{1,0:T(8,128)(2,1)S(1)}, bf16[128,1536]{1,0:T(8,128)(2,1)S(1)}, u32[]{:S(2)}, u32[]{:S(2)}) collective-permute-start(bf16[128,1536]{1,0:T(8,128)(2,1)S(1)} %forward_kernel.1.refs_2_.refs_8_.refs_7_), channel_id=1, source_target_pairs={{0,1},{1,0},{2,3},{3,2},{4,5},{5,4},{6,7},{7,6},{8,9},{9,8},{10,11... | collective-permute-start | bytes 1179656 | tf_op jit(solution)/shard_map/ppermute | solution.py:21
  31.7 17.5 %collective-permute-start.12 = (bf16[48,1536]{1,0:T(8,128)(2,1)S(1)}, bf16[48,1536]{1,0:T(8,128)(2,1)S(1)}, u32[]{:S(2)}, u32[]{:S(2)}) collective-permute-start(bf16[48,1536]{1,0:T(8,128)(2,1)S(1)} %slice.32), channel_id=1, source_target_pairs={{4,0},{24,16},{6,2},{26,18},{12,4},{16,20},{14,6},{18,22},{0,8},{2... | collective-permute-start | bytes 442376 | tf_op jit(solution)/shard_map/ppermute | solution.py:42
  32.1 17.6 %collective-permute-start.13 = (bf16[48,1536]{1,0:T(8,128)(2,1)S(1)}, bf16[48,1536]{1,0:T(8,128)(2,1)S(1)}, u32[]{:S(2)}, u32[]{:S(2)}) collective-permute-start(bf16[48,1536]{1,0:T(8,128)(2,1)S(1)} %slice.33), channel_id=1, source_target_pairs={{0,6},{16,26},{2,4},{18,24},{4,14},{20,18},{6,12},{22,16},{8,2},{2... | collective-permute-start | bytes 442376 | tf_op jit(solution)/shard_map/ppermute | solution.py:42
  46.5 3.2 %copy-start.7 = (bf16[1,128,128]{2,1,0:T(8,128)(2,1)S(1)}, bf16[1,128,128]{2,1,0:T(8,128)(2,1)}, u32[]{:S(2)}) copy-start(bf16[1,128,128]{2,1,0:T(8,128)(2,1)} %param.15) | copy-start | bytes 98308
  46.5 14.4 %collective-permute-start.9 = (bf16[192,1536]{1,0:T(8,128)(2,1)S(1)}, bf16[192,1536]{1,0:T(8,128)(2,1)S(1)}, u32[]{:S(2)}, u32[]{:S(2)}) collective-permute-start(bf16[192,1536]{1,0:T(8,128)(2,1)S(1)} %slice.30), channel_id=1, source_target_pairs={{0,16},{16,0},{1,17},{17,1},{2,18},{18,2},{3,19},{19,3},{4,20},{20... | collective-permute-start | bytes 1769480 | tf_op jit(solution)/shard_map/ppermute | solution.py:21
  47.6 13.3 %collective-permute-start.10 = (bf16[192,1536]{1,0:T(8,128)(2,1)S(1)}, bf16[192,1536]{1,0:T(8,128)(2,1)S(1)}, u32[]{:S(2)}, u32[]{:S(2)}) collective-permute-start(bf16[192,1536]{1,0:T(8,128)(2,1)S(1)} %slice.31), channel_id=1, source_target_pairs={{0,2},{2,0},{4,6},{6,4},{8,10},{10,8},{12,14},{14,12},{1,3},{3,1},... | collective-permute-start | bytes 1769480 | tf_op jit(solution)/shard_map/ppermute | solution.py:21
  52.6 2.7 %collective-permute-start.14 = (bf16[8,288,128]{2,1,0:T(8,128)(2,1)S(1)}, bf16[8,288,128]{2,1,0:T(8,128)(2,1)S(1)}, u32[]{:S(2)}, u32[]{:S(2)}) collective-permute-start(bf16[8,288,128]{2,1,0:T(8,128)(2,1)S(1)} %get-tuple-element.75), channel_id=1, source_target_pairs={{0,1},{1,0},{2,3},{3,2},{4,5},{5,4},{6,7},{7,6},{8,9},{9,8},{10,11... | collective-permute-start | bytes 1769480 | tf_op jit(solution)/shard_map/ppermute | solution.py:21
  54.8 2.4 %collective-permute-start.18 = (bf16[128,768]{1,0:T(8,128)(2,1)S(1)}, bf16[128,768]{1,0:T(8,128)(2,1)S(1)}, u32[]{:S(2)}, u32[]{:S(2)}) collective-permute-start(bf16[128,768]{1,0:T(8,128)(2,1)S(1)} %get-tuple-element.78), channel_id=1, source_target_pairs={{0,1},{1,0},{2,3},{3,2},{4,5},{5,4},{6,7},{7,6},{8,9},{9,8},{10,11... | collective-permute-start | bytes 589832 | tf_op jit(solution)/shard_map/ppermute | solution.py:21
  55.5 9.4 %collective-permute-start.15 = (bf16[4,288,128]{2,1,0:T(8,128)(2,1)S(1)}, bf16[4,288,128]{2,1,0:T(8,128)(2,1)S(1)}, u32[]{:S(2)}, u32[]{:S(2)}) collective-permute-start(bf16[4,288,128]{2,1,0:T(8,128)(2,1)S(1)} %slice.51), channel_id=1, source_target_pairs={{0,4},{2,6},{4,0},{6,2},{8,12},{10,14},{12,8},{14,10},{1,5},{3,7},... | collective-permute-start | bytes 884744 | tf_op jit(solution)/shard_map/ppermute | solution.py:21
  60.8 12.5 %collective-permute-start.21 = (bf16[2,128,768]{2,1,0:T(8,128)(2,1)S(1)}, bf16[2,128,768]{2,1,0:T(8,128)(2,1)S(1)}, u32[]{:S(2)}, u32[]{:S(2)}) collective-permute-start(bf16[2,128,768]{2,1,0:T(8,128)(2,1)S(1)} %get-tuple-element.94), channel_id=1, source_target_pairs={{0,1},{1,0},{2,3},{3,2},{4,5},{5,4},{6,7},{7,6},{8,9},{9,8},{10,11... | collective-permute-start | bytes 1179656 | tf_op jit(solution)/shard_map/ppermute | solution.py:21
  63.8 10.8 %collective-permute-start.11 = (bf16[128,1536]{1,0:T(8,128)(2,1)S(1)}, bf16[128,1536]{1,0:T(8,128)(2,1)S(1)}, u32[]{:S(2)}, u32[]{:S(2)}) collective-permute-start(bf16[128,1536]{1,0:T(8,128)(2,1)S(1)} %get-tuple-element.71), channel_id=1, source_target_pairs={{0,1},{1,0},{2,3},{3,2},{4,5},{5,4},{6,7},{7,6},{8,9},{9,8},{10,11... | collective-permute-start | bytes 1179656 | tf_op jit(solution)/shard_map/ppermute | solution.py:21
  64.3 1.5 %collective-permute-start.19 = (bf16[128,384]{1,0:T(8,128)(2,1)S(1)}, bf16[128,384]{1,0:T(8,128)(2,1)S(1)}, u32[]{:S(2)}, u32[]{:S(2)}) collective-permute-start(bf16[128,384]{1,0:T(8,128)(2,1)S(1)} %get-tuple-element.85), channel_id=1, source_target_pairs={{0,1},{1,0},{2,3},{3,2},{4,5},{5,4},{6,7},{7,6},{8,9},{9,8},{10,11... | collective-permute-start | bytes 294920 | tf_op jit(solution)/shard_map/ppermute | solution.py:21
  64.4 3.7 %collective-permute-start.20 = (bf16[128,384]{1,0:T(8,128)(2,1)S(1)}, bf16[128,384]{1,0:T(8,128)(2,1)S(1)}, u32[]{:S(2)}, u32[]{:S(2)}) collective-permute-start(bf16[128,384]{1,0:T(8,128)(2,1)S(1)} %get-tuple-element.89), channel_id=1, source_target_pairs={{0,1},{1,0},{2,3},{3,2},{4,5},{5,4},{6,7},{7,6},{8,9},{9,8},{10,11... | collective-permute-start | bytes 294920 | tf_op jit(solution)/shard_map/ppermute | solution.py:21
  64.9 5.9 %collective-permute-start.16 = (bf16[2,288,128]{2,1,0:T(8,128)(2,1)S(1)}, bf16[2,288,128]{2,1,0:T(8,128)(2,1)S(1)}, u32[]{:S(2)}, u32[]{:S(2)}) collective-permute-start(bf16[2,288,128]{2,1,0:T(8,128)(2,1)S(1)} %slice.52), channel_id=1, source_target_pairs={{0,2},{2,0},{4,6},{6,4},{8,10},{10,8},{12,14},{14,12},{1,3},{3,1},... | collective-permute-start | bytes 442376 | tf_op jit(solution)/shard_map/ppermute | solution.py:21
  67.6 5.8 %collective-permute-start.22 = (bf16[2,128,384]{2,1,0:T(8,128)(2,1)S(1)}, bf16[2,128,384]{2,1,0:T(8,128)(2,1)S(1)}, u32[]{:S(2)}, u32[]{:S(2)}) collective-permute-start(bf16[2,128,384]{2,1,0:T(8,128)(2,1)S(1)} %get-tuple-element.95), channel_id=1, source_target_pairs={{0,1},{1,0},{2,3},{3,2},{4,5},{5,4},{6,7},{7,6},{8,9},{9,8},{10,11... | collective-permute-start | bytes 589832 | tf_op jit(solution)/shard_map/ppermute | solution.py:21
  69.8 3.5 %collective-permute-start.23 = (bf16[2,128,384]{2,1,0:T(8,128)(2,1)S(1)}, bf16[2,128,384]{2,1,0:T(8,128)(2,1)S(1)}, u32[]{:S(2)}, u32[]{:S(2)}) collective-permute-start(bf16[2,128,384]{2,1,0:T(8,128)(2,1)S(1)} %get-tuple-element.96), channel_id=1, source_target_pairs={{0,1},{1,0},{2,3},{3,2},{4,5},{5,4},{6,7},{7,6},{8,9},{9,8},{10,11... | collective-permute-start | bytes 589832 | tf_op jit(solution)/shard_map/ppermute | solution.py:21
  70.9 6.3 %collective-permute-start.17 = (bf16[288,128]{1,0:T(8,128)(2,1)S(1)}, bf16[288,128]{1,0:T(8,128)(2,1)S(1)}, u32[]{:S(2)}, u32[]{:S(2)}) collective-permute-start(bf16[288,128]{1,0:T(8,128)(2,1)S(1)} %fusion), channel_id=1, source_target_pairs={{0,8},{2,10},{4,12},{6,14},{8,0},{10,2},{12,4},{14,6},{1,9},{3,11}... | collective-permute-start | bytes 221192 | tf_op jit(solution)/shard_map/ppermute | solution.py:21
